TPU v7x, 32 devices: a whole 2x2x4 slice. The times are simulated.
32 devices in a mesh: tile: 8 (over z, x), chan: 4 (over y, core).
Axes of the slice: x: 2, y: 2, z: 4, core: 2. Of those that a mesh axis runs over, the one named last changes fastest.
Arguments:
- tiles: bfloat16 [8, 128, 16, 16, 128], P('tile'), may hold values from -6 to 6
- orientation: int32 [8], P('tile'), may hold values from 0 to 3
- weight: bfloat16 [3, 3, 128, 128], P(None, None, None, 'chan'), may hold values from -0.1875 to 0.1875
- grad_out: bfloat16 [8, 128, 16, 16, 128], P('tile'), may hold values from -6 to 6
Outputs:
- conv_out: bfloat16 [8, 128, 16, 16, 128], P('tile', None, None, None, 'chan')
- grad_input: bfloat16 [8, 128, 16, 16, 128], P('tile', None, None, None, 'chan')
- grad_weight: float32 [3, 3, 128, 128], P(None, None, None, 'chan')
All inputs are finite; a program needn't handle non-finite values.
Results may differ from a plain program's by a relative error of at most 0.0034.
Values may be sent and summed in bfloat16 or wider, within the bound.
No kernel may reach another device: no remote copies, remote signals or barrier semaphores. Data moves between devices by JAX's collectives and lax.ppermute only.
A program may use at most 128 MiB of HBM per device.

v0:
```python
from functools import partial
import math

import jax
import jax.numpy as jnp
from jax import lax
from jax.sharding import PartitionSpec as P

seam_table = ((1, 2), (-2, 3), (-1, 0), (2, 1))


def passed_along(value, axis, by):
    length = lax.axis_size(axis)
    return lax.ppermute(value, axis, [(i, (i + by) % length) for i in range(length)])


def as_sent(value):

    def short(part):
        return part.astype(jnp.bfloat16) if part.dtype == jnp.float32 else part

    return jax.tree.map(short, value)


def turn_fixed(edges, repeat_count):
    northern, eastern, southern, western = edges
    for step in range(repeat_count):
        northern, eastern, southern, western = (
            eastern,
            jnp.flip(southern, 1),
            western,
            jnp.flip(northern, 1),
        )
    return (northern, eastern, southern, western)


def turn_edges(edges, quarters):
    branches = [partial(turn_fixed, repeat_count=amount) for amount in range(4)]
    return lax.switch(quarters, branches, edges)


def border_edges(block):
    return (block[:, 0], block[:, :, -1], block[:, -1], block[:, :, 0])


def keep_present(edges, position):
    across = position % 2
    northern, eastern, southern, western = edges
    northern = jnp.where(across == 1, northern, jnp.zeros_like(northern))
    southern = jnp.where(across == 0, southern, jnp.zeros_like(southern))
    return (northern, eastern, southern, western)


def with_margins(field, margins):
    northern, eastern, southern, western = margins
    middle = jnp.concatenate([western[:, :, None], field, eastern[:, :, None]], axis=2)
    upper = jnp.pad(northern, ((0, 0), (1, 1), (0, 0)))[:, None]
    lower = jnp.pad(southern, ((0, 0), (1, 1), (0, 0)))[:, None]
    return jnp.concatenate([upper, middle, lower], axis=1)


def per_device(tiles, orientation, weight, grad_out):
    field = tiles[0]
    quarters = orientation[0]
    position = lax.axis_index("tile")
    layout_spec = ("NHWC", "HWIO", "NHWC")
    arrived_edges = []
    stacked = jnp.stack(border_edges(field), 1)
    code_value = orientation.astype(jnp.bfloat16)
    for offset, facing in seam_table:
        arrived, their_code = passed_along((stacked, code_value), "tile", offset)
        source_quarters = their_code[0].astype(jnp.int32)
        theirs = turn_edges(
            tuple((arrived[:, edge_slot] for edge_slot in range(4))), (4 - source_quarters) % 4
        )
        arrived_edges.append(theirs[facing])
    margins = turn_edges(keep_present(tuple(arrived_edges), position), quarters)
    padded = with_margins(field, margins)
    conv_out = lax.conv_general_dilated(
        padded,
        weight,
        (1, 1),
        "VALID",
        dimension_numbers=layout_spec,
        preferred_element_type=jnp.float32,
    ).astype(jnp.bfloat16)
    share = weight.shape[3]
    chan_index = lax.axis_index("chan")
    full_weight = lax.all_gather(weight, "chan", axis=3, tiled=True)
    weight_rows = lax.dynamic_slice_in_dim(full_weight, chan_index * share, share, 2)
    flipped = jnp.flip(weight_rows, (0, 1)).transpose(0, 1, 3, 2)
    upstream = grad_out[0]
    grad_padded = lax.conv_general_dilated(
        upstream,
        flipped,
        (1, 1),
        ((2, 2), (2, 2)),
        dimension_numbers=layout_spec,
        preferred_element_type=jnp.float32,
    )
    border = (
        grad_padded[:, 0, 1:-1],
        grad_padded[:, 1:-1, -1],
        grad_padded[:, -1, 1:-1],
        grad_padded[:, 1:-1, 0],
    )
    outgoing = turn_edges(border, (4 - quarters) % 4)
    incoming = []
    for offset, facing in seam_table:
        incoming.append(passed_along(as_sent(outgoing[facing]), "tile", offset))
    extra = turn_edges(keep_present(tuple(incoming), position), quarters)
    interior = grad_padded[:, 1:-1, 1:-1]
    interior = interior.at[:, 0].add(extra[0])
    interior = interior.at[:, :, -1].add(extra[1])
    interior = interior.at[:, -1].add(extra[2])
    interior = interior.at[:, :, 0].add(extra[3])
    grad_input = interior.astype(jnp.bfloat16)[None]
    tile_count = lax.axis_size("tile")
    upstream_cols = lax.dynamic_slice_in_dim(upstream, chan_index * share, share, 3)
    height = field.shape[1]
    breadth = field.shape[2]
    partial_grads = []
    for row_off in range(3):
        for col_off in range(3):
            window = padded[:, row_off : row_off + height, col_off : col_off + breadth]
            partial_grads.append(
                jnp.einsum(
                    "bhwc,bhwo->co", window, upstream_cols, preferred_element_type=jnp.float32
                )
            )
    local_grad = jnp.stack(partial_grads).reshape(3, 3, field.shape[3], share)
    normalizer = 1.0 / math.sqrt(tile_count * field.shape[0] * height * breadth)
    grad_weight = lax.psum(local_grad, "tile") * normalizer
    return (conv_out[None], grad_input, grad_weight)


def solution(mesh):
    in_specs = (
        P("tile", None, None, None, None),
        P("tile"),
        P(None, None, None, "chan"),
        P("tile", None, None, None, None),
    )
    out_specs = (
        P("tile", None, None, None, "chan"),
        P("tile", None, None, None, "chan"),
        P(None, None, None, "chan"),
    )
    return jax.shard_map(
        per_device, mesh=mesh, in_specs=in_specs, out_specs=out_specs, check_vma=False
    )
```

profile of v0, /device:TPU:0, one launch (start us, length us, event | category | flops | bytes accessed | tf_op | source)
XLA Modules:
  0.0 452.9 jit_solution(13118155155996494246)
XLA Ops:
  7.2 12.1 %copy.228 = bf16[1,128,16,16,128]{4,1,3,2,0:T(8,128)(2,1)} copy(bf16[1,128,16,16,128]{4,3,2,1,0:T(8,128)(2,1)} %param.40) | data formatting | bytes 16777216 | tf_op args[0]
  21.7 3.3 slice.254
  25.4 1.6 pad_maximum_fusion.5
  27.0 6.0 %collective-permute-start.7 = (bf16[128,4,16,128]{3,0,2,1:T(8,128)(2,1)}, bf16[128,4,16,128]{3,0,2,1:T(8,128)(2,1)}, u32[]{:S(2)}, u32[]{:S(2)}) collective-permute-start(bf16[128,4,16,128]{3,0,2,1:T(8,128)(2,1)} %pad_maximum_fusion.5), channel_id=1, source_target_pairs={{0,28},{4,0},{8,4},{12,8},{16,12},{20,16},{24,20},{28,24},{1,29},{... | collective-permute-start | bytes 6291464 | tf_op jit(solution)/shard_map/ppermute | solution.py:14
  33.6 89.5 %collective-permute-start.6 = (bf16[1]{0:T(256)(128)(2,1)}, bf16[1]{0:T(256)(128)(2,1)}, u32[]{:S(2)}, u32[]{:S(2)}) collective-permute-start(bf16[1]{0:T(256)(128)(2,1)} %convert_element_type.84), channel_id=1, source_target_pairs={{0,28},{4,0},{8,4},{12,8},{16,12},{20,16},{24,20},{28,24},{1,29},{... | collective-permute-start | bytes 14 | tf_op jit(solution)/shard_map/ppermute | solution.py:14
  123.2 6.1 %all_gather.3 = bf16[3,3,128,128]{2,3,1,0:T(8,128)(2,1)S(1)} all-gather(bf16[3,3,128,32]{2,3,1,0:T(8,128)(2,1)S(1)} %copy-done.9), channel_id=1, replica_groups=mesh['tile'=8,'chan'=4] {'chan'}, dimensions={3}, use_global_device_ids=true | all-gather | bytes 368640 | tf_op jit(solution)/shard_map/all_gather | solution.py:89
  129.3 36.5 %fusion.26 = f32[128,18,18,32]{0,3,2,1:T(8,128)S(1)} fusion(bf16[128,16,16,128]{3,2,1,0:T(8,128)(2,1)} %bitcast.264, bf16[3,3,128,128]{2,3,1,0:T(8,128)(2,1)S(1)} %all_gather.3, s32[]{:T(128)S(6)} %select_n.70), kind=kOutput, calls=%fused_computation.62 | convolution fusion | flops 2415919104 | bytes 13991940 | tf_op jit(solution)/shard_map/conv_general_dilated | solution.py:93
  165.9 2.3 copy-done
  168.2 3.9 conditional.12
  172.1 9.4 %constant_dynamic-slice_fusion = bf16[1,128,16,16,32]{4,3,2,1,0:T(8,128)(2,1)} fusion(bf16[1,128,16,16,128]{4,3,2,1,0:T(8,128)(2,1)} %param.43, s32[]{:T(128)S(6)} %select_n.70), kind=kLoop, calls=%fused_computation.120 | loop fusion | bytes 4194308 | tf_op jit(solution)/shard_map/dynamic_slice | solution.py:119
  181.5 4.8 %slice.257 = f32[128,16,16,32]{0,3,2,1:T(8,128)} slice(f32[128,18,18,32]{0,3,2,1:T(8,128)} %copy-done), slice={[0:128], [1:17], [1:17], [0:32]} | slice | bytes 8388608 | tf_op jit(solution)/shard_map/slice | solution.py:112
  186.3 10.1 %copy.128 = bf16[1,128,16,16,32]{1,4,3,2,0:T(8,128)(2,1)S(1)} copy(bf16[1,128,16,16,32]{4,3,2,1,0:T(8,128)(2,1)} %constant_dynamic-slice_fusion) | data formatting | bytes 4194304 | tf_op jit(solution)/shard_map/dynamic_slice | solution.py:119
  198.4 4.3 collective-permute-done.4
  204.7 3.4 collective-permute-done.2
  208.1 1.7 collective-permute-start
  211.6 2.2 collective-permute-start.9
  214.7 12.0 %collective-permute-done.9 = bf16[128,16,32]{2,1,0:T(8,128)(2,1)S(1)} collective-permute-done((bf16[128,16,32]{2,1,0:T(8,128)(2,1)}, bf16[128,16,32]{2,1,0:T(8,128)(2,1)S(1)}, u32[]{:S(2)}, u32[]{:S(2)}) %collective-permute-start.9) | collective-permute-done | bytes 131104 | tf_op jit(solution)/shard_map/ppermute | solution.py:14
  226.7 4.0 collective-permute-start.1
  230.7 7.1 %collective-permute-done.10 = bf16[128,16,32]{2,1,0:T(8,128)(2,1)S(1)} collective-permute-done((bf16[128,16,32]{2,1,0:T(8,128)(2,1)}, bf16[128,16,32]{2,1,0:T(8,128)(2,1)S(1)}, u32[]{:S(2)}, u32[]{:S(2)}) %collective-permute-start.10) | collective-permute-done | bytes 131104 | tf_op jit(solution)/shard_map/ppermute | solution.py:14
  237.9 53.3 %collective-permute-done.11 = bf16[128,16,32]{2,1,0:T(8,128)(2,1)} collective-permute-done((bf16[128,16,32]{2,1,0:T(8,128)(2,1)}, bf16[128,16,32]{2,1,0:T(8,128)(2,1)}, u32[]{:S(2)}, u32[]{:S(2)}) %collective-permute-start.11) | collective-permute-done | bytes 131104 | tf_op jit(solution)/shard_map/ppermute | solution.py:14
  291.2 19.5 %conditional.13 = (f32[128,1,16,32]{0,3,2,1:T(8,128)}, f32[128,16,1,32]{0,3,2,1:T(8,128)S(1)}, f32[128,1,16,32]{0,3,2,1:T(8,128)}, f32[128,16,1,32]{0,3,2,1:T(8,128)}) conditional(s32[]{:T(128)} %bitcast.32, (bf16[128,16,32]{2,1,0:T(8,128)(2,1)S(1)}, bf16[128,16,32]{2,1,0:T(8,128)(2,1)}, ...), branch_computations={%region_24.25_spmd, %region_25.26_spmd, %region_26.27_spmd, %regio... | conditional | flops 262144 | bytes 5242940 | solution.py:39
  292.3 2.1 bitcast_convert_fusion.11
  294.4 2.3 copy.157
  296.7 1.8 rev.120
  298.5 2.1 bitcast_convert_fusion.10
  300.6 1.6 copy.161
  303.1 2.1 bitcast_convert_fusion.9
  305.2 2.3 copy.165
  310.7 1.8 fusion.122
  312.4 1.7 fusion.121
  314.2 1.8 fusion.120
  315.9 1.8 fusion.119
  317.7 4.0 convert_bitcast_fusion
  323.2 3.4 conditional.9
  330.6 3.6 conditional.7
  334.2 5.5 %conditional.11 = (bf16[128,16,128]{2,1,0:T(8,128)(2,1)}, bf16[128,16,128]{2,1,0:T(8,128)(2,1)}, bf16[128,16,128]{2,1,0:T(8,128)(2,1)}, bf16[]{:T(256)}, bf16[128,16,128]{2,1,0:T(8,128)(2,1)}) conditional(s32[]{:T(128)} %bitcast.32, (bf16[128,16,128]{2,1,0:T(8,128)(2,1)S(1)}, bf16[128,16,128]{2,1,0:T(8,128)(2,1)S(1)}, ...), branch_computations={%region_16.17_spmd, %region_17.18_spmd, %region_18.19_spmd, %regio... | conditional | bytes 4194348 | solution.py:39
  336.0 1.8 rev.105
  337.8 1.8 rev.106
  343.6 10.1 %pad_maximum_fusion = (bf16[128,17,18,128]{3,0,2,1:T(8,128)(2,1)S(1)}, bf16[128,17,18,128]{3,0,2,1:T(8,128)(2,1)S(1)}) fusion(bf16[128,1,18,128]{3,0,2,1:T(8,128)(2,1)S(1)} %get-tuple-element.423, bf16[128,16,1,128]{3,0,2,1:T(8,128)(2,1)S(1)} %get-tuple-element.425, bf16[128,16,16,128]{3,0,2,1:T(8,128)(2,1)} %bitcast.267, ...), kind=kLoop, calls=%fused_computation.43 | loop fusion | flops 30081024 | bytes 30670848 | tf_op jit(solution)/shard_map/concatenate | solution.py:59
  359.1 1.7 fusion.79
  360.7 8.0 %fusion.43 = f32[9,128,32]{1,2,0:T(8,128)S(1)} fusion(f32[9,128,32]{1,2,0:T(8,128)S(1)} %fusion.79, bf16[1,128,16,16,32]{1,4,3,2,0:T(8,128)(2,1)S(1)} %copy.128, bf16[1,128,16,16,128]{4,3,2,1,0:T(8,128)(2,1)} %param.40), kind=kOutput, calls=%fused_computation.79 | convolution fusion | flops 268435456 | bytes 10502144 | tf_op jit(solution)/shard_map/bhwc,bhwo->co/dot_general | solution.py:127
  368.8 1.7 fusion.85
  370.4 1.7 fusion.93
  372.1 1.5 fusion.103
  373.6 1.5 fusion.113
  375.8 26.1 %convert_bitcast_fusion.1 = bf16[1,128,16,16,32]{1,4,3,2,0:T(8,128)(2,1)} fusion(bf16[3,3,128,32]{2,3,1,0:T(8,128)(2,1)S(1)} %copy-done.9, bf16[128,1,18,128]{3,0,2,1:T(8,128)(2,1)S(1)} %get-tuple-element.423, bf16[128,16,1,128]{3,0,2,1:T(8,128)(2,1)} %copy-done.4, bf16[128,16,16,128]{3,0,2,1:T(8,128)(2,1)} %bitcast.268, ...), kind=kOutput, calls=%fused_computation.77 | convolution fusion | flops 2438201344 | bytes 12787712 | tf_op jit(solution)/shard_map/conv_general_dilated | solution.py:79
  401.9 42.3 %all-reduce.4.cloned.1.call-done = f32[3,3,128,32]{2,3,1,0:T(8,128)} async-done(((f32[3,3,128,32]{2,3,1,0:T(8,128)}), f32[3,3,128,32]{2,3,1,0:T(8,128)}) %all-reduce.4.cloned.1.call-update) | async-done | bytes 147472 | tf_op jit(solution)/shard_map/psum | solution.py:133
  444.3 1.6 broadcast_multiply_fusion
  (83 shorter events, 41.8 us)
Async XLA Ops:
  7.2 437.1 %all-reduce.4.cloned.1.call-start = ((), (), s32[]{:S(2)}) async-start(), calls=%async_computation | async-start | bytes 294912 | tf_op jit(solution)/shard_map/psum | solution.py:133
  19.3 103.9 %copy-start.9 = (bf16[3,3,128,32]{2,3,1,0:T(8,128)(2,1)S(1)}, bf16[3,3,128,32]{2,3,1,0:T(8,128)(2,1)}, u32[]{:S(2)}) copy-start(bf16[3,3,128,32]{2,3,1,0:T(8,128)(2,1)} %param.42) | copy-start | bytes 221188
  27.0 294.8 %collective-permute-start.7 = (bf16[128,4,16,128]{3,0,2,1:T(8,128)(2,1)}, bf16[128,4,16,128]{3,0,2,1:T(8,128)(2,1)}, u32[]{:S(2)}, u32[]{:S(2)}) collective-permute-start(bf16[128,4,16,128]{3,0,2,1:T(8,128)(2,1)} %pad_maximum_fusion.5), channel_id=1, source_target_pairs={{0,28},{4,0},{8,4},{12,8},{16,12},{20,16},{24,20},{28,24},{1,29},{... | collective-permute-start | bytes 6291464 | tf_op jit(solution)/shard_map/ppermute | solution.py:14
  33.0 290.2 %collective-permute-start.5 = (bf16[128,4,16,128]{3,0,2,1:T(8,128)(2,1)}, bf16[128,4,16,128]{3,0,2,1:T(8,128)(2,1)}, u32[]{:S(2)}, u32[]{:S(2)}) collective-permute-start(bf16[128,4,16,128]{3,0,2,1:T(8,128)(2,1)} %pad_maximum_fusion.5), channel_id=1, source_target_pairs={{0,4},{4,8},{8,12},{12,16},{16,20},{20,24},{24,28},{28,0},{1,5},{5... | collective-permute-start | bytes 6291464 | tf_op jit(solution)/shard_map/ppermute | solution.py:14
  33.0 293.7 %collective-permute-start.3 = (bf16[128,4,16,128]{3,0,2,1:T(8,128)(2,1)}, bf16[128,4,16,128]{3,0,2,1:T(8,128)(2,1)}, u32[]{:S(2)}, u32[]{:S(2)}) collective-permute-start(bf16[128,4,16,128]{3,0,2,1:T(8,128)(2,1)} %pad_maximum_fusion.5), channel_id=1, source_target_pairs={{0,8},{4,12},{8,16},{12,20},{16,24},{20,28},{24,0},{28,4},{1,9},{5... | collective-permute-start | bytes 6291464 | tf_op jit(solution)/shard_map/ppermute | solution.py:14
  33.6 162.8 %collective-permute-start.6 = (bf16[1]{0:T(256)(128)(2,1)}, bf16[1]{0:T(256)(128)(2,1)}, u32[]{:S(2)}, u32[]{:S(2)}) collective-permute-start(bf16[1]{0:T(256)(128)(2,1)} %convert_element_type.84), channel_id=1, source_target_pairs={{0,28},{4,0},{8,4},{12,8},{16,12},{20,16},{24,20},{28,24},{1,29},{... | collective-permute-start | bytes 14 | tf_op jit(solution)/shard_map/ppermute | solution.py:14
  165.8 2.3 copy-start
  172.1 9.4 %copy-start.6 = (bf16[128,16,32]{2,1,0:T(8,128)(2,1)}, bf16[128,16,32]{2,1,0:T(8,128)(2,1)S(1)}, u32[]{:S(2)}) copy-start(bf16[128,16,32]{2,1,0:T(8,128)(2,1)S(1)} %get-tuple-element.358) | copy-start | bytes 393220
  172.1 9.4 %copy-start.7 = (bf16[128,16,32]{2,1,0:T(8,128)(2,1)}, bf16[128,16,32]{2,1,0:T(8,128)(2,1)S(1)}, u32[]{:S(2)}) copy-start(bf16[128,16,32]{2,1,0:T(8,128)(2,1)S(1)} %get-tuple-element.356) | copy-start | bytes 393220
  172.1 42.5 %collective-permute-start.8 = (bf16[128,16,32]{2,1,0:T(8,128)(2,1)S(1)}, bf16[128,16,32]{2,1,0:T(8,128)(2,1)}, u32[]{:S(2)}, u32[]{:S(2)}) collective-permute-start(bf16[128,16,32]{2,1,0:T(8,128)(2,1)S(1)} %get-tuple-element.355), channel_id=1, source_target_pairs={{0,4},{4,8},{8,12},{12,16},{16,20},{20,24},{24,28},{28,0},{1,5},{5... | collective-permute-start | bytes 393224 | tf_op jit(solution)/shard_map/ppermute | solution.py:14
  196.4 6.2 %collective-permute-start.4 = (bf16[1]{0:T(256)(128)(2,1)}, bf16[1]{0:T(256)(128)(2,1)}, u32[]{:S(2)}, u32[]{:S(2)}) collective-permute-start(bf16[1]{0:T(256)(128)(2,1)} %convert_element_type.84), channel_id=1, source_target_pairs={{0,4},{4,8},{8,12},{12,16},{16,20},{20,24},{24,28},{28,0},{1,5},{5... | collective-permute-start | bytes 14 | tf_op jit(solution)/shard_map/ppermute | solution.py:14
  202.7 5.4 %collective-permute-start.2 = (bf16[1]{0:T(256)(128)(2,1)}, bf16[1]{0:T(256)(128)(2,1)}, u32[]{:S(2)}, u32[]{:S(2)}) collective-permute-start(bf16[1]{0:T(256)(128)(2,1)} %convert_element_type.84), channel_id=1, source_target_pairs={{0,8},{4,12},{8,16},{12,20},{16,24},{20,28},{24,0},{28,4},{1,9},{5... | collective-permute-start | bytes 14 | tf_op jit(solution)/shard_map/ppermute | solution.py:14
  208.1 3.5 collective-permute-start
  211.6 15.1 %collective-permute-start.9 = (bf16[128,16,32]{2,1,0:T(8,128)(2,1)}, bf16[128,16,32]{2,1,0:T(8,128)(2,1)S(1)}, u32[]{:S(2)}, u32[]{:S(2)}) collective-permute-start(bf16[128,16,32]{2,1,0:T(8,128)(2,1)} %copy-done.7), channel_id=1, source_target_pairs={{0,24},{4,28},{8,0},{12,4},{16,8},{20,12},{24,16},{28,20},{1,25},{... | collective-permute-start | bytes 393224 | tf_op jit(solution)/shard_map/ppermute | solution.py:14
  214.6 23.2 %collective-permute-start.10 = (bf16[128,16,32]{2,1,0:T(8,128)(2,1)}, bf16[128,16,32]{2,1,0:T(8,128)(2,1)S(1)}, u32[]{:S(2)}, u32[]{:S(2)}) collective-permute-start(bf16[128,16,32]{2,1,0:T(8,128)(2,1)} %get-tuple-element.357), channel_id=1, source_target_pairs={{0,28},{4,0},{8,4},{12,8},{16,12},{20,16},{24,20},{28,24},{1,29},{... | collective-permute-start | bytes 393224 | tf_op jit(solution)/shard_map/ppermute | solution.py:14
  226.7 11.1 %copy-start.1 = (bf16[128,16,32]{2,1,0:T(8,128)(2,1)}, bf16[128,16,32]{2,1,0:T(8,128)(2,1)S(1)}, u32[]{:S(2)}) copy-start(bf16[128,16,32]{2,1,0:T(8,128)(2,1)S(1)} %collective-permute-done.9) | copy-start | bytes 393220
  226.7 103.9 %collective-permute-start.1 = (bf16[128,4,16,128]{3,0,2,1:T(8,128)(2,1)}, bf16[128,4,16,128]{3,0,2,1:T(8,128)(2,1)}, u32[]{:S(2)}, u32[]{:S(2)}) collective-permute-start(bf16[128,4,16,128]{3,0,2,1:T(8,128)(2,1)} %pad_maximum_fusion.5), channel_id=1, source_target_pairs={{0,24},{4,28},{8,0},{12,4},{16,8},{20,12},{24,16},{28,20},{1,25},{... | collective-permute-start | bytes 6291464 | tf_op jit(solution)/shard_map/ppermute | solution.py:14
  237.8 53.3 %collective-permute-start.11 = (bf16[128,16,32]{2,1,0:T(8,128)(2,1)}, bf16[128,16,32]{2,1,0:T(8,128)(2,1)}, u32[]{:S(2)}, u32[]{:S(2)}) collective-permute-start(bf16[128,16,32]{2,1,0:T(8,128)(2,1)} %copy-done.6), channel_id=1, source_target_pairs={{0,8},{4,12},{8,16},{12,20},{16,24},{20,28},{24,0},{28,4},{1,9},{5... | collective-permute-start | bytes 393224 | tf_op jit(solution)/shard_map/ppermute | solution.py:14
  292.3 15.3 %copy-start.2 = (bf16[128,16,32]{2,1,0:T(8,128)(2,1)S(1)}, bf16[128,16,32]{2,1,0:T(8,128)(2,1)}, u32[]{:S(2)}) copy-start(bf16[128,16,32]{2,1,0:T(8,128)(2,1)} %get-tuple-element.329) | copy-start | bytes 393220 | tf_op jit(solution)/shard_map/cond
  326.6 0.8 copy-start.3
  343.5 14.7 %copy-start.5 = (bf16[128,16,1,128]{3,0,2,1:T(8,128)(2,1)}, bf16[128,16,1,128]{3,0,2,1:T(8,128)(2,1)S(1)}, u32[]{:S(2)}) copy-start(bf16[128,16,1,128]{3,0,2,1:T(8,128)(2,1)S(1)} %get-tuple-element.426) | copy-start | bytes 1572868
  343.5 25.3 %copy-start.4 = (bf16[128,16,1,128]{3,0,2,1:T(8,128)(2,1)}, bf16[128,16,1,128]{3,0,2,1:T(8,128)(2,1)S(1)}, u32[]{:S(2)}) copy-start(bf16[128,16,1,128]{3,0,2,1:T(8,128)(2,1)S(1)} %get-tuple-element.425) | copy-start | bytes 1572868
  355.2 3.0 slice-start
  356.7 2.4 slice-start.1
  375.1 0.7 copy-start.8
Sparse Core Ops, SparseCore 0:
  375.9 68.2 all-reduce.3
where the time goes:
time: 460 us; the launch traced here: 453 us
  waiting for transfers between devices  124 us (27%)
  starting transfers between devices  106 us (23%)
  matrix products  83.1 us (18%)
  local copies, waits for them, and re-layouts  81.4 us (18%)
  other arithmetic  33.5 us (7%)
  between operations  17.8 us (4%)
  blocking collectives  6.12 us (1%)
    ppermute x12, starting transfers between devices, passed_along(): lax.ppermute(value, axis, [(i, (i + by) % length) for i in range(length)])  106 us
    ppermute x12, waiting for transfers between devices, passed_along(): lax.ppermute(value, axis, [(i, (i + by) % length) for i in range(length)])  81.3 us
    psum x1, waiting for transfers between devices, per_device(): grad_weight = lax.psum(local_grad, 'tile') * normalizer  42.3 us
    conv_general_dilated x1, matrix products, per_device(): lax.conv_general_dilated(upstream, flipped, (1, 1), ((2, 2), (2, 2)), dim...  36.5 us
    conv_general_dilated x1, matrix products, per_device(): lax.conv_general_dilated(padded, weight, (1, 1), 'VALID', dimension_numbe...  26.1 us
    dot_general x9, matrix products, per_device(): jnp.einsum('bhwc,bhwo->co', window, upstream_cols, preferred_element_type...  20.5 us
    dynamic_slice x2, local copies, waits for them, and re-layouts, per_device(): lax.dynamic_slice_in_dim(upstream, chan_index * share, share, 3)  19.5 us
    unnamed x24, local copies, waits for them, and re-layouts  17 us
  transfers between devices with their start and end apart: 13, of which 7 were waited for; matrix products, arithmetic and copies ran while one was open for 28% of the time, Pallas kernels for 0%

commit v1 on v0

v1 whole, which is shorter than its diff:
```python
import math

import jax
import jax.numpy as jnp
from jax import lax
from jax.experimental import pallas as pl
from jax.experimental.pallas import tpu as pltpu
from jax.sharding import PartitionSpec as P

ROWS = 4
COLS = 2
BIG = 56 << 20


def passed_along(value, axis, pairs):
    return lax.ppermute(value, axis, pairs)


def dot_nt(left, right):
    return lax.dot_general(
        left, right, (((1,), (1,)), ((), ())), preferred_element_type=jnp.float32
    )


def dot_nn(left, right):
    return lax.dot_general(
        left, right, (((1,), (0,)), ((), ())), preferred_element_type=jnp.float32
    )


def relay_kernel(field, upstream, pick, field_out, upstream_out, turned_out):
    rows, side, batch, channels = field_out.shape
    for row in range(rows):
        field_out[row] = jnp.swapaxes(field[:, row], 0, 1)
        block = jnp.swapaxes(upstream[:, row], 0, 1)
        upstream_out[row] = block
        turned_out[row] = dot_nt(
            pick[...], block.reshape(side * batch, channels)
        ).astype(jnp.bfloat16)


def relay(field, upstream, pick):
    batch, side, _, channels = field.shape
    share = pick.shape[0]
    rows = 2
    laid = jax.ShapeDtypeStruct((side, side, batch, channels), jnp.bfloat16)
    in_spec = pl.BlockSpec((batch, rows, side, channels), lambda i: (0, i, 0, 0))
    out_spec = pl.BlockSpec((rows, side, batch, channels), lambda i: (i, 0, 0, 0))
    return pl.pallas_call(
        relay_kernel,
        grid=(side // rows,),
        in_specs=[in_spec, in_spec, pl.BlockSpec(memory_space=pltpu.VMEM)],
        out_specs=[
            out_spec,
            out_spec,
            pl.BlockSpec((rows, share, side * batch), lambda i: (i, 0, 0)),
        ],
        out_shape=[
            laid,
            laid,
            jax.ShapeDtypeStruct((side, share, side * batch), jnp.bfloat16),
        ],
        compiler_params=pltpu.CompilerParams(vmem_limit_bytes=BIG),
        cost_estimate=pl.CostEstimate(
            flops=2 * field.size * share, bytes_accessed=8 * field.size, transcendentals=0
        ),
        name="relay",
    )(field, upstream, pick)


def fetch_edges(place, source, held, sems):
    side = held.shape[1]
    for edge in range(3):
        for pos in range(side):
            pixel = place[edge, 0] + pos * place[edge, 1]
            pltpu.make_async_copy(
                source.at[pixel], held.at[edge, pos], sems.at[edge]
            ).start()


def wait_edge(source, held, sems, edge):
    side = held.shape[1]
    pltpu.make_async_copy(
        source.at[pl.ds(0, side)], held.at[edge], sems.at[edge]
    ).wait()


def later(value, width):
    empty = jnp.zeros((value.shape[0], width), value.dtype)
    return jnp.concatenate([empty, value[:, :-width]], axis=1)


def earlier(value, width):
    empty = jnp.zeros((value.shape[0], width), value.dtype)
    return jnp.concatenate([value[:, width:], empty], axis=1)


def edge_kernel(
    place, conv_tap, grad_tap, field, upstream, weight, whole, pick,
    east, west, across, field_edge, upstream_edge, rowed, field_sem, upstream_sem,
):
    share, channels = pick.shape
    taps = weight.shape[0]
    side, batch = field_edge.shape[1:3]
    fetch_edges(place, field, field_edge, field_sem)
    fetch_edges(place, upstream, upstream_edge, upstream_sem)
    for tap in range(taps):
        rowed[tap] = dot_nt(pick[...], whole[tap]).astype(jnp.bfloat16)

    def gathered(product):
        return (
            later(product[:share], batch)
            + product[share : 2 * share]
            + earlier(product[2 * share : 3 * share], batch)
        )

    for edge, out in enumerate((east, west, across)):
        wait_edge(field, field_edge, field_sem, edge)
        wait_edge(upstream, upstream_edge, upstream_sem, edge)
        filters = jnp.concatenate([weight[conv_tap[edge, d]] for d in range(3)], axis=0)
        product = dot_nt(filters, field_edge[edge].reshape(side * batch, channels))
        out[0:share] = gathered(product).astype(jnp.bfloat16)
        filters = jnp.concatenate(
            [rowed[grad_tap[edge, 2 - d]] for d in range(3)] + [pick[...]], axis=0
        )
        product = dot_nt(filters, upstream_edge[edge].reshape(side * batch, channels))
        out[share : 2 * share] = gathered(product).astype(jnp.bfloat16)
        out[2 * share :] = product[3 * share :].astype(jnp.bfloat16)


def edge_messages(place, conv_tap, grad_tap, field, upstream, weight, whole, pick, side):
    pixels, batch, channels = field.shape
    share = pick.shape[0]
    message = jax.ShapeDtypeStruct((3 * share, side * batch), jnp.bfloat16)
    smem = pl.BlockSpec(memory_space=pltpu.SMEM)
    vmem = pl.BlockSpec(memory_space=pltpu.VMEM)
    anywhere = pl.BlockSpec(memory_space=pl.ANY)
    return pl.pallas_call(
        edge_kernel,
        in_specs=[smem] * 3 + [anywhere] * 2 + [vmem] * 3,
        out_specs=[vmem] * 3,
        out_shape=[message] * 3,
        scratch_shapes=[
            pltpu.VMEM((3, side, batch, channels), jnp.bfloat16),
            pltpu.VMEM((3, side, batch, channels), jnp.bfloat16),
            pltpu.VMEM((weight.shape[0], share, channels), jnp.bfloat16),
            pltpu.SemaphoreType.DMA((3,)),
            pltpu.SemaphoreType.DMA((3,)),
        ],
        compiler_params=pltpu.CompilerParams(vmem_limit_bytes=BIG),
        cost_estimate=pl.CostEstimate(
            flops=6 * 7 * share * side * batch * channels,
            bytes_accessed=12 * side * batch * channels,
            transcendentals=0,
        ),
        name="edges",
    )(place, conv_tap, grad_tap, field, upstream, weight, whole, pick)


def filters_kernel(turned, field, out, padded, total, sem):
    step = pl.program_id(0)
    rows, side, batch, channels = field.shape
    share = turned.shape[1]
    width = side * batch

    @pl.when(step == 0)
    def _():
        copy = pltpu.make_async_copy(
            turned, padded.at[pl.ds(1, side), :, pl.ds(batch, width)], sem
        )
        copy.start()
        padded[0] = jnp.zeros(padded.shape[1:], padded.dtype)
        padded[side + 1] = jnp.zeros(padded.shape[1:], padded.dtype)
        column = jnp.zeros((side, share, batch), padded.dtype)
        padded[1 : side + 1, :, 0:batch] = column
        padded[1 : side + 1, :, width + batch :] = column
        total[...] = jnp.zeros_like(total)
        copy.wait()

    first = step * rows
    parts = []
    for col in range(3):
        part = padded[pl.ds(first, rows + 2), :, (2 - col) * batch : (2 - col) * batch + width]
        parts.append(part.reshape((rows + 2) * share, width))
    left = jnp.concatenate(parts, axis=0)
    right = jnp.concatenate([field[row].reshape(width, channels) for row in range(rows)], axis=1)
    total[...] += dot_nn(left, right)

    @pl.when(step == pl.num_programs(0) - 1)
    def _():
        for row_tap in range(3):
            for col_tap in range(3):
                value = jnp.zeros((share, channels), jnp.float32)
                for row in range(rows):
                    start = col_tap * (rows + 2) * share + (row + 2 - row_tap) * share
                    value += total[
                        start : start + share, row * channels : (row + 1) * channels
                    ]
                out[row_tap * 3 + col_tap] = value


def filter_terms(turned, field):
    side, _, batch, channels = field.shape
    share = turned.shape[1]
    rows = 2
    return pl.pallas_call(
        filters_kernel,
        grid=(side // rows,),
        in_specs=[
            pl.BlockSpec(memory_space=pl.ANY),
            pl.BlockSpec((rows, side, batch, channels), lambda i: (i, 0, 0, 0)),
        ],
        out_specs=pl.BlockSpec((9, share, channels), lambda i: (0, 0, 0)),
        out_shape=jax.ShapeDtypeStruct((9, share, channels), jnp.float32),
        scratch_shapes=[
            pltpu.VMEM((side + 2, share, (side + 2) * batch), jnp.bfloat16),
            pltpu.VMEM((3 * (rows + 2) * share, rows * channels), jnp.float32),
            pltpu.SemaphoreType.DMA,
        ],
        compiler_params=pltpu.CompilerParams(vmem_limit_bytes=BIG),
        cost_estimate=pl.CostEstimate(
            flops=24 * share * field.size, bytes_accessed=3 * field.size, transcendentals=0
        ),
        name="filters",
    )(turned, field)


def seam_filters_kernel(
    scale, place, conv_tap, field, inner, east, west, across, out, field_edge, sem
):
    share = out.shape[1]
    side, batch, channels = field_edge.shape[1:]
    fetch_edges(place, field, field_edge, sem)
    out[...] = inner[...]
    for edge, message in enumerate((east, west, across)):
        wait_edge(field, field_edge, sem, edge)
        turned = message[2 * share :]
        left = jnp.concatenate([earlier(turned, batch), turned, later(turned, batch)], axis=0)
        terms = dot_nn(left, field_edge[edge].reshape(side * batch, channels))
        for d in range(3):
            out[conv_tap[edge, d]] += terms[d * share : (d + 1) * share]
    out[...] = out[...] * scale


def seam_filters(scale, place, conv_tap, field, inner, messages, side):
    _, batch, channels = field.shape
    smem = pl.BlockSpec(memory_space=pltpu.SMEM)
    vmem = pl.BlockSpec(memory_space=pltpu.VMEM)

    def body(*refs):
        seam_filters_kernel(scale, *refs)

    return pl.pallas_call(
        body,
        in_specs=[smem] * 2 + [pl.BlockSpec(memory_space=pl.ANY)] + [vmem] * 4,
        out_specs=vmem,
        out_shape=jax.ShapeDtypeStruct(inner.shape, jnp.float32),
        scratch_shapes=[
            pltpu.VMEM((3, side, batch, channels), jnp.bfloat16),
            pltpu.SemaphoreType.DMA((3,)),
        ],
        compiler_params=pltpu.CompilerParams(vmem_limit_bytes=BIG),
        cost_estimate=pl.CostEstimate(
            flops=18 * inner.shape[1] * side * batch * channels,
            bytes_accessed=6 * side * batch * channels,
            transcendentals=0,
        ),
        name="seam_filters",
    )(place, conv_tap, field, inner, *messages)


def conv_kernel(mirrored, source, weight, whole, pick, out, padded, spread, sems):
    step = pl.program_id(0)
    _, side, batch, channels = source.shape
    share = pick.shape[0]
    in_rows, in_cols = ROWS + 2, COLS + 2

    def row_copy(row):
        return pltpu.make_async_copy(
            source.at[row], padded.at[row + 1, pl.ds(1, side)], sems.at[row]
        )

    @pl.when(step == 0)
    def _():
        for row in range(side):
            row_copy(row).start()
        edge = jnp.zeros((side + 2, batch, channels), padded.dtype)
        padded[0] = edge
        padded[side + 1] = edge
        tile = jnp.zeros((batch, channels), padded.dtype)

        @pl.loop(1, side + 1)
        def _(row):
            padded[row, 0] = tile
            padded[row, side + 1] = tile

        spread[...] = jnp.zeros_like(spread)
        for tap in range(9):
            if mirrored:
                block = dot_nt(pick[...], whole[8 - tap]).astype(jnp.bfloat16)
            else:
                block = weight[tap]
            for row in range(ROWS):
                for col in range(COLS):
                    at = (row + tap // 3) * in_cols + col + tap % 3
                    to = row * COLS + col
                    spread[
                        to * share : (to + 1) * share, at * channels : (at + 1) * channels
                    ] = block
        row_copy(0).wait()

    for row in range(ROWS):
        ahead = step * ROWS + row + 1

        @pl.when(ahead < side)
        def _():
            row_copy(ahead).wait()

    first = step * ROWS

    @pl.loop(0, side // (2 * COLS))
    def _(pair):
        rights = []
        for half in range(2):
            start = pair * (2 * COLS) + half * COLS
            rights.append(
                jnp.concatenate(
                    [
                        padded[first + row, start + col]
                        for row in range(in_rows)
                        for col in range(in_cols)
                    ],
                    axis=1,
                )
            )
        result = dot_nt(spread[...], jnp.concatenate(rights, axis=0))
        for half in range(2):
            for row in range(ROWS):
                for col in range(COLS):
                    to = row * COLS + col
                    out[row, pair * (2 * COLS) + half * COLS + col] = result[
                        to * share : (to + 1) * share, half * batch : (half + 1) * batch
                    ].astype(jnp.bfloat16)


def convolved(mirrored, source, weight, whole, pick):
    side, _, batch, channels = source.shape
    share = pick.shape[0]
    vmem = pl.BlockSpec(memory_space=pltpu.VMEM)

    def body(*refs):
        conv_kernel(mirrored, *refs)

    return pl.pallas_call(
        body,
        grid=(side // ROWS,),
        in_specs=[pl.BlockSpec(memory_space=pl.ANY)] + [vmem] * 3,
        out_specs=pl.BlockSpec((ROWS, side, share, batch), lambda i: (i, 0, 0, 0)),
        out_shape=jax.ShapeDtypeStruct((side, side, share, batch), jnp.bfloat16),
        scratch_shapes=[
            pltpu.VMEM((side + 2, side + 2, batch, channels), jnp.bfloat16),
            pltpu.VMEM(
                (ROWS * COLS * share, (ROWS + 2) * (COLS + 2) * channels), jnp.bfloat16
            ),
            pltpu.SemaphoreType.DMA((side,)),
        ],
        compiler_params=pltpu.CompilerParams(vmem_limit_bytes=BIG),
        cost_estimate=pl.CostEstimate(
            flops=48 * share * source.size, bytes_accessed=3 * source.size, transcendentals=0
        ),
        name="grad_conv" if mirrored else "conv",
    )(source, weight, whole, pick)


def border_kernel(
    place, conv_in, grad_in, east, west, across, conv_out, grad_out,
    conv_held, grad_held, in_sem, out_sem,
):
    side, _, share, batch = conv_held.shape

    def pieces(source, target, sem):
        inner = pl.ds(1, side - 2)
        return [
            pltpu.make_async_copy(source.at[where], target.at[where], sem.at[index])
            for index, where in enumerate(
                ((0,), (side - 1,), (inner, 0), (inner, side - 1))
            )
        ]

    def both(step):
        if step == 0:
            return pieces(conv_in, conv_held, in_sem.at[0]) + pieces(
                grad_in, grad_held, in_sem.at[1]
            )
        return pieces(conv_held, conv_out, out_sem.at[0]) + pieces(
            grad_held, grad_out, out_sem.at[1]
        )

    for copy in both(0):
        copy.start()
    for copy in both(0):
        copy.wait()
    for edge, message in enumerate((east, west, across)):
        for pos in range(side):
            pixel = place[edge, 0] + pos * place[edge, 1]
            row, col = pixel // side, pixel % side
            for part, held in enumerate((conv_held, grad_held)):
                term = message[
                    part * share : (part + 1) * share, pos * batch : (pos + 1) * batch
                ]
                held[row, col] = (
                    held[row, col].astype(jnp.float32) + term.astype(jnp.float32)
                ).astype(jnp.bfloat16)
    for copy in both(1):
        copy.start()
    for copy in both(1):
        copy.wait()


def with_borders(place, conv, grad, messages):
    smem = pl.BlockSpec(memory_space=pltpu.SMEM)
    vmem = pl.BlockSpec(memory_space=pltpu.VMEM)
    anywhere = pl.BlockSpec(memory_space=pl.ANY)
    whole = jax.ShapeDtypeStruct(conv.shape, conv.dtype)
    return pl.pallas_call(
        border_kernel,
        in_specs=[smem] + [anywhere] * 2 + [vmem] * 3,
        out_specs=[anywhere] * 2,
        out_shape=[whole] * 2,
        scratch_shapes=[
            pltpu.VMEM(conv.shape, conv.dtype),
            pltpu.VMEM(conv.shape, conv.dtype),
            pltpu.SemaphoreType.DMA((2, 4)),
            pltpu.SemaphoreType.DMA((2, 4)),
        ],
        input_output_aliases={1: 0, 2: 1},
        compiler_params=pltpu.CompilerParams(vmem_limit_bytes=BIG),
        name="borders",
    )(place, conv, grad, *messages)


def stored(turn, row, col, last):
    rows = jnp.stack([row, last - col, last - row, col])
    cols = jnp.stack([col, row, last - col, last - row])
    return jnp.take(rows, turn), jnp.take(cols, turn)


def edge_tables(turns, position, side):
    last = side - 1
    lower = position % 2
    zero = jnp.zeros((), jnp.int32)
    full = jnp.full((), last, jnp.int32)
    edge_row = last * (1 - lower)

    def pixel(row, col):
        r, c = stored(turns[0], row, col, last)
        return r * side + c

    place = []
    for start, end in (
        ((zero, full), (zero + 1, full)),
        ((zero, zero), (zero + 1, zero)),
        ((edge_row, zero), (edge_row, zero + 1)),
    ):
        place.append(jnp.stack([pixel(*start), pixel(*end) - pixel(*start)]))

    def taps(turn, cells):
        out = []
        for row, col in cells:
            r, c = stored(turn, row, col, 2)
            out.append(r * 3 + c)
        return jnp.stack(out)

    ones = [zero + d for d in range(3)]
    two = zero + 2
    conv_tap = jnp.stack(
        [
            taps(turns[1], [(d, zero) for d in ones]),
            taps(turns[2], [(d, two) for d in ones]),
            taps(turns[3], [(2 * lower, d) for d in ones]),
        ]
    )
    grad_tap = jnp.stack(
        [
            taps(turns[0], [(d, two) for d in ones]),
            taps(turns[0], [(d, zero) for d in ones]),
            taps(turns[0], [(2 - 2 * lower, d) for d in ones]),
        ]
    )
    return jnp.stack(place), conv_tap, grad_tap


def per_device(tiles, orientation, weight, grad_out):
    field = tiles[0]
    upstream = grad_out[0]
    batch, side, _, channels = field.shape
    share = weight.shape[3]
    position = lax.axis_index("tile").astype(jnp.int32)
    chan_index = lax.axis_index("chan").astype(jnp.int32)
    count = lax.axis_size("tile")
    eastward = [(i, (i + 2) % count) for i in range(count)]
    westward = [(i, (i - 2) % count) for i in range(count)]
    acrossward = [(i, i ^ 1) for i in range(count)]

    code = orientation.astype(jnp.bfloat16)
    codes = [
        lax.ppermute(code, "tile", pairs) for pairs in (westward, eastward, acrossward)
    ]
    turns = [orientation[0]] + [c[0].astype(jnp.int32) for c in codes]
    place, conv_tap, grad_tap = edge_tables(turns, position, side)

    own = weight.transpose(0, 1, 3, 2).reshape(9, share, channels)
    whole = lax.all_gather(own, "chan", axis=1, tiled=True)
    pick = (
        lax.broadcasted_iota(jnp.int32, (share, channels), 0) + chan_index * share
        == lax.broadcasted_iota(jnp.int32, (share, channels), 1)
    ).astype(jnp.bfloat16)

    field_laid, upstream_laid, turned = relay(field, upstream, pick)
    field_flat = field_laid.reshape(side * side, batch, channels)
    upstream_flat = upstream_laid.reshape(side * side, batch, channels)
    sends = edge_messages(
        place, conv_tap, grad_tap, field_flat, upstream_flat, own, whole, pick, side
    )
    from_west = lax.ppermute(sends[0], "tile", eastward)
    from_east = lax.ppermute(sends[1], "tile", westward)
    from_across = lax.ppermute(sends[2], "tile", acrossward)
    messages = (from_east, from_west, from_across)

    inner = filter_terms(turned, field_laid)
    grad = convolved(True, upstream_laid, own, whole, pick)
    scale = 1.0 / math.sqrt(count * batch * side * side)
    total = seam_filters(scale, place, conv_tap, field_flat, inner, messages, side)
    conv = convolved(False, field_laid, own, whole, pick)
    bit = 1
    while bit < count:
        pairs = [(i, i ^ bit) for i in range(count)]
        total = total + lax.ppermute(total, "tile", pairs)
        bit *= 2
    conv, grad = with_borders(place, conv, grad, messages)
    conv_out = conv.transpose(3, 0, 1, 2)[None]
    grad_input = grad.transpose(3, 0, 1, 2)[None]
    grad_weight = total.reshape(3, 3, share, channels).transpose(0, 1, 3, 2)
    return conv_out, grad_input, grad_weight


def solution(mesh):
    in_specs = (
        P("tile", None, None, None, None),
        P("tile"),
        P(None, None, None, "chan"),
        P("tile", None, None, None, None),
    )
    out_specs = (
        P("tile", None, None, None, "chan"),
        P("tile", None, None, None, "chan"),
        P(None, None, None, "chan"),
    )
    return jax.shard_map(
        per_device, mesh=mesh, in_specs=in_specs, out_specs=out_specs, check_vma=False
    )
```

time: 460 us -> 159 us (0.35); the launches traced: 453 us -> 158 us
  waiting for transfers between devices: 124 us -> 12.2 us
  starting transfers between devices: 106 us -> 16.2 us
  matrix products: 83.1 us -> 0 us
  Pallas kernels: 0 us -> 65 us
  local copies, waits for them, and re-layouts: 81.4 us -> 22.5 us
  other arithmetic: 33.5 us -> 5.31 us
  between operations: 17.8 us -> 28.7 us
    ppermute x12 -> x9, starting transfers between devices: 106 us -> 16.2 us  [the longest x3 10.7 us: per_device(): lax.ppermute(code, 'tile', pairs)]
    ppermute x12 -> x9, waiting for transfers between devices: 81.3 us -> 12.2 us  [the longest x1 7.23 us: per_device(): from_west = lax.ppermute(sends[0], 'tile', eastward)]
    pallas_call x0 -> x7, Pallas kernels: none -> 65 us  [the longest x2 26.8 us: convolved(): pl.pallas_call(body, grid=(side // ROWS,), in_specs=[pl.BlockSpec(memory_...]
    conv_general_dilated x2 -> x0, matrix products: 62.6 us -> none  [the longest x1 36.5 us: per_device(): lax.conv_general_dilated(upstream, flipped, (1, 1), ((2, 2), (2, 2)), dim...]
    psum x1 -> x0, waiting for transfers between devices: 42.3 us -> none  [per_device(): grad_weight = lax.psum(local_grad, 'tile') * normalizer]
    dot_general x9 -> x0, matrix products: 20.5 us -> none  [per_device(): jnp.einsum('bhwc,bhwo->co', window, upstream_cols, preferred_element_type...]
    dynamic_slice x2 -> x0, local copies, waits for them, and re-layouts: 19.5 us -> none  [per_device(): lax.dynamic_slice_in_dim(upstream, chan_index * share, share, 3)]
    another operation x5 -> x27, local copies, waits for them, and re-layouts: 2.83 us -> 20.9 us  [stored(): return (jnp.take(rows, turn), jnp.take(cols, turn))]
  transfers between devices with their start and end apart: 13 -> 9, of which waited for: 7 -> 2; matrix products, arithmetic and copies ran while one was open for 28% -> 11% of each run, Pallas kernels for 0% -> 36%
where the time goes in v1:
time: 159 us; the launch traced here: 158 us
  Pallas kernels  65 us (41%)
  between operations  28.7 us (18%)
  local copies, waits for them, and re-layouts  22.5 us (14%)
  starting transfers between devices  16.2 us (10%)
  waiting for transfers between devices  12.2 us (8%)
  blocking collectives  7.56 us (5%)
  other arithmetic  5.31 us (3%)
    pallas_call x2, Pallas kernels, convolved(): pl.pallas_call(body, grid=(side // ROWS,), in_specs=[pl.BlockSpec(memory_...  26.8 us
    another operation x27, local copies, waits for them, and re-layouts, stored(): return (jnp.take(rows, turn), jnp.take(cols, turn))  20.9 us
    pallas_call x1, Pallas kernels, relay(): pl.pallas_call(relay_kernel, grid=(side // rows,), in_specs=[in_spec, in_...  15.7 us
    ppermute x3, starting transfers between devices, per_device(): lax.ppermute(code, 'tile', pairs)  10.7 us
    pallas_call x1, Pallas kernels, filter_terms(): pl.pallas_call(filters_kernel, grid=(side // rows,), in_specs=[pl.BlockSp...  10.4 us
    all_gather x1, blocking collectives, per_device(): whole = lax.all_gather(own, 'chan', axis=1, tiled=True)  7.56 us
    ppermute x1, waiting for transfers between devices, per_device(): from_west = lax.ppermute(sends[0], 'tile', eastward)  7.23 us
    ppermute x3, waiting for transfers between devices, per_device(): total = total + lax.ppermute(total, 'tile', pairs)  4.97 us
  transfers between devices with their start and end apart: 9, of which 2 were waited for; matrix products, arithmetic and copies ran while one was open for 11% of the time, Pallas kernels for 36%

profile of v1, /device:TPU:0, one launch (start us, length us, event | category | flops | bytes accessed | tf_op | source)
XLA Modules:
  0.0 157.5 jit_solution(3631435638559733811)
XLA Ops:
  1.3 4.3 %collective-permute-start.2 = (bf16[1]{0:T(256)(128)(2,1)}, bf16[1]{0:T(256)(128)(2,1)}, u32[]{:S(2)}, u32[]{:S(2)}) collective-permute-start(bf16[1]{0:T(256)(128)(2,1)} %convert_element_type.25), channel_id=1, source_target_pairs={{0,4},{4,0},{8,12},{12,8},{16,20},{20,16},{24,28},{28,24},{1,5},{5... | collective-permute-start | bytes 14 | tf_op jit(solution)/shard_map/ppermute | solution.py:507
  5.6 2.9 %collective-permute-start.1 = (bf16[1]{0:T(256)(128)(2,1)}, bf16[1]{0:T(256)(128)(2,1)}, u32[]{:S(2)}, u32[]{:S(2)}) collective-permute-start(bf16[1]{0:T(256)(128)(2,1)} %convert_element_type.25), channel_id=1, source_target_pairs={{0,8},{4,12},{8,16},{12,20},{16,24},{20,28},{24,0},{28,4},{1,9},{5... | collective-permute-start | bytes 14 | tf_op jit(solution)/shard_map/ppermute | solution.py:507
  8.5 3.5 %collective-permute-start = (bf16[1]{0:T(256)(128)(2,1)}, bf16[1]{0:T(256)(128)(2,1)}, u32[]{:S(2)}, u32[]{:S(2)}) collective-permute-start(bf16[1]{0:T(256)(128)(2,1)} %convert_element_type.25), channel_id=1, source_target_pairs={{0,24},{4,28},{8,0},{12,4},{16,8},{20,12},{24,16},{28,20},{1,25},{... | collective-permute-start | bytes 14 | tf_op jit(solution)/shard_map/ppermute | solution.py:507
  12.5 1.3 dynamic-slice.154
  13.9 1.2 dynamic-slice.153
  16.3 1.2 dynamic-slice.152
  18.1 1.2 dynamic-slice.151
  19.9 1.2 dynamic-slice.150
  21.7 1.2 dynamic-slice.149
  23.5 1.2 dynamic-slice.148
  25.3 0.6 dynamic-slice.116
  28.9 0.6 dynamic-slice.115
  30.1 0.6 dynamic-slice.114
  31.4 0.6 dynamic-slice.147
  32.7 0.6 dynamic-slice.144
  33.9 0.6 dynamic-slice.142
  35.2 0.6 dynamic-slice.143
  36.4 0.6 dynamic-slice.146
  37.6 0.7 fusion.pick.refs_3_
  38.3 7.6 %all_gather.3.refs_2_.whole = bf16[9,128,128]{2,1,0:T(8,128)(2,1)} all-gather(bf16[9,32,128]{2,1,0:T(8,128)(2,1)} %bitcast.67), channel_id=1, replica_groups=mesh['tile'=8,'chan'=4] {'chan'}, dimensions={1}, use_global_device_ids=true | all-gather | bytes 368640 | tf_op jit(solution)/shard_map/all_gather | solution.py:513
  45.9 0.6 pad_add_fusion.place.refs_0_
  46.7 15.7 %relay.1 = (bf16[16,16,128,128]{3,2,1,0:T(8,128)(2,1)}, bf16[16,16,128,128]{3,2,1,0:T(8,128)(2,1)}, bf16[16,32,2048]{2,1,0:T(8,128)(2,1)}) custom-call(bf16[128,16,16,128]{3,2,1,0:T(8,128)(2,1)} %bitcast.63, bf16[128,16,16,128]{3,2,1,0:T(8,128)(2,1)} %bitcast.64, bf16[32,128]{1,0:T(8,128)(2,1)} %fusion.pick.refs_3_), custom_call_target="tpu_custom_call" | custom-call | flops 268435456 | bytes 33554432 | tf_op jit(solution)/shard_map/relay/pallas_call | solution.py:49
  64.3 0.7 dynamic-slice.132
  64.9 0.7 dynamic-slice.131
  66.2 0.6 dynamic-slice.129
  66.8 0.6 dynamic-slice.128
  71.7 0.7 fusion.17
  74.9 0.7 fusion.21
  78.1 0.7 fusion.19
  81.8 0.7 fusion.23
  86.1 0.6 pad_add_fusion.1.conv_tap.refs_1_
  86.6 0.6 pad_add_fusion.2.grad_tap
  87.2 4.4 %edges.1 = (bf16[96,2048]{1,0:T(8,128)(2,1)}, bf16[96,2048]{1,0:T(8,128)(2,1)}, bf16[96,2048]{1,0:T(8,128)(2,1)}) custom-call(s32[3,2]{1,0:T(4,128)} %pad_add_fusion.place.refs_0_, s32[3,3]{1,0:T(4,128)} %pad_add_fusion.1.conv_tap.refs_1_, s32[3,3]{1,0:T(4,128)} %pad_add_fusion.2.grad_tap, bf16[256,128,128]{2,1,0:T(8,128)(2,1)} %bitcast.60, ...), custom_call_target="tpu_custom_call" | custom-call | flops 352321536 | bytes 3145728 | tf_op jit(solution)/shard_map/edges/pallas_call | solution.py:138
  91.6 1.9 %collective-permute-start.3 = (bf16[96,2048]{1,0:T(8,128)(2,1)}, bf16[96,2048]{1,0:T(8,128)(2,1)S(1)}, u32[]{:S(2)}, u32[]{:S(2)}) collective-permute-start(bf16[96,2048]{1,0:T(8,128)(2,1)} %get-tuple-element.13), channel_id=1, source_target_pairs={{0,24},{4,28},{8,0},{12,4},{16,8},{20,12},{24,16},{28,20},{1,25},{... | collective-permute-start | bytes 1179656 | tf_op jit(solution)/shard_map/ppermute | solution.py:526
  94.2 10.4 %filters.1.refs_3_ = f32[9,32,128]{2,1,0:T(8,128)} custom-call(bf16[16,32,2048]{2,1,0:T(8,128)(2,1)} %get-tuple-element.18.turned, bf16[16,16,128,128]{3,2,1,0:T(8,128)(2,1)} %get-tuple-element.11.refs_0_.field), custom_call_target="tpu_custom_call" | custom-call | flops 3221225472 | bytes 12582912 | tf_op jit(solution)/shard_map/filters/pallas_call | solution.py:206
  104.7 7.2 %collective-permute-done.4.west.refs_5_ = bf16[96,2048]{1,0:T(8,128)(2,1)S(1)} collective-permute-done((bf16[96,2048]{1,0:T(8,128)(2,1)}, bf16[96,2048]{1,0:T(8,128)(2,1)S(1)}, u32[]{:S(2)}, u32[]{:S(2)}) %collective-permute-start.4) | collective-permute-done | bytes 393248 | tf_op jit(solution)/shard_map/ppermute | solution.py:525
  111.9 0.7 copy-done.1
  112.7 0.8 copy-done.2
  113.4 3.8 %seam_filters.1 = f32[9,32,128]{2,1,0:T(8,128)} custom-call(s32[3,2]{1,0:T(4,128)} %pad_add_fusion.place.refs_0_, s32[3,3]{1,0:T(4,128)} %pad_add_fusion.1.conv_tap.refs_1_, bf16[256,128,128]{2,1,0:T(8,128)(2,1)} %bitcast.61, f32[9,32,128]{2,1,0:T(8,128)} %filters.1.refs_3_, bf16[96,2048]{1,0:T(8,128)(2,1)} %copy-done, bf16[96,2048]{1,0:T(8,128)(2,1)} %copy-done.1, ...), custom_call_target="tpu_custom_call" | custom-call | flops 150994944 | bytes 1572864 | tf_op jit(solution)/shard_map/seam_filters/pallas_call | solution.py:253
  117.2 0.6 collective-permute-start.6
  117.8 5.0 %collective-permute-done.6 = f32[9,32,128]{2,1,0:T(8,128)S(1)} collective-permute-done((f32[9,32,128]{2,1,0:T(8,128)}, f32[9,32,128]{2,1,0:T(8,128)S(1)}, u32[]{:S(2)}, u32[]{:S(2)}) %collective-permute-start.6) | collective-permute-done | bytes 147488 | tf_op jit(solution)/shard_map/ppermute | solution.py:538
  122.8 0.9 add.189
  123.7 1.7 %collective-permute-start.7 = (f32[9,32,128]{2,1,0:T(8,128)S(1)}, f32[9,32,128]{2,1,0:T(8,128)S(1)}, u32[]{:S(2)}, u32[]{:S(2)}) collective-permute-start(f32[9,32,128]{2,1,0:T(8,128)S(1)} %add.189), channel_id=1, source_target_pairs={{0,8},{4,12},{8,0},{12,4},{16,24},{20,28},{24,16},{28,20},{1,9},{5... | collective-permute-start | bytes 442376 | tf_op jit(solution)/shard_map/ppermute | solution.py:538
  125.4 13.4 %grad_conv.1.grad_in = bf16[16,16,32,128]{3,2,1,0:T(8,128)(2,1)} custom-call(bf16[16,16,128,128]{3,2,1,0:T(8,128)(2,1)} %get-tuple-element.12.refs_0_, bf16[9,32,128]{2,1,0:T(8,128)(2,1)} %bitcast.69, bf16[9,128,128]{2,1,0:T(8,128)(2,1)} %all_gather.3.refs_2_.whole, bf16[32,128]{1,0:T(8,128)(2,1)} %fusion.pick.refs_3_), custom_call_target="tpu_custom_call" | custom-call | flops 6442450944 | bytes 12582912 | tf_op jit(solution)/shard_map/grad_conv/pallas_call | solution.py:354
  138.9 0.6 collective-permute-start.8
  139.5 13.4 %conv.1.conv_in = bf16[16,16,32,128]{3,2,1,0:T(8,128)(2,1)} custom-call(bf16[16,16,128,128]{3,2,1,0:T(8,128)(2,1)} %get-tuple-element.11.refs_0_.field, bf16[9,32,128]{2,1,0:T(8,128)(2,1)} %bitcast.70, bf16[9,128,128]{2,1,0:T(8,128)(2,1)} %all_gather.3.refs_2_.whole, bf16[32,128]{1,0:T(8,128)(2,1)} %fusion.pick.refs_3_), custom_call_target="tpu_custom_call" | custom-call | flops 6442450944 | bytes 12582912 | tf_op jit(solution)/shard_map/conv/pallas_call | solution.py:354
  152.9 3.9 %borders.1 = (bf16[16,16,32,128]{3,2,1,0:T(8,128)(2,1)}, bf16[16,16,32,128]{3,2,1,0:T(8,128)(2,1)}) custom-call(s32[3,2]{1,0:T(4,128)} %pad_add_fusion.place.refs_0_, bf16[16,16,32,128]{3,2,1,0:T(8,128)(2,1)} %conv.1.conv_in, bf16[16,16,32,128]{3,2,1,0:T(8,128)(2,1)} %grad_conv.1.grad_in, ...), custom_call_target="tpu_custom_call", output_to_operand_aliasing={{0}: (1, {}), {1}: (2, {})} | custom-call | tf_op jit(solution)/shard_map/borders/pallas_call | solution.py:425
  156.8 0.7 add.191
  (51 shorter events, 4.4 us)
Async XLA Ops:
  1.3 61.1 %collective-permute-start.2 = (bf16[1]{0:T(256)(128)(2,1)}, bf16[1]{0:T(256)(128)(2,1)}, u32[]{:S(2)}, u32[]{:S(2)}) collective-permute-start(bf16[1]{0:T(256)(128)(2,1)} %convert_element_type.25), channel_id=1, source_target_pairs={{0,4},{4,0},{8,12},{12,8},{16,20},{20,16},{24,28},{28,24},{1,5},{5... | collective-permute-start | bytes 14 | tf_op jit(solution)/shard_map/ppermute | solution.py:507
  5.6 57.4 %collective-permute-start.1 = (bf16[1]{0:T(256)(128)(2,1)}, bf16[1]{0:T(256)(128)(2,1)}, u32[]{:S(2)}, u32[]{:S(2)}) collective-permute-start(bf16[1]{0:T(256)(128)(2,1)} %convert_element_type.25), channel_id=1, source_target_pairs={{0,8},{4,12},{8,16},{12,20},{16,24},{20,28},{24,0},{28,4},{1,9},{5... | collective-permute-start | bytes 14 | tf_op jit(solution)/shard_map/ppermute | solution.py:507
  8.5 55.2 %collective-permute-start = (bf16[1]{0:T(256)(128)(2,1)}, bf16[1]{0:T(256)(128)(2,1)}, u32[]{:S(2)}, u32[]{:S(2)}) collective-permute-start(bf16[1]{0:T(256)(128)(2,1)} %convert_element_type.25), channel_id=1, source_target_pairs={{0,24},{4,28},{8,0},{12,4},{16,8},{20,12},{24,16},{28,20},{1,25},{... | collective-permute-start | bytes 14 | tf_op jit(solution)/shard_map/ppermute | solution.py:507
  46.6 25.1 %copy-start.7 = (s32[4]{0:T(128)S(1)}, s32[4]{0:T(128)}, u32[]{:S(2)}) copy-start(s32[4]{0:T(128)} %constant.402.clone.1..sunk.4) | copy-start | bytes 52
  46.6 25.1 %copy-start.8 = (s32[4]{0:T(128)S(1)}, s32[4]{0:T(128)}, u32[]{:S(2)}) copy-start(s32[4]{0:T(128)} %constant.401.clone.1..sunk.4) | copy-start | bytes 52
  46.6 28.2 %copy-start.5 = (s32[4]{0:T(128)S(1)}, s32[4]{0:T(128)}, u32[]{:S(2)}) copy-start(s32[4]{0:T(128)} %constant.398.clone.1..sunk.4) | copy-start | bytes 52
  46.6 28.2 %copy-start.6 = (s32[4]{0:T(128)S(1)}, s32[4]{0:T(128)}, u32[]{:S(2)}) copy-start(s32[4]{0:T(128)} %constant.397.clone.1..sunk.4) | copy-start | bytes 52
  46.6 31.4 %copy-start.4 = (s32[4]{0:T(128)S(1)}, s32[4]{0:T(128)}, u32[]{:S(2)}) copy-start(s32[4]{0:T(128)} %constant.396.clone.1..sunk.6) | copy-start | bytes 52
  46.6 31.4 %copy-start.10 = (s32[4]{0:T(128)S(1)}, s32[4]{0:T(128)}, u32[]{:S(2)}) copy-start(s32[4]{0:T(128)} %constant.400.clone.1..sunk.4) | copy-start | bytes 52
  46.7 35.1 %copy-start.3 = (s32[4]{0:T(128)S(1)}, s32[4]{0:T(128)}, u32[]{:S(2)}) copy-start(s32[4]{0:T(128)} %constant.399.clone.1..sunk.6) | copy-start | bytes 52
  46.7 35.1 %copy-start.9 = (s32[4]{0:T(128)S(1)}, s32[4]{0:T(128)}, u32[]{:S(2)}) copy-start(s32[4]{0:T(128)} %constant.394.clone.1..sunk.4) | copy-start | bytes 52
  91.6 13.0 %collective-permute-start.3 = (bf16[96,2048]{1,0:T(8,128)(2,1)}, bf16[96,2048]{1,0:T(8,128)(2,1)S(1)}, u32[]{:S(2)}, u32[]{:S(2)}) collective-permute-start(bf16[96,2048]{1,0:T(8,128)(2,1)} %get-tuple-element.13), channel_id=1, source_target_pairs={{0,24},{4,28},{8,0},{12,4},{16,8},{20,12},{24,16},{28,20},{1,25},{... | collective-permute-start | bytes 1179656 | tf_op jit(solution)/shard_map/ppermute | solution.py:526
  93.5 18.4 %collective-permute-start.4 = (bf16[96,2048]{1,0:T(8,128)(2,1)}, bf16[96,2048]{1,0:T(8,128)(2,1)S(1)}, u32[]{:S(2)}, u32[]{:S(2)}) collective-permute-start(bf16[96,2048]{1,0:T(8,128)(2,1)} %get-tuple-element.14), channel_id=1, source_target_pairs={{0,8},{4,12},{8,16},{12,20},{16,24},{20,28},{24,0},{28,4},{1,9},{5... | collective-permute-start | bytes 1179656 | tf_op jit(solution)/shard_map/ppermute | solution.py:525
  93.7 18.2 %collective-permute-start.5 = (bf16[96,2048]{1,0:T(8,128)(2,1)}, bf16[96,2048]{1,0:T(8,128)(2,1)S(1)}, u32[]{:S(2)}, u32[]{:S(2)}) collective-permute-start(bf16[96,2048]{1,0:T(8,128)(2,1)} %get-tuple-element.15), channel_id=1, source_target_pairs={{0,4},{4,0},{8,12},{12,8},{16,20},{20,16},{24,28},{28,24},{1,5},{5... | collective-permute-start | bytes 1179656 | tf_op jit(solution)/shard_map/ppermute | solution.py:527
  104.7 7.2 %copy-start = (bf16[96,2048]{1,0:T(8,128)(2,1)}, bf16[96,2048]{1,0:T(8,128)(2,1)S(1)}, u32[]{:S(2)}) copy-start(bf16[96,2048]{1,0:T(8,128)(2,1)S(1)} %collective-permute-done.3.east.refs_4_) | copy-start | bytes 1179652
  111.9 0.8 copy-start.1
  112.7 0.8 copy-start.2
  117.2 5.6 %collective-permute-start.6 = (f32[9,32,128]{2,1,0:T(8,128)}, f32[9,32,128]{2,1,0:T(8,128)S(1)}, u32[]{:S(2)}, u32[]{:S(2)}) collective-permute-start(f32[9,32,128]{2,1,0:T(8,128)} %seam_filters.1), channel_id=1, source_target_pairs={{0,4},{4,0},{8,12},{12,8},{16,20},{20,16},{24,28},{28,24},{1,5},{5... | collective-permute-start | bytes 442376 | tf_op jit(solution)/shard_map/ppermute | solution.py:538
  123.7 15.1 %collective-permute-start.7 = (f32[9,32,128]{2,1,0:T(8,128)S(1)}, f32[9,32,128]{2,1,0:T(8,128)S(1)}, u32[]{:S(2)}, u32[]{:S(2)}) collective-permute-start(f32[9,32,128]{2,1,0:T(8,128)S(1)} %add.189), channel_id=1, source_target_pairs={{0,8},{4,12},{8,0},{12,4},{16,24},{20,28},{24,16},{28,20},{1,9},{5... | collective-permute-start | bytes 442376 | tf_op jit(solution)/shard_map/ppermute | solution.py:538
  138.9 18.0 %collective-permute-start.8 = (f32[9,32,128]{2,1,0:T(8,128)S(1)}, f32[9,32,128]{2,1,0:T(8,128)S(1)}, u32[]{:S(2)}, u32[]{:S(2)}) collective-permute-start(f32[9,32,128]{2,1,0:T(8,128)S(1)} %add.190), channel_id=1, source_target_pairs={{0,16},{4,20},{8,24},{12,28},{16,0},{20,4},{24,8},{28,12},{1,17},{... | collective-permute-start | bytes 442376 | tf_op jit(solution)/shard_map/ppermute | solution.py:538

commit v2 on v1

v2 whole, which is shorter than its diff:
```python
import math

import jax
import jax.numpy as jnp
from jax import lax
from jax.experimental import pallas as pl
from jax.experimental.pallas import tpu as pltpu
from jax.sharding import PartitionSpec as P

BIG = 56 << 20
FLAT = (((1,), (0,)), ((), ()))
TURNED = (((1,), (1,)), ((), ()))


def dot(left, right, dims):
    return lax.dot_general(left, right, dims, preferred_element_type=jnp.float32)


def stored(turn, row, col, last):

    def chosen(values):
        return jnp.where(
            turn < 2,
            jnp.where(turn == 0, values[0], values[1]),
            jnp.where(turn == 2, values[2], values[3]),
        )

    return (
        chosen((row, last - col, last - row, col)),
        chosen((col, row, last - col, last - row)),
    )


def edge_place(turn, lower, edge, side):
    last = side - 1
    if edge == 0:
        start, after = (0, last), (1, last)
    elif edge == 1:
        start, after = (0, 0), (1, 0)
    else:
        row = last * (1 - lower)
        start, after = (row, 0), (row, 1)
    first = stored(turn, *start, last)
    second = stored(turn, *after, last)
    return first, (second[0] - first[0], second[1] - first[1])


def edge_tap(turn, lower, edge, along, outward):
    if edge == 0:
        cell = (along, 2 if outward else 0)
    elif edge == 1:
        cell = (along, 0 if outward else 2)
    else:
        cell = (2 - 2 * lower if outward else 2 * lower, along)
    row, col = stored(turn, *cell, 2)
    return row * 3 + col


def one_hot(share, channels):
    chan = lax.axis_index("chan").astype(jnp.int32)
    rows = lax.broadcasted_iota(jnp.int32, (share, channels), 0) + chan * share
    cols = lax.broadcasted_iota(jnp.int32, (share, channels), 1)
    return jnp.where(rows == cols, 1.0, 0.0).astype(jnp.bfloat16)


def relay_kernel(field, upstream, field_out, upstream_out, turned_out, shuffle):
    rows, side, batch, channels = field_out.shape
    share = turned_out.shape[1]
    group = 256 // side

    @pl.when(pl.program_id(0) == 0)
    def _():
        to = lax.broadcasted_iota(jnp.int32, (256, 256), 0)
        come = lax.broadcasted_iota(jnp.int32, (256, 256), 1)
        same = (to // group == come % side) & (to % group == come // side)
        shuffle[...] = jnp.where(same, 1.0, 0.0).astype(jnp.bfloat16)

    for source, out in ((upstream, upstream_out), (field, field_out)):
        for start in range(0, batch, group):
            block = jnp.concatenate(
                [
                    source[start : start + group, row].reshape(256, channels)
                    for row in range(rows)
                ],
                axis=1,
            )
            moved = dot(shuffle[...], block, FLAT).astype(jnp.bfloat16)
            for row in range(rows):
                out[row, :, start : start + group] = moved[
                    :, row * channels : (row + 1) * channels
                ].reshape(side, group, channels)
    pick = one_hot(share, channels)
    for row in range(rows):
        turned_out[row] = dot(
            pick, upstream_out[row].reshape(side * batch, channels), TURNED
        ).astype(jnp.bfloat16)


def relay(field, upstream, share):
    batch, side, _, channels = field.shape
    rows = 2
    laid = jax.ShapeDtypeStruct((side, side, batch, channels), jnp.bfloat16)
    in_spec = pl.BlockSpec((batch, rows, side, channels), lambda i: (0, i, 0, 0))
    out_spec = pl.BlockSpec((rows, side, batch, channels), lambda i: (i, 0, 0, 0))
    return pl.pallas_call(
        relay_kernel,
        grid=(side // rows,),
        in_specs=[in_spec, in_spec],
        out_specs=[
            out_spec,
            out_spec,
            pl.BlockSpec((rows, share, side * batch), lambda i: (i, 0, 0)),
        ],
        out_shape=[
            laid,
            laid,
            jax.ShapeDtypeStruct((side, share, side * batch), jnp.bfloat16),
        ],
        scratch_shapes=[pltpu.VMEM((256, 256), jnp.bfloat16)],
        compiler_params=pltpu.CompilerParams(vmem_limit_bytes=BIG),
        cost_estimate=pl.CostEstimate(
            flops=1024 * field.size, bytes_accessed=8 * field.size, transcendentals=0
        ),
        name="relay",
    )(field, upstream)


def fetch_edges(turn, lower, source, held, sems):
    side = held.shape[1]
    for edge in range(3):
        (row, col), (down, right) = edge_place(turn, lower, edge, side)
        for pos in range(side):
            pltpu.make_async_copy(
                source.at[row + pos * down, col + pos * right],
                held.at[edge, pos],
                sems.at[edge],
            ).start()


def wait_edge(source, held, sems, edge):
    pltpu.make_async_copy(source.at[0], held.at[edge], sems.at[edge]).wait()


def later(value, width):
    empty = jnp.zeros((value.shape[0], width), value.dtype)
    return jnp.concatenate([empty, value[:, :-width]], axis=1)


def earlier(value, width):
    empty = jnp.zeros((value.shape[0], width), value.dtype)
    return jnp.concatenate([value[:, width:], empty], axis=1)


def gather_filters(parts, whole):
    taps, share, _ = parts[0].shape
    chan = lax.axis_index("chan").astype(jnp.int32)
    for flip, part in enumerate(parts):
        start = pl.multiple_of((chan ^ flip) * share, share)
        for tap in range(taps):
            whole[tap, pl.ds(start, share)] = part[tap]


def edge_kernel(
    own_turn, east_turn, west_turn, across_turn, field, upstream, weight, *refs
):
    others = refs[:-10]
    east, west, across = refs[-10:-7]
    field_edge, upstream_edge, whole, rowed, field_sem, upstream_sem, _ = refs[-7:]
    taps, share, channels = weight.shape
    side, batch = field_edge.shape[1:3]
    lower = lax.axis_index("tile").astype(jnp.int32) % 2
    turn = own_turn[0]
    fetch_edges(turn, lower, field, field_edge, field_sem)
    fetch_edges(turn, lower, upstream, upstream_edge, upstream_sem)
    pick = one_hot(share, channels)
    gather_filters((weight,) + others, whole)
    for tap in range(taps):
        rowed[tap] = dot(pick, whole[tap], TURNED).astype(jnp.bfloat16)

    def gathered(product):
        return (
            later(product[:share], batch)
            + product[share : 2 * share]
            + earlier(product[2 * share : 3 * share], batch)
        )

    turns = (east_turn[0], west_turn[0], across_turn[0])
    for edge, out in enumerate((east, west, across)):
        wait_edge(field, field_edge, field_sem, edge)
        wait_edge(upstream, upstream_edge, upstream_sem, edge)
        filters = jnp.concatenate(
            [weight[edge_tap(turns[edge], lower, edge, d, False)] for d in range(3)], axis=0
        )
        product = dot(filters, field_edge[edge].reshape(side * batch, channels), TURNED)
        out[0:share] = gathered(product).astype(jnp.bfloat16)
        filters = jnp.concatenate(
            [rowed[edge_tap(turn, lower, edge, 2 - d, True)] for d in range(3)] + [pick],
            axis=0,
        )
        product = dot(filters, upstream_edge[edge].reshape(side * batch, channels), TURNED)
        out[share : 2 * share] = gathered(product).astype(jnp.bfloat16)
        out[2 * share :] = product[3 * share :].astype(jnp.bfloat16)


def edge_messages(turns, field, upstream, weights):
    side, _, batch, channels = field.shape
    taps, share, _ = weights[0].shape
    message = jax.ShapeDtypeStruct((3 * share, side * batch), jnp.bfloat16)
    smem = pl.BlockSpec(memory_space=pltpu.SMEM)
    vmem = pl.BlockSpec(memory_space=pltpu.VMEM)
    anywhere = pl.BlockSpec(memory_space=pl.ANY)
    return pl.pallas_call(
        edge_kernel,
        in_specs=[smem] * 4 + [anywhere] * 2 + [vmem] * len(weights),
        out_specs=[vmem] * 3,
        out_shape=[message] * 3,
        scratch_shapes=[
            pltpu.VMEM((3, side, batch, channels), jnp.bfloat16),
            pltpu.VMEM((3, side, batch, channels), jnp.bfloat16),
            pltpu.VMEM((taps, channels, channels), jnp.bfloat16),
            pltpu.VMEM((taps, share, channels), jnp.bfloat16),
            pltpu.SemaphoreType.DMA((3,)),
            pltpu.SemaphoreType.DMA((3,)),
            pltpu.SMEM((1,), jnp.int32),
        ],
        compiler_params=pltpu.CompilerParams(vmem_limit_bytes=BIG),
        cost_estimate=pl.CostEstimate(
            flops=6 * 7 * share * side * batch * channels,
            bytes_accessed=12 * side * batch * channels,
            transcendentals=0,
        ),
        name="edges",
    )(*turns, field, upstream, *weights)


def filters_kernel(turned, field, out, padded, total, sem):
    step = pl.program_id(0)
    rows, side, batch, channels = field.shape
    share = turned.shape[1]
    width = side * batch

    @pl.when(step == 0)
    def _():
        copy = pltpu.make_async_copy(
            turned, padded.at[pl.ds(1, side), :, pl.ds(batch, width)], sem
        )
        copy.start()
        padded[0] = jnp.zeros(padded.shape[1:], padded.dtype)
        padded[side + 1] = jnp.zeros(padded.shape[1:], padded.dtype)
        column = jnp.zeros((side, share, batch), padded.dtype)
        padded[1 : side + 1, :, 0:batch] = column
        padded[1 : side + 1, :, width + batch :] = column
        total[...] = jnp.zeros_like(total)
        copy.wait()

    first = step * rows
    cols = 4
    for start in range(0, side, cols):
        parts = []
        for tap in range(3):
            at = (start + 2 - tap) * batch
            part = padded[pl.ds(first, rows + 2), :, at : at + cols * batch]
            parts.append(part.reshape((rows + 2) * share, cols * batch))
        left = jnp.concatenate(parts, axis=0)
        right = jnp.concatenate(
            [
                field[row, start : start + cols].reshape(cols * batch, channels)
                for row in range(rows)
            ],
            axis=1,
        )
        total[...] += dot(left, right, FLAT)

    @pl.when(step == pl.num_programs(0) - 1)
    def _():
        for row_tap in range(3):
            for col_tap in range(3):
                value = jnp.zeros((share, channels), jnp.float32)
                for row in range(rows):
                    start = col_tap * (rows + 2) * share + (row + 2 - row_tap) * share
                    value += total[
                        start : start + share, row * channels : (row + 1) * channels
                    ]
                out[row_tap * 3 + col_tap] = value


def filter_terms(turned, field):
    side, _, batch, channels = field.shape
    share = turned.shape[1]
    rows = 2
    return pl.pallas_call(
        filters_kernel,
        grid=(side // rows,),
        in_specs=[
            pl.BlockSpec(memory_space=pl.ANY),
            pl.BlockSpec((rows, side, batch, channels), lambda i: (i, 0, 0, 0)),
        ],
        out_specs=pl.BlockSpec((9, share, channels), lambda i: (0, 0, 0)),
        out_shape=jax.ShapeDtypeStruct((9, share, channels), jnp.float32),
        scratch_shapes=[
            pltpu.VMEM((side + 2, share, (side + 2) * batch), jnp.bfloat16),
            pltpu.VMEM((3 * (rows + 2) * share, rows * channels), jnp.float32),
            pltpu.SemaphoreType.DMA,
        ],
        compiler_params=pltpu.CompilerParams(vmem_limit_bytes=BIG),
        cost_estimate=pl.CostEstimate(
            flops=24 * share * field.size, bytes_accessed=3 * field.size, transcendentals=0
        ),
        name="filters",
    )(turned, field)


def seam_kernel(
    scale, own_turn, east_turn, west_turn, across_turn, field, after, inner,
    east, west, across, out, field_edge, sem,
):
    share = out.shape[1]
    side, batch, channels = field_edge.shape[1:]
    lower = lax.axis_index("tile").astype(jnp.int32) % 2
    turns = (east_turn[0], west_turn[0], across_turn[0])
    fetch_edges(own_turn[0], lower, field, field_edge, sem)
    out[...] = inner[...]
    for edge, message in enumerate((east, west, across)):
        wait_edge(field, field_edge, sem, edge)
        turned = message[2 * share :]
        left = jnp.concatenate([earlier(turned, batch), turned, later(turned, batch)], axis=0)
        terms = dot(left, field_edge[edge].reshape(side * batch, channels), FLAT)
        for d in range(3):
            tap = edge_tap(turns[edge], lower, edge, d, False)
            out[tap] += terms[d * share : (d + 1) * share]
    out[...] = out[...] * scale


def seam_filters(scale, turns, field, after, inner, messages):
    side, _, batch, channels = field.shape
    smem = pl.BlockSpec(memory_space=pltpu.SMEM)
    vmem = pl.BlockSpec(memory_space=pltpu.VMEM)
    anywhere = pl.BlockSpec(memory_space=pl.ANY)

    def body(*refs):
        seam_kernel(scale, *refs)

    return pl.pallas_call(
        body,
        in_specs=[smem] * 4 + [anywhere] * 2 + [vmem] * 4,
        out_specs=vmem,
        out_shape=jax.ShapeDtypeStruct(inner.shape, jnp.float32),
        scratch_shapes=[
            pltpu.VMEM((3, side, batch, channels), jnp.bfloat16),
            pltpu.SemaphoreType.DMA((3,)),
        ],
        compiler_params=pltpu.CompilerParams(vmem_limit_bytes=BIG),
        cost_estimate=pl.CostEstimate(
            flops=18 * inner.shape[1] * side * batch * channels,
            bytes_accessed=6 * side * batch * channels,
            transcendentals=0,
        ),
        name="seam_filters",
    )(*turns, field, after, inner, *messages)


def padded_rows(source, padded, sems):
    side, _, batch, channels = source.shape

    def row_copy(row):
        return pltpu.make_async_copy(
            source.at[row], padded.at[row, pl.ds(1, side)], sems.at[row]
        )

    for row in range(side):
        row_copy(row).start()
    tile = jnp.zeros((batch, channels), padded.dtype)

    @pl.loop(0, side)
    def _(row):
        padded[row, 0] = tile
        padded[row, side + 1] = tile

    return row_copy


def spread_filters(block_of, spread, share, channels):
    empty = jnp.zeros((share, channels), spread.dtype)
    for row in range(3):
        for out_col in range(2):
            for in_col in range(4):
                tap = in_col - out_col
                to = (row * 2 + out_col) * share
                at = in_col * channels
                spread[to : to + share, at : at + channels] = (
                    block_of(row, tap) if 0 <= tap <= 2 else empty
                )


def convolve_rows(row_copy, padded, spread, sums, finished, share):
    side, cols, batch, channels = padded.shape
    cols -= 2

    @pl.loop(0, side)
    def _(row):
        row_copy(row).wait()
        for start in range(0, cols, 4):
            right = jnp.concatenate(
                [
                    jnp.concatenate(
                        [padded[row, start + half + col] for col in range(4)], axis=1
                    )
                    for half in (0, 2)
                ],
                axis=0,
            )
            terms = dot(spread[...], right, TURNED)
            for half in (0, 2):
                for col in range(2):
                    at = start + half + col
                    part = [
                        terms[
                            (k * 2 + col) * share : (k * 2 + col + 1) * share,
                            half // 2 * batch : (half // 2 + 1) * batch,
                        ]
                        for k in range(3)
                    ]
                    sums[row + 2, at] += part[0]
                    sums[row + 1, at] += part[1]
                    finished(row, at, sums[row, at] + part[2])

    for at in range(cols):
        finished(side, at, sums[side, at])


def grad_kernel(weight, other1, other2, other3, source, out, padded, spread, sums, whole, sems):
    side, _, batch, channels = source.shape
    share = weight.shape[1]
    row_copy = padded_rows(source, padded, sems)
    gather_filters((weight, other1, other2, other3), whole)
    pick = one_hot(share, channels)

    def block_of(row, col):
        return dot(pick, whole[8 - row * 3 - col], TURNED).astype(jnp.bfloat16)

    spread_filters(block_of, spread, share, channels)
    sums[...] = jnp.zeros_like(sums)

    def finished(row, col, value):
        out[jnp.maximum(row - 1, 0), col] = value.astype(out.dtype)

    convolve_rows(row_copy, padded, spread, sums, finished, share)


def grad_conv(source, weights):
    side, _, batch, channels = source.shape
    taps, share, _ = weights[0].shape
    vmem = pl.BlockSpec(memory_space=pltpu.VMEM)
    return pl.pallas_call(
        grad_kernel,
        in_specs=[vmem] * len(weights) + [pl.BlockSpec(memory_space=pl.ANY)],
        out_specs=vmem,
        out_shape=jax.ShapeDtypeStruct((side, side, share, batch), jnp.bfloat16),
        scratch_shapes=[
            pltpu.VMEM((side, side + 2, batch, channels), jnp.bfloat16),
            pltpu.VMEM((6 * share, 4 * channels), jnp.bfloat16),
            pltpu.VMEM((side + 2, side, share, batch), jnp.float32),
            pltpu.VMEM((taps, channels, channels), jnp.bfloat16),
            pltpu.SemaphoreType.DMA((side,)),
        ],
        compiler_params=pltpu.CompilerParams(vmem_limit_bytes=BIG),
        cost_estimate=pl.CostEstimate(
            flops=24 * share * source.size, bytes_accessed=3 * source.size, transcendentals=0
        ),
        name="grad_conv",
    )(*weights, source)


def border_pieces(side, source, target, sems):
    inner = pl.ds(1, side - 2)
    return [
        pltpu.make_async_copy(source.at[where], target.at[where], sems.at[index])
        for index, where in enumerate(((0,), (side - 1,), (inner, 0), (inner, side - 1)))
    ]


def conv_kernel(
    own_turn, weight, source, east, west, across, grad_in, out, grad_out,
    padded, spread, sums, grad_held, sems, in_sems, out_sems,
):
    side, _, batch, channels = source.shape
    share = weight.shape[1]
    row_copy = padded_rows(source, padded, sems)
    for copy in border_pieces(side, grad_in, grad_held, in_sems):
        copy.start()

    def block_of(row, col):
        return weight[row * 3 + col]

    spread_filters(block_of, spread, share, channels)
    sums[...] = jnp.zeros_like(sums)
    lower = lax.axis_index("tile").astype(jnp.int32) % 2
    turn = own_turn[0]
    for copy in border_pieces(side, grad_in, grad_held, in_sems):
        copy.wait()
    for edge, message in enumerate((east, west, across)):
        (row, col), (down, right) = edge_place(turn, lower, edge, side)
        for pos in range(side):
            here, there = row + pos * down, col + pos * right
            lanes = slice(pos * batch, (pos + 1) * batch)
            sums[here + 1, there] += message[0:share, lanes].astype(jnp.float32)
            term = message[share : 2 * share, lanes].astype(jnp.float32)
            grad_held[here, there] = (
                grad_held[here, there].astype(jnp.float32) + term
            ).astype(jnp.bfloat16)
    for copy in border_pieces(side, grad_held, grad_out, out_sems):
        copy.start()

    def finished(row, col, value):
        out[jnp.maximum(row - 1, 0), col] = value.astype(out.dtype)

    convolve_rows(row_copy, padded, spread, sums, finished, share)
    for copy in border_pieces(side, grad_held, grad_out, out_sems):
        copy.wait()


def conv_and_borders(turn, weight, source, messages, grad):
    side, _, batch, channels = source.shape
    _, share, _ = weight.shape
    smem = pl.BlockSpec(memory_space=pltpu.SMEM)
    vmem = pl.BlockSpec(memory_space=pltpu.VMEM)
    anywhere = pl.BlockSpec(memory_space=pl.ANY)
    shape = jax.ShapeDtypeStruct((side, side, share, batch), jnp.bfloat16)
    return pl.pallas_call(
        conv_kernel,
        in_specs=[smem, vmem, anywhere] + [vmem] * 3 + [anywhere],
        out_specs=[vmem, anywhere],
        out_shape=[shape, shape],
        scratch_shapes=[
            pltpu.VMEM((side, side + 2, batch, channels), jnp.bfloat16),
            pltpu.VMEM((6 * share, 4 * channels), jnp.bfloat16),
            pltpu.VMEM((side + 2, side, share, batch), jnp.float32),
            pltpu.VMEM((side, side, share, batch), jnp.bfloat16),
            pltpu.SemaphoreType.DMA((side,)),
            pltpu.SemaphoreType.DMA((4,)),
            pltpu.SemaphoreType.DMA((4,)),
        ],
        input_output_aliases={6: 1},
        compiler_params=pltpu.CompilerParams(vmem_limit_bytes=BIG),
        cost_estimate=pl.CostEstimate(
            flops=24 * share * source.size, bytes_accessed=3 * source.size, transcendentals=0
        ),
        name="conv",
    )(turn, weight, source, *messages, grad)


def per_device(tiles, orientation, weight, grad_out):
    field = tiles[0]
    upstream = grad_out[0]
    batch, side, _, channels = field.shape
    share = weight.shape[3]
    count = lax.axis_size("tile")
    eastward = [(i, (i + 2) % count) for i in range(count)]
    westward = [(i, (i - 2) % count) for i in range(count)]
    acrossward = [(i, i ^ 1) for i in range(count)]

    turns = [orientation] + [
        lax.ppermute(orientation, "tile", pairs)
        for pairs in (westward, eastward, acrossward)
    ]
    own = weight.transpose(0, 1, 3, 2).reshape(9, share, channels)
    weights = [own] + [
        lax.ppermute(own, "chan", [(i, i ^ flip) for i in range(channels // share)])
        for flip in range(1, channels // share)
    ]

    field_laid, upstream_laid, turned = relay(field, upstream, share)
    sends = edge_messages(turns, field_laid, upstream_laid, weights)
    from_west = lax.ppermute(sends[0], "tile", eastward)
    from_east = lax.ppermute(sends[1], "tile", westward)
    from_across = lax.ppermute(sends[2], "tile", acrossward)
    messages = (from_east, from_west, from_across)

    inner = filter_terms(turned, field_laid)
    grad = grad_conv(upstream_laid, weights)
    scale = 1.0 / math.sqrt(count * batch * side * side)
    total = seam_filters(scale, turns, field_laid, grad, inner, messages)
    conv, grad = conv_and_borders(orientation, own, field_laid, messages, grad)
    bit = 1
    while bit < count:
        pairs = [(i, i ^ bit) for i in range(count)]
        total = total + lax.ppermute(total, "tile", pairs)
        bit *= 2
    conv_out = conv.transpose(3, 0, 1, 2)[None]
    grad_input = grad.transpose(3, 0, 1, 2)[None]
    grad_weight = total.reshape(3, 3, share, channels).transpose(0, 1, 3, 2)
    return conv_out, grad_input, grad_weight


def solution(mesh):
    in_specs = (
        P("tile", None, None, None, None),
        P("tile"),
        P(None, None, None, "chan"),
        P("tile", None, None, None, None),
    )
    out_specs = (
        P("tile", None, None, None, "chan"),
        P("tile", None, None, None, "chan"),
        P(None, None, None, "chan"),
    )
    return jax.shard_map(
        per_device, mesh=mesh, in_specs=in_specs, out_specs=out_specs, check_vma=False
    )
```

time: 159 us -> 99.5 us (0.63)
  between operations: 28.7 us -> 1.43 us
  local copies, waits for them, and re-layouts: 22.5 us -> 2.34 us
  blocking collectives: 7.56 us -> 0 us
  other arithmetic: 5.31 us -> 1.64 us
  waiting for transfers between devices: 12.2 us -> 13.8 us
    another operation x27 -> x0, local copies, waits for them, and re-layouts: 20.9 us -> none  [stored(): return (jnp.take(rows, turn), jnp.take(cols, turn))]
    all_gather x1 -> x0, blocking collectives: 7.56 us -> none  [per_device(): whole = lax.all_gather(own, 'chan', axis=1, tiled=True)]
    ppermute x1, waiting for transfers between devices: 7.23 us -> 0.01 us  [per_device(): from_west = lax.ppermute(sends[0], 'tile', eastward)]
    ppermute x3, waiting for transfers between devices: 4.97 us -> 11.6 us  [per_device(): total = total + lax.ppermute(total, 'tile', pairs)]
    another operation x19 -> x0, other arithmetic: 3 us -> none  [the longest x4 0.82 us: edge_tables(): jnp.stack([taps(turns[1], [(d, zero) for d in ones]), taps(turns[2], [(d,...]
    ppermute x3 -> x6, waiting for transfers between devices: 0.01 us -> 2.15 us  [the longest x3 2.14 us: per_device(): lax.ppermute(orientation, 'tile', pairs)]
    ppermute x3 -> x6, starting transfers between devices: 10.7 us -> 8.74 us  [the longest x3 6.88 us: per_device(): lax.ppermute(orientation, 'tile', pairs)]
    pallas_call x5 -> x4, Pallas kernels: 38.9 us -> 38.1 us  [the longest x1 14.7 us: conv_and_borders(): pl.pallas_call(conv_kernel, in_specs=[smem, vmem, anywhere] + [vmem] * 3...]
  transfers between devices with their start and end apart: 9 -> 12, of which waited for: 2 -> 3; matrix products, arithmetic and copies ran while one was open for 11% -> 0% of each run, Pallas kernels for 36% -> 53%
where the time goes in v2:
time: 99.5 us; the launch traced here: 98.7 us
  Pallas kernels  64.6 us (65%)
  starting transfers between devices  15 us (15%)
  waiting for transfers between devices  13.8 us (14%)
  local copies, waits for them, and re-layouts  2.34 us (2%)
  other arithmetic  1.64 us (2%)
  between operations  1.43 us (1%)
    pallas_call x1, Pallas kernels, relay(): pl.pallas_call(relay_kernel, grid=(side // rows,), in_specs=[in_spec, in_...  16.1 us
    pallas_call x1, Pallas kernels, conv_and_borders(): pl.pallas_call(conv_kernel, in_specs=[smem, vmem, anywhere] + [vmem] * 3...  14.7 us
    ppermute x3, waiting for transfers between devices, per_device(): total = total + lax.ppermute(total, 'tile', pairs)  11.6 us
    pallas_call x1, Pallas kernels, grad_conv(): pl.pallas_call(grad_kernel, in_specs=[vmem] * len(weights) + [pl.BlockSpe...  11.6 us
    pallas_call x1, Pallas kernels, filter_terms(): pl.pallas_call(filters_kernel, grid=(side // rows,), in_specs=[pl.BlockSp...  10.4 us
    ppermute x3, starting transfers between devices, per_device(): lax.ppermute(orientation, 'tile', pairs)  6.88 us
    pallas_call x1, Pallas kernels, edge_messages(): pl.pallas_call(edge_kernel, in_specs=[smem] * 4 + [anywhere] * 2 + [vmem]...  6.2 us
    pallas_call x1, Pallas kernels, seam_filters(): pl.pallas_call(body, in_specs=[smem] * 4 + [anywhere] * 2 + [vmem] * 4, o...  5.59 us
  transfers between devices with their start and end apart: 12, of which 3 were waited for; matrix products, arithmetic and copies ran while one was open for 0% of the time, Pallas kernels for 53%

profile of v2, /device:TPU:0, one launch (start us, length us, event | category | flops | bytes accessed | tf_op | source)
XLA Modules:
  0.0 98.7 jit_solution(12999149553497313200)
XLA Ops:
  0.6 3.1 %collective-permute-start.1 = (s32[1]{0:T(128)}, s32[1]{0:T(128)}, u32[]{:S(2)}, u32[]{:S(2)}) collective-permute-start(s32[1]{0:T(128)} %param.5), channel_id=1, source_target_pairs={{0,8},{4,12},{8,16},{12,20},{16,24},{20,28},{24,0},{28,4},{1,9},{5... | collective-permute-start | bytes 20 | tf_op jit(solution)/shard_map/ppermute | solution.py:563
  3.7 2.1 %collective-permute-start = (s32[1]{0:T(128)}, s32[1]{0:T(128)}, u32[]{:S(2)}, u32[]{:S(2)}) collective-permute-start(s32[1]{0:T(128)} %param.5), channel_id=1, source_target_pairs={{0,24},{4,28},{8,0},{12,4},{16,8},{20,12},{24,16},{28,20},{1,25},{... | collective-permute-start | bytes 20 | tf_op jit(solution)/shard_map/ppermute | solution.py:563
  5.8 0.7 collective-permute-start.5
  6.5 1.0 %collective-permute-start.4 = (bf16[9,32,128]{2,1,0:T(8,128)(2,1)}, bf16[9,32,128]{2,1,0:T(8,128)(2,1)S(1)}, u32[]{:S(2)}, u32[]{:S(2)}) collective-permute-start(bf16[9,32,128]{2,1,0:T(8,128)(2,1)} %bitcast.19), channel_id=1, source_target_pairs={{0,2},{1,3},{2,0},{3,1},{4,6},{5,7},{6,4},{7,5},{8,10},{9,11},{10,... | collective-permute-start | bytes 221192 | tf_op jit(solution)/shard_map/ppermute | solution.py:568
  7.5 0.2 collective-permute-start.3
  7.7 16.1 %relay.1 = (bf16[16,16,128,128]{3,2,1,0:T(8,128)(2,1)}, bf16[16,16,128,128]{3,2,1,0:T(8,128)(2,1)}, bf16[16,32,2048]{2,1,0:T(8,128)(2,1)}) custom-call(bf16[128,16,16,128]{3,2,1,0:T(8,128)(2,1)} %bitcast.14, bf16[128,16,16,128]{3,2,1,0:T(8,128)(2,1)} %bitcast.15), custom_call_target="tpu_custom_call" | custom-call | flops 4294967296 | bytes 33554432 | tf_op jit(solution)/shard_map/relay/pallas_call | solution.py:105
  24.4 0.0 collective-permute-done.1.west_turn.refs_2_
  24.4 1.7 %collective-permute-start.2 = (s32[1]{0:T(128)}, s32[1]{0:T(128)}, u32[]{:S(2)}, u32[]{:S(2)}) collective-permute-start(s32[1]{0:T(128)} %param.5), channel_id=1, source_target_pairs={{0,4},{4,0},{8,12},{12,8},{16,20},{20,16},{24,28},{28,24},{1,5},{5... | collective-permute-start | bytes 20 | tf_op jit(solution)/shard_map/ppermute | solution.py:563
  26.1 0.0 collective-permute-done.east_turn.refs_1_
  26.1 2.1 %collective-permute-done.2.across_turn.refs_3_ = s32[1]{0:T(128)} collective-permute-done((s32[1]{0:T(128)}, s32[1]{0:T(128)}, u32[]{:S(2)}, u32[]{:S(2)}) %collective-permute-start.2) | collective-permute-done | bytes 36 | tf_op jit(solution)/shard_map/ppermute | solution.py:563
  28.2 0.0 collective-permute-done.5.refs_2_.other3
  28.2 0.0 copy-start.3
  28.2 0.0 collective-permute-done.4.refs_1_.other2
  28.3 0.0 copy-start.4
  28.3 0.0 collective-permute-done.3.refs_0_.other1
  28.3 0.0 copy-start.5
  28.3 0.6 copy-done.3
  28.9 0.0 copy-done.4
  28.9 0.0 copy-done.5
  28.9 6.2 %edges.1 = (bf16[96,2048]{1,0:T(8,128)(2,1)}, bf16[96,2048]{1,0:T(8,128)(2,1)}, bf16[96,2048]{1,0:T(8,128)(2,1)}) custom-call(s32[1]{0:T(128)S(6)} %copy.9.own_turn.refs_0_, s32[1]{0:T(128)} %collective-permute-done.east_turn.refs_1_, s32[1]{0:T(128)} %collective-permute-done.1.west_turn.refs_2_, s32[1]{0:T(128)} %collective-permute-done.2.across_turn.refs_3_, ...), custom_call_target="tpu_custom_call" | custom-call | flops 352321536 | bytes 3145728 | tf_op jit(solution)/shard_map/edges/pallas_call | solution.py:212
  35.1 2.0 %collective-permute-start.6 = (bf16[96,2048]{1,0:T(8,128)(2,1)}, bf16[96,2048]{1,0:T(8,128)(2,1)S(1)}, u32[]{:S(2)}, u32[]{:S(2)}) collective-permute-start(bf16[96,2048]{1,0:T(8,128)(2,1)} %get-tuple-element.13), channel_id=1, source_target_pairs={{0,24},{4,28},{8,0},{12,4},{16,8},{20,12},{24,16},{28,20},{1,25},{... | collective-permute-start | bytes 1179656 | tf_op jit(solution)/shard_map/ppermute | solution.py:575
  37.2 0.1 collective-permute-start.7
  37.2 1.6 %collective-permute-start.8 = (bf16[96,2048]{1,0:T(8,128)(2,1)}, bf16[96,2048]{1,0:T(8,128)(2,1)S(1)}, u32[]{:S(2)}, u32[]{:S(2)}) collective-permute-start(bf16[96,2048]{1,0:T(8,128)(2,1)} %get-tuple-element.15), channel_id=1, source_target_pairs={{0,4},{4,0},{8,12},{12,8},{16,20},{20,16},{24,28},{28,24},{1,5},{5... | collective-permute-start | bytes 1179656 | tf_op jit(solution)/shard_map/ppermute | solution.py:576
  38.9 10.4 %filters.1.refs_6_ = f32[9,32,128]{2,1,0:T(8,128)} custom-call(bf16[16,32,2048]{2,1,0:T(8,128)(2,1)} %get-tuple-element.18.turned, bf16[16,16,128,128]{3,2,1,0:T(8,128)(2,1)} %get-tuple-element.11.field.source.refs_4_), custom_call_target="tpu_custom_call" | custom-call | flops 3221225472 | bytes 12582912 | tf_op jit(solution)/shard_map/filters/pallas_call | solution.py:291
  49.3 11.6 %grad_conv.1.grad_in.refs_5_ = bf16[16,16,32,128]{3,2,1,0:T(8,128)(2,1)} custom-call(bf16[9,32,128]{2,1,0:T(8,128)(2,1)} %bitcast.22, bf16[9,32,128]{2,1,0:T(8,128)(2,1)} %copy-done.5, bf16[9,32,128]{2,1,0:T(8,128)(2,1)} %copy-done.4, bf16[9,32,128]{2,1,0:T(8,128)(2,1)} %copy-done.3, bf16[16,16,128,128]{3,2,1,0:T(8,128)(2,1)} %get-tuple-element.12.upstream.source), custom_call_target="tpu_custom_call" | custom-call | flops 3221225472 | bytes 12582912 | tf_op jit(solution)/shard_map/grad_conv/pallas_call | solution.py:454
  60.9 0.0 collective-permute-done.6.east.refs_7_
  60.9 0.0 copy-start
  60.9 0.0 collective-permute-done.7.west.refs_8_
  60.9 0.0 copy-start.1
  60.9 0.0 collective-permute-done.8.across.refs_9_
  60.9 0.7 copy-done
  61.7 0.2 copy-done.1
  61.9 0.0 copy-start.2
  61.9 0.7 copy-done.2
  62.6 5.6 %seam_filters.1 = f32[9,32,128]{2,1,0:T(8,128)} custom-call(s32[1]{0:T(128)S(6)} %copy.9.own_turn.refs_0_, s32[1]{0:T(128)} %collective-permute-done.east_turn.refs_1_, s32[1]{0:T(128)} %collective-permute-done.1.west_turn.refs_2_, s32[1]{0:T(128)} %collective-permute-done.2.across_turn.refs_3_, ...), custom_call_target="tpu_custom_call" | custom-call | flops 150994944 | bytes 1572864 | tf_op jit(solution)/shard_map/seam_filters/pallas_call | solution.py:343
  68.2 0.4 collective-permute-start.9
  68.6 5.0 %collective-permute-done.9 = f32[9,32,128]{2,1,0:T(8,128)S(1)} collective-permute-done((f32[9,32,128]{2,1,0:T(8,128)}, f32[9,32,128]{2,1,0:T(8,128)S(1)}, u32[]{:S(2)}, u32[]{:S(2)}) %collective-permute-start.9) | collective-permute-done | bytes 147488 | tf_op jit(solution)/shard_map/ppermute | solution.py:587
  73.6 0.9 add.9
  74.6 0.1 collective-permute-start.10
  74.6 6.6 %collective-permute-done.10 = f32[9,32,128]{2,1,0:T(8,128)S(1)} collective-permute-done((f32[9,32,128]{2,1,0:T(8,128)S(1)}, f32[9,32,128]{2,1,0:T(8,128)S(1)}, u32[]{:S(2)}, u32[]{:S(2)}) %collective-permute-start.10) | collective-permute-done | bytes 147488 | tf_op jit(solution)/shard_map/ppermute | solution.py:587
  81.3 2.0 %collective-permute-start.11 = (f32[9,32,128]{2,1,0:T(8,128)S(1)}, f32[9,32,128]{2,1,0:T(8,128)S(1)}, u32[]{:S(2)}, u32[]{:S(2)}) collective-permute-start(f32[9,32,128]{2,1,0:T(8,128)S(1)} %add.10), channel_id=1, source_target_pairs={{0,16},{4,20},{8,24},{12,28},{16,0},{20,4},{24,8},{28,12},{1,17},{... | collective-permute-start | bytes 442376 | tf_op jit(solution)/shard_map/ppermute | solution.py:587
  83.3 14.7 %conv.1 = (bf16[16,16,32,128]{3,2,1,0:T(8,128)(2,1)}, bf16[16,16,32,128]{3,2,1,0:T(8,128)(2,1)}) custom-call(s32[1]{0:T(128)S(6)} %copy.9.own_turn.refs_0_, bf16[9,32,128]{2,1,0:T(8,128)(2,1)} %bitcast.23, bf16[16,16,128,128]{3,2,1,0:T(8,128)(2,1)} %get-tuple-element.11.field.source.refs_4_, ...), custom_call_target="tpu_custom_call", output_to_operand_aliasing={{1}: (6, {})} | custom-call | flops 3221225472 | bytes 12582912 | tf_op jit(solution)/shard_map/conv/pallas_call | solution.py:529
  98.0 0.0 collective-permute-done.11
  98.0 0.7 add.11
  (1 shorter events, 0.0 us)
Async XLA Ops:
  0.6 23.8 %collective-permute-start.1 = (s32[1]{0:T(128)}, s32[1]{0:T(128)}, u32[]{:S(2)}, u32[]{:S(2)}) collective-permute-start(s32[1]{0:T(128)} %param.5), channel_id=1, source_target_pairs={{0,8},{4,12},{8,16},{12,20},{16,24},{20,28},{24,0},{28,4},{1,9},{5... | collective-permute-start | bytes 20 | tf_op jit(solution)/shard_map/ppermute | solution.py:563
  3.7 22.4 %collective-permute-start = (s32[1]{0:T(128)}, s32[1]{0:T(128)}, u32[]{:S(2)}, u32[]{:S(2)}) collective-permute-start(s32[1]{0:T(128)} %param.5), channel_id=1, source_target_pairs={{0,24},{4,28},{8,0},{12,4},{16,8},{20,12},{24,16},{28,20},{1,25},{... | collective-permute-start | bytes 20 | tf_op jit(solution)/shard_map/ppermute | solution.py:563
  5.8 22.4 %collective-permute-start.5 = (bf16[9,32,128]{2,1,0:T(8,128)(2,1)}, bf16[9,32,128]{2,1,0:T(8,128)(2,1)S(1)}, u32[]{:S(2)}, u32[]{:S(2)}) collective-permute-start(bf16[9,32,128]{2,1,0:T(8,128)(2,1)} %bitcast.18), channel_id=1, source_target_pairs={{0,3},{1,2},{2,1},{3,0},{4,7},{5,6},{6,5},{7,4},{8,11},{9,10},{10,... | collective-permute-start | bytes 221192 | tf_op jit(solution)/shard_map/ppermute | solution.py:568
  6.5 21.8 %collective-permute-start.4 = (bf16[9,32,128]{2,1,0:T(8,128)(2,1)}, bf16[9,32,128]{2,1,0:T(8,128)(2,1)S(1)}, u32[]{:S(2)}, u32[]{:S(2)}) collective-permute-start(bf16[9,32,128]{2,1,0:T(8,128)(2,1)} %bitcast.19), channel_id=1, source_target_pairs={{0,2},{1,3},{2,0},{3,1},{4,6},{5,7},{6,4},{7,5},{8,10},{9,11},{10,... | collective-permute-start | bytes 221192 | tf_op jit(solution)/shard_map/ppermute | solution.py:568
  7.5 20.8 %collective-permute-start.3 = (bf16[9,32,128]{2,1,0:T(8,128)(2,1)}, bf16[9,32,128]{2,1,0:T(8,128)(2,1)S(1)}, u32[]{:S(2)}, u32[]{:S(2)}) collective-permute-start(bf16[9,32,128]{2,1,0:T(8,128)(2,1)} %bitcast.20), channel_id=1, source_target_pairs={{0,1},{1,0},{2,3},{3,2},{4,5},{5,4},{6,7},{7,6},{8,9},{9,8},{10,11... | collective-permute-start | bytes 221192 | tf_op jit(solution)/shard_map/ppermute | solution.py:568
  24.4 3.8 %collective-permute-start.2 = (s32[1]{0:T(128)}, s32[1]{0:T(128)}, u32[]{:S(2)}, u32[]{:S(2)}) collective-permute-start(s32[1]{0:T(128)} %param.5), channel_id=1, source_target_pairs={{0,4},{4,0},{8,12},{12,8},{16,20},{20,16},{24,28},{28,24},{1,5},{5... | collective-permute-start | bytes 20 | tf_op jit(solution)/shard_map/ppermute | solution.py:563
  28.2 0.6 copy-start.3
  28.3 0.6 copy-start.4
  28.3 0.7 copy-start.5
  35.1 25.7 %collective-permute-start.6 = (bf16[96,2048]{1,0:T(8,128)(2,1)}, bf16[96,2048]{1,0:T(8,128)(2,1)S(1)}, u32[]{:S(2)}, u32[]{:S(2)}) collective-permute-start(bf16[96,2048]{1,0:T(8,128)(2,1)} %get-tuple-element.13), channel_id=1, source_target_pairs={{0,24},{4,28},{8,0},{12,4},{16,8},{20,12},{24,16},{28,20},{1,25},{... | collective-permute-start | bytes 1179656 | tf_op jit(solution)/shard_map/ppermute | solution.py:575
  37.2 23.7 %collective-permute-start.7 = (bf16[96,2048]{1,0:T(8,128)(2,1)}, bf16[96,2048]{1,0:T(8,128)(2,1)S(1)}, u32[]{:S(2)}, u32[]{:S(2)}) collective-permute-start(bf16[96,2048]{1,0:T(8,128)(2,1)} %get-tuple-element.14), channel_id=1, source_target_pairs={{0,8},{4,12},{8,16},{12,20},{16,24},{20,28},{24,0},{28,4},{1,9},{5... | collective-permute-start | bytes 1179656 | tf_op jit(solution)/shard_map/ppermute | solution.py:574
  37.2 23.7 %collective-permute-start.8 = (bf16[96,2048]{1,0:T(8,128)(2,1)}, bf16[96,2048]{1,0:T(8,128)(2,1)S(1)}, u32[]{:S(2)}, u32[]{:S(2)}) collective-permute-start(bf16[96,2048]{1,0:T(8,128)(2,1)} %get-tuple-element.15), channel_id=1, source_target_pairs={{0,4},{4,0},{8,12},{12,8},{16,20},{20,16},{24,28},{28,24},{1,5},{5... | collective-permute-start | bytes 1179656 | tf_op jit(solution)/shard_map/ppermute | solution.py:576
  60.9 0.8 copy-start
  60.9 0.9 copy-start.1
  61.9 0.8 copy-start.2
  68.2 5.4 %collective-permute-start.9 = (f32[9,32,128]{2,1,0:T(8,128)}, f32[9,32,128]{2,1,0:T(8,128)S(1)}, u32[]{:S(2)}, u32[]{:S(2)}) collective-permute-start(f32[9,32,128]{2,1,0:T(8,128)} %seam_filters.1), channel_id=1, source_target_pairs={{0,4},{4,0},{8,12},{12,8},{16,20},{20,16},{24,28},{28,24},{1,5},{5... | collective-permute-start | bytes 442376 | tf_op jit(solution)/shard_map/ppermute | solution.py:587
  74.6 6.7 %collective-permute-start.10 = (f32[9,32,128]{2,1,0:T(8,128)S(1)}, f32[9,32,128]{2,1,0:T(8,128)S(1)}, u32[]{:S(2)}, u32[]{:S(2)}) collective-permute-start(f32[9,32,128]{2,1,0:T(8,128)S(1)} %add.9), channel_id=1, source_target_pairs={{0,8},{4,12},{8,0},{12,4},{16,24},{20,28},{24,16},{28,20},{1,9},{5... | collective-permute-start | bytes 442376 | tf_op jit(solution)/shard_map/ppermute | solution.py:587
  81.3 16.7 %collective-permute-start.11 = (f32[9,32,128]{2,1,0:T(8,128)S(1)}, f32[9,32,128]{2,1,0:T(8,128)S(1)}, u32[]{:S(2)}, u32[]{:S(2)}) collective-permute-start(f32[9,32,128]{2,1,0:T(8,128)S(1)} %add.10), channel_id=1, source_target_pairs={{0,16},{4,20},{8,24},{12,28},{16,0},{20,4},{24,8},{28,12},{1,17},{... | collective-permute-start | bytes 442376 | tf_op jit(solution)/shard_map/ppermute | solution.py:587

commit v3 on v0

v3 whole, which is shorter than its diff:
```python
import math

import jax
import jax.numpy as jnp
from jax import lax
from jax.experimental import pallas as pl
from jax.experimental.pallas import tpu as pltpu
from jax.sharding import PartitionSpec as P

BIG = 56 << 20
FLAT = (((1,), (0,)), ((), ()))
TURNED = (((1,), (1,)), ((), ()))


def dot(left, right, dims):
    return lax.dot_general(left, right, dims, preferred_element_type=jnp.float32)


def stored(turn, row, col, last):

    def chosen(values):
        return jnp.where(
            turn < 2,
            jnp.where(turn == 0, values[0], values[1]),
            jnp.where(turn == 2, values[2], values[3]),
        )

    return (
        chosen((row, last - col, last - row, col)),
        chosen((col, row, last - col, last - row)),
    )


def edge_place(turn, lower, edge, side):
    last = side - 1
    if edge == 0:
        start, after = (0, last), (1, last)
    elif edge == 1:
        start, after = (0, 0), (1, 0)
    else:
        row = last * (1 - lower)
        start, after = (row, 0), (row, 1)
    row, col = stored(turn, *start, last)
    below, beside = stored(turn, *after, last)
    first = row * side + col
    return first, below * side + beside - first


def edge_tap(turn, lower, edge, along, outward):
    if edge == 0:
        cell = (along, 2 if outward else 0)
    elif edge == 1:
        cell = (along, 0 if outward else 2)
    else:
        cell = (2 - 2 * lower if outward else 2 * lower, along)
    row, col = stored(turn, *cell, 2)
    return row * 3 + col


def one_hot(share, channels):
    chan = lax.axis_index("chan").astype(jnp.int32)
    rows = lax.broadcasted_iota(jnp.int32, (share, channels), 0) + chan * share
    cols = lax.broadcasted_iota(jnp.int32, (share, channels), 1)
    return jnp.where(rows == cols, 1.0, 0.0).astype(jnp.bfloat16)


def half_of_band():
    return lax.axis_index("tile").astype(jnp.int32) % 2


def later(value, width):
    empty = jnp.zeros((value.shape[0], width), value.dtype)
    return jnp.concatenate([empty, value[:, :-width]], axis=1)


def earlier(value, width):
    empty = jnp.zeros((value.shape[0], width), value.dtype)
    return jnp.concatenate([value[:, width:], empty], axis=1)


def edge_pixels(turn, lower, edge, held, side):
    first, step = edge_place(turn, lower, edge, side)
    return jnp.concatenate([held[first + pos * step] for pos in range(side)], axis=0)


def terms_of(product, share, batch):
    return (
        later(product[:share], batch)
        + product[share : 2 * share]
        + earlier(product[2 * share : 3 * share], batch)
    ).astype(jnp.bfloat16)


def gather_filters(parts, whole):
    taps, share, _ = parts[0].shape
    chan = lax.axis_index("chan").astype(jnp.int32)
    for flip, part in enumerate(parts):
        start = pl.multiple_of((chan ^ flip) * share, share)
        for tap in range(taps):
            whole[tap, pl.ds(start, share)] = part[tap]


def pair_in(source, stage, sems, pair):
    return pltpu.make_async_copy(
        source.at[:, pl.ds(2 * pair, 2)], stage.at[pair], sems.at[pair]
    )


def pair_out(held, laid, sems, pair, side):
    pixels = pl.ds(2 * pair * side, 2 * side)
    return pltpu.make_async_copy(held.at[pixels], laid.at[pixels], sems.at[pair])


def upstream_kernel(
    own_turn, weight, other1, other2, other3, upstream,
    laid, turned, east, west, across,
    stage, held, flat, whole, rowed, shuffle, in_sems, out_sems, turned_sems,
):
    pairs, batch, rows, side, channels = stage.shape
    taps, share, _ = weight.shape
    group = 256 // side
    for pair in range(pairs):
        pair_in(upstream, stage, in_sems, pair).start()
    to = lax.broadcasted_iota(jnp.int32, (256, 256), 0)
    come = lax.broadcasted_iota(jnp.int32, (256, 256), 1)
    same = (to // group == come % side) & (to % group == come // side)
    shuffle[...] = jnp.where(same, 1.0, 0.0).astype(jnp.bfloat16)
    pick = one_hot(share, channels)
    gather_filters((weight, other1, other2, other3), whole)
    for tap in range(taps):
        rowed[tap] = dot(pick, whole[tap], TURNED).astype(jnp.bfloat16)

    def turned_out(pair):
        part = pl.ds(2 * pair, 2)
        return pltpu.make_async_copy(flat.at[part], turned.at[part], turned_sems.at[pair])

    @pl.loop(0, pairs)
    def _(pair):
        pair_in(upstream, stage, in_sems, pair).wait()
        for start in range(0, batch, group):
            block = jnp.concatenate(
                [
                    stage[pair, start : start + group, row].reshape(256, channels)
                    for row in range(rows)
                ],
                axis=1,
            )
            moved = dot(shuffle[...], block, FLAT).astype(jnp.bfloat16)
            for row in range(rows):
                pixels = pl.ds((2 * pair + row) * side, side)
                held[pixels, start : start + group] = moved[
                    :, row * channels : (row + 1) * channels
                ].reshape(side, group, channels)
        pair_out(held, laid, out_sems, pair, side).start()
        for row in range(rows):
            pixels = pl.ds((2 * pair + row) * side, side)
            flat[2 * pair + row] = dot(
                pick, held[pixels].reshape(side * batch, channels), TURNED
            ).astype(jnp.bfloat16)
        turned_out(pair).start()

    lower = half_of_band()
    turn = own_turn[0]
    for edge, out in enumerate((east, west, across)):
        filters = jnp.concatenate(
            [rowed[edge_tap(turn, lower, edge, 2 - d, True)] for d in range(3)] + [pick],
            axis=0,
        )
        product = dot(filters, edge_pixels(turn, lower, edge, held, side), TURNED)
        out[0:share] = terms_of(product, share, batch)
        out[share:] = product[3 * share :].astype(jnp.bfloat16)
    for pair in range(pairs):
        pair_out(held, laid, out_sems, pair, side).wait()
        turned_out(pair).wait()


def lay_upstream(turn, weights, upstream):
    batch, side, _, channels = upstream.shape
    taps, share, _ = weights[0].shape
    smem = pl.BlockSpec(memory_space=pltpu.SMEM)
    vmem = pl.BlockSpec(memory_space=pltpu.VMEM)
    anywhere = pl.BlockSpec(memory_space=pl.ANY)
    pairs = side // 2
    laid = jax.ShapeDtypeStruct((side * side, batch, channels), jnp.bfloat16)
    turned = jax.ShapeDtypeStruct((side, share, side * batch), jnp.bfloat16)
    message = jax.ShapeDtypeStruct((2 * share, side * batch), jnp.bfloat16)
    return pl.pallas_call(
        upstream_kernel,
        in_specs=[smem] + [vmem] * len(weights) + [anywhere],
        out_specs=[anywhere] * 2 + [vmem] * 3,
        out_shape=[laid, turned] + [message] * 3,
        scratch_shapes=[
            pltpu.VMEM((pairs, batch, 2, side, channels), jnp.bfloat16),
            pltpu.VMEM(laid.shape, jnp.bfloat16),
            pltpu.VMEM(turned.shape, jnp.bfloat16),
            pltpu.VMEM((taps, channels, channels), jnp.bfloat16),
            pltpu.VMEM((taps, share, channels), jnp.bfloat16),
            pltpu.VMEM((256, 256), jnp.bfloat16),
            pltpu.SemaphoreType.DMA((pairs,)),
            pltpu.SemaphoreType.DMA((pairs,)),
            pltpu.SemaphoreType.DMA((pairs,)),
        ],
        compiler_params=pltpu.CompilerParams(vmem_limit_bytes=BIG),
        cost_estimate=pl.CostEstimate(
            flops=1024 * upstream.size, bytes_accessed=5 * upstream.size, transcendentals=0
        ),
        name="lay_upstream",
    )(turn, *weights, upstream)


def field_kernel(
    own_turn, east_turn, west_turn, across_turn, weight, field, turned,
    laid, edges, inner, east, west, across,
    stage, held, padded, total, in_sems, out_sems, turned_sem, edge_sems,
):
    pairs, batch, rows, side, channels = stage.shape
    taps, share, _ = weight.shape
    width = side * batch
    turned_in = pltpu.make_async_copy(
        turned, padded.at[pl.ds(1, side), :, pl.ds(batch, width)], turned_sem
    )
    pair_in(field, stage, in_sems, 0).start()
    turned_in.start()
    for pair in range(1, pairs):
        pair_in(field, stage, in_sems, pair).start()
    padded[0] = jnp.zeros(padded.shape[1:], padded.dtype)
    padded[side + 1] = jnp.zeros(padded.shape[1:], padded.dtype)
    column = jnp.zeros((side, share, batch), padded.dtype)
    padded[1 : side + 1, :, 0:batch] = column
    padded[1 : side + 1, :, width + batch :] = column
    total[...] = jnp.zeros_like(total)

    def lay(pair):
        pair_in(field, stage, in_sems, pair).wait()
        for row in range(rows):
            held[pl.ds((2 * pair + row) * side, side)] = jnp.swapaxes(stage[pair, :, row], 0, 1)
        pair_out(held, laid, out_sems, pair, side).start()

    def add_filters(pair):
        cols = 4
        for start in range(0, side, cols):
            parts = []
            for tap in range(3):
                at = (start + 2 - tap) * batch
                part = padded[pl.ds(2 * pair, rows + 2), :, at : at + cols * batch]
                parts.append(part.reshape((rows + 2) * share, cols * batch))
            left = jnp.concatenate(parts, axis=0)
            right = jnp.concatenate(
                [
                    held[pl.ds((2 * pair + row) * side + start, cols)].reshape(
                        cols * batch, channels
                    )
                    for row in range(rows)
                ],
                axis=1,
            )
            total[...] += dot(left, right, FLAT)

    lay(0)
    turned_in.wait()

    @pl.loop(1, pairs)
    def _(pair):
        add_filters(pair - 1)
        lay(pair)

    lower = half_of_band()
    turn = own_turn[0]
    for edge in range(3):
        first, step = edge_place(turn, lower, edge, side)
        for pos in range(side):
            pltpu.make_async_copy(
                held.at[first + pos * step], edges.at[edge, pos], edge_sems.at[edge]
            ).start()
    turns = (east_turn[0], west_turn[0], across_turn[0])
    for edge, out in enumerate((east, west, across)):
        filters = jnp.concatenate(
            [weight[edge_tap(turns[edge], lower, edge, d, False)] for d in range(3)], axis=0
        )
        product = dot(filters, edge_pixels(turn, lower, edge, held, side), TURNED)
        out[...] = terms_of(product, share, batch)
    add_filters(pairs - 1)
    for row_tap in range(3):
        for col_tap in range(3):
            value = jnp.zeros((share, channels), jnp.float32)
            for row in range(rows):
                start = col_tap * (rows + 2) * share + (row + 2 - row_tap) * share
                value += total[start : start + share, row * channels : (row + 1) * channels]
            inner[row_tap * 3 + col_tap] = value
    for pair in range(pairs):
        pair_out(held, laid, out_sems, pair, side).wait()
    for edge in range(3):
        pltpu.make_async_copy(
            held.at[pl.ds(0, side)], edges.at[edge], edge_sems.at[edge]
        ).wait()


def lay_field(turns, weight, field, turned):
    batch, side, _, channels = field.shape
    taps, share, _ = weight.shape
    smem = pl.BlockSpec(memory_space=pltpu.SMEM)
    vmem = pl.BlockSpec(memory_space=pltpu.VMEM)
    anywhere = pl.BlockSpec(memory_space=pl.ANY)
    pairs = side // 2
    laid = jax.ShapeDtypeStruct((side * side, batch, channels), jnp.bfloat16)
    edges = jax.ShapeDtypeStruct((3, side, batch, channels), jnp.bfloat16)
    inner = jax.ShapeDtypeStruct((taps, share, channels), jnp.float32)
    message = jax.ShapeDtypeStruct((share, side * batch), jnp.bfloat16)
    return pl.pallas_call(
        field_kernel,
        in_specs=[smem] * 4 + [vmem] + [anywhere] * 2,
        out_specs=[anywhere] * 2 + [vmem] * 4,
        out_shape=[laid, edges, inner] + [message] * 3,
        scratch_shapes=[
            pltpu.VMEM((pairs, batch, 2, side, channels), jnp.bfloat16),
            pltpu.VMEM(laid.shape, jnp.bfloat16),
            pltpu.VMEM((side + 2, share, (side + 2) * batch), jnp.bfloat16),
            pltpu.VMEM((12 * share, 2 * channels), jnp.float32),
            pltpu.SemaphoreType.DMA((pairs,)),
            pltpu.SemaphoreType.DMA((pairs,)),
            pltpu.SemaphoreType.DMA,
            pltpu.SemaphoreType.DMA((3,)),
        ],
        compiler_params=pltpu.CompilerParams(vmem_limit_bytes=BIG),
        cost_estimate=pl.CostEstimate(
            flops=1800 * field.size, bytes_accessed=5 * field.size, transcendentals=0
        ),
        name="lay_field",
    )(*turns, weight, field, turned)


def seam_kernel(
    scale, east_turn, west_turn, across_turn, edges, inner, east, west, across, out
):
    side, batch, channels = edges.shape[1:]
    share = out.shape[1]
    lower = half_of_band()
    turns = (east_turn[0], west_turn[0], across_turn[0])
    out[...] = inner[...]
    for edge, message in enumerate((east, west, across)):
        turned = message[share:]
        left = jnp.concatenate([earlier(turned, batch), turned, later(turned, batch)], axis=0)
        terms = dot(left, edges[edge].reshape(side * batch, channels), FLAT)
        for d in range(3):
            tap = edge_tap(turns[edge], lower, edge, d, False)
            out[tap] += terms[d * share : (d + 1) * share]
    out[...] = out[...] * scale


def seam_filters(scale, turns, edges, inner, messages):
    _, side, batch, channels = edges.shape
    share = inner.shape[1]
    smem = pl.BlockSpec(memory_space=pltpu.SMEM)
    vmem = pl.BlockSpec(memory_space=pltpu.VMEM)

    def body(*refs):
        seam_kernel(scale, *refs)

    return pl.pallas_call(
        body,
        in_specs=[smem] * 3 + [vmem] * 5,
        out_specs=vmem,
        out_shape=jax.ShapeDtypeStruct(inner.shape, jnp.float32),
        compiler_params=pltpu.CompilerParams(vmem_limit_bytes=BIG),
        cost_estimate=pl.CostEstimate(
            flops=18 * share * side * batch * channels,
            bytes_accessed=6 * side * batch * channels,
            transcendentals=0,
        ),
        name="seam_filters",
    )(*turns[1:], edges, inner, *messages)


def conv_kernel(mirrored, own_turn, east, west, across, source, *refs):
    out, padded, spread, sums, whole, sems = refs[-6:]
    weights = refs[:-6]
    side, cols, batch, channels = padded.shape
    cols -= 2
    share = weights[0].shape[1]

    def row_copy(row):
        return pltpu.make_async_copy(
            source.at[pl.ds(row * cols, cols)], padded.at[row, pl.ds(1, cols)], sems.at[row]
        )

    for row in range(side):
        row_copy(row).start()
    tile = jnp.zeros((batch, channels), padded.dtype)
    for row in range(side):
        padded[row, 0] = tile
        padded[row, cols + 1] = tile

    if mirrored:
        gather_filters(weights, whole)
        pick = one_hot(share, channels)
    empty = jnp.zeros((share, channels), spread.dtype)
    blocks = [
        dot(pick, whole[8 - tap], TURNED).astype(jnp.bfloat16) if mirrored else weights[0][tap]
        for tap in range(9)
    ]
    for row in range(3):
        for out_col in range(2):
            for in_col in range(4):
                tap = in_col - out_col
                to = (row * 2 + out_col) * share
                at = in_col * channels
                spread[to : to + share, at : at + channels] = (
                    blocks[row * 3 + tap] if 0 <= tap <= 2 else empty
                )
    sums[...] = jnp.zeros_like(sums)
    lower = half_of_band()
    for edge, message in enumerate((east, west, across)):
        first, step = edge_place(own_turn[0], lower, edge, side)
        for pos in range(side):
            sums[first + pos * step + cols] += message[
                0:share, pos * batch : (pos + 1) * batch
            ].astype(jnp.float32)

    @pl.loop(0, side, unroll=4)
    def _(row):
        row_copy(row).wait()
        for start in range(0, cols, 4):
            right = jnp.concatenate(
                [
                    jnp.concatenate(
                        [padded[row, start + half + col] for col in range(4)], axis=1
                    )
                    for half in (0, 2)
                ],
                axis=0,
            )
            terms = dot(spread[...], right, TURNED)
            for half in (0, 2):
                for col in range(2):
                    at = start + half + col
                    part = [
                        terms[
                            (k * 2 + col) * share : (k * 2 + col + 1) * share,
                            half // 2 * batch : (half // 2 + 1) * batch,
                        ]
                        for k in range(3)
                    ]
                    pixel = row * cols + at
                    sums[pixel + 2 * cols] += part[0]
                    sums[pixel + cols] += part[1]
                    done = jnp.maximum(pixel - cols, at)
                    out[done] = (sums[pixel] + part[2]).astype(out.dtype)

    for at in range(cols):
        out[(side - 1) * cols + at] = sums[side * cols + at].astype(out.dtype)


def convolved(mirrored, turn, messages, source, weights, *after):
    pixels, batch, channels = source.shape
    taps, share, _ = weights[0].shape
    side = math.isqrt(pixels)
    smem = pl.BlockSpec(memory_space=pltpu.SMEM)
    vmem = pl.BlockSpec(memory_space=pltpu.VMEM)

    def body(*refs):
        conv_kernel(mirrored, *refs)

    return pl.pallas_call(
        body,
        in_specs=[smem] + [vmem] * 3
        + [pl.BlockSpec(memory_space=pl.ANY)]
        + [vmem] * len(weights)
        + [pl.BlockSpec(memory_space=pl.ANY)] * len(after),
        out_specs=vmem,
        out_shape=jax.ShapeDtypeStruct((pixels, share, batch), jnp.bfloat16),
        scratch_shapes=[
            pltpu.VMEM((side, side + 2, batch, channels), jnp.bfloat16),
            pltpu.VMEM((6 * share, 4 * channels), jnp.bfloat16),
            pltpu.VMEM((pixels + 2 * side, share, batch), jnp.float32),
            pltpu.VMEM((taps, channels, channels), jnp.bfloat16),
            pltpu.SemaphoreType.DMA((side,)),
        ],
        compiler_params=pltpu.CompilerParams(vmem_limit_bytes=BIG),
        cost_estimate=pl.CostEstimate(
            flops=2400 * source.size, bytes_accessed=3 * source.size, transcendentals=0
        ),
        name="grad_conv" if mirrored else "conv",
    )(turn, *messages, source, *weights, *after)


def sum_over_tiles(total, count):
    bit = 1
    while bit < count:
        left = count // bit

        def other(flip):
            return lax.ppermute(total, "tile", [(i, i ^ flip) for i in range(count)])

        if left % 4 == 0 and left.bit_length() % 2 == 1:
            near, far, farther = other(bit), other(2 * bit), other(3 * bit)
            total = (total + near) + (far + farther)
            bit *= 4
        else:
            total = total + other(bit)
            bit *= 2
    return total


def per_device(tiles, orientation, weight, grad_out):
    batch, side, _, channels = tiles.shape[1:]
    share = weight.shape[3]
    count = lax.axis_size("tile")
    eastward = [(i, (i + 2) % count) for i in range(count)]
    westward = [(i, (i - 2) % count) for i in range(count)]
    acrossward = [(i, i ^ 1) for i in range(count)]

    def exchanged(sends):
        return [
            lax.ppermute(sends[1], "tile", westward),
            lax.ppermute(sends[0], "tile", eastward),
            lax.ppermute(sends[2], "tile", acrossward),
        ]

    own = weight.transpose(0, 1, 3, 2).reshape(9, share, channels)
    weights = [own] + [
        lax.ppermute(own, "chan", [(i, i ^ flip) for i in range(channels // share)])
        for flip in range(1, channels // share)
    ]
    turns = [orientation] + [
        lax.ppermute(orientation, "tile", pairs)
        for pairs in (westward, eastward, acrossward)
    ]
    upstream, turned, *sends = lay_upstream(orientation, weights, grad_out[0])
    grad_messages = exchanged(sends)
    field, edges, inner, *sends = lay_field(turns, own, tiles[0], turned)
    conv_messages = exchanged(sends)
    scale = 1.0 / math.sqrt(count * batch * side * side)
    total = seam_filters(scale, turns, edges, inner, grad_messages)
    grad = convolved(True, orientation, grad_messages, upstream, weights)
    conv = convolved(False, orientation, conv_messages, field, weights[:1], grad)
    total = sum_over_tiles(total, count)
    shape = (side, side, share, batch)
    conv_out = conv.reshape(shape).transpose(3, 0, 1, 2)[None]
    grad_input = grad.reshape(shape).transpose(3, 0, 1, 2)[None]
    grad_weight = total.reshape(3, 3, share, channels).transpose(0, 1, 3, 2)
    return conv_out, grad_input, grad_weight


def solution(mesh):
    in_specs = (
        P("tile", None, None, None, None),
        P("tile"),
        P(None, None, None, "chan"),
        P("tile", None, None, None, None),
    )
    out_specs = (
        P("tile", None, None, None, "chan"),
        P("tile", None, None, None, "chan"),
        P(None, None, None, "chan"),
    )
    return jax.shard_map(
        per_device, mesh=mesh, in_specs=in_specs, out_specs=out_specs, check_vma=False
    )
```

time: 460 us -> 82.2 us (0.18); the launches traced: 453 us -> 81.9 us
  waiting for transfers between devices: 124 us -> 0.04 us
  starting transfers between devices: 106 us -> 22.8 us
  matrix products: 83.1 us -> 0 us
  local copies, waits for them, and re-layouts: 81.4 us -> 2.08 us
  Pallas kernels: 0 us -> 54.8 us
  other arithmetic: 33.5 us -> 0.73 us
  between operations: 17.8 us -> 1.48 us
  blocking collectives: 6.12 us -> 0 us
    ppermute x12 -> x16, starting transfers between devices: 106 us -> 22.8 us  [the longest x4 5.96 us: other(): return lax.ppermute(total, 'tile', [(i, i ^ flip) for i in range(count)])]
    ppermute x12 -> x16, waiting for transfers between devices: 81.3 us -> 0.04 us  [the longest x4 0.01 us: other(): return lax.ppermute(total, 'tile', [(i, i ^ flip) for i in range(count)])]
    conv_general_dilated x2 -> x0, matrix products: 62.6 us -> none  [the longest x1 36.5 us: per_device(): lax.conv_general_dilated(upstream, flipped, (1, 1), ((2, 2), (2, 2)), dim...]
    pallas_call x0 -> x5, Pallas kernels: none -> 54.8 us  [the longest x2 24 us: convolved(): pl.pallas_call(body, in_specs=[smem] + [vmem] * 3 + [pl.BlockSpec(memory_...]
    psum x1 -> x0, waiting for transfers between devices: 42.3 us -> none  [per_device(): grad_weight = lax.psum(local_grad, 'tile') * normalizer]
    dot_general x9 -> x0, matrix products: 20.5 us -> none  [per_device(): jnp.einsum('bhwc,bhwo->co', window, upstream_cols, preferred_element_type...]
    dynamic_slice x2 -> x0, local copies, waits for them, and re-layouts: 19.5 us -> none  [per_device(): lax.dynamic_slice_in_dim(upstream, chan_index * share, share, 3)]
    unnamed x24 -> x20, local copies, waits for them, and re-layouts: 17 us -> 2.08 us
  transfers between devices with their start and end apart: 13 -> 16, of which waited for: 7 -> 0; matrix products, arithmetic and copies ran while one was open for 28% -> 0% of each run, Pallas kernels for 0% -> 67%
where the time goes in v3:
time: 82.2 us; the launch traced here: 81.9 us
  Pallas kernels  54.8 us (67%)
  starting transfers between devices  22.8 us (28%)
  local copies, waits for them, and re-layouts  2.08 us (3%)
  between operations  1.48 us (2%)
    pallas_call x2, Pallas kernels, convolved(): pl.pallas_call(body, in_specs=[smem] + [vmem] * 3 + [pl.BlockSpec(memory_...  24 us
    pallas_call x1, Pallas kernels, lay_field(): pl.pallas_call(field_kernel, in_specs=[smem] * 4 + [vmem] + [anywhere] *...  15.6 us
    pallas_call x1, Pallas kernels, lay_upstream(): pl.pallas_call(upstream_kernel, in_specs=[smem] + [vmem] * len(weights) +...  10.5 us
    ppermute x4, starting transfers between devices, other(): return lax.ppermute(total, 'tile', [(i, i ^ flip) for i in range(count)])  5.96 us
    ppermute x2, starting transfers between devices, exchanged(): lax.ppermute(sends[1], 'tile', westward)  5.93 us
    ppermute x3, starting transfers between devices, per_device(): lax.ppermute(orientation, 'tile', pairs)  5.6 us
    pallas_call x1, Pallas kernels, seam_filters(): pl.pallas_call(body, in_specs=[smem] * 3 + [vmem] * 5, out_specs=vmem, ou...  4.71 us
    ppermute x3, starting transfers between devices, per_device(): lax.ppermute(own, 'chan', [(i, i ^ flip) for i in range(channels // share)])  3.15 us
  transfers between devices with their start and end apart: 16, of which 0 were waited for; matrix products, arithmetic and copies ran while one was open for 0% of the time, Pallas kernels for 67%

profile of v3, /device:TPU:0, one launch (start us, length us, event | category | flops | bytes accessed | tf_op | source)
XLA Modules:
  0.0 81.9 jit_solution(10690988088789308516)
XLA Ops:
  0.6 2.5 %collective-permute-start.5 = (bf16[9,32,128]{2,1,0:T(8,128)(2,1)}, bf16[9,32,128]{2,1,0:T(8,128)(2,1)S(1)}, u32[]{:S(2)}, u32[]{:S(2)}) collective-permute-start(bf16[9,32,128]{2,1,0:T(8,128)(2,1)} %bitcast.21), channel_id=1, source_target_pairs={{0,3},{1,2},{2,1},{3,0},{4,7},{5,6},{6,5},{7,4},{8,11},{9,10},{10,... | collective-permute-start | bytes 221192 | tf_op jit(solution)/shard_map/ppermute | solution.py:521
  3.1 0.6 collective-permute-start.4
  3.7 0.0 collective-permute-start.3
  3.8 1.8 %collective-permute-start.1 = (s32[1]{0:T(128)}, s32[1]{0:T(128)}, u32[]{:S(2)}, u32[]{:S(2)}) collective-permute-start(s32[1]{0:T(128)} %param.5), channel_id=1, source_target_pairs={{0,8},{4,12},{8,16},{12,20},{16,24},{20,28},{24,0},{28,4},{1,9},{5... | collective-permute-start | bytes 20 | tf_op jit(solution)/shard_map/ppermute | solution.py:525
  5.6 2.0 %collective-permute-start = (s32[1]{0:T(128)}, s32[1]{0:T(128)}, u32[]{:S(2)}, u32[]{:S(2)}) collective-permute-start(s32[1]{0:T(128)} %param.5), channel_id=1, source_target_pairs={{0,24},{4,28},{8,0},{12,4},{16,8},{20,12},{24,16},{28,20},{1,25},{... | collective-permute-start | bytes 20 | tf_op jit(solution)/shard_map/ppermute | solution.py:525
  8.3 0.0 collective-permute-done.5.other3.refs_8_
  8.3 0.0 copy-start.7
  8.3 1.8 %collective-permute-start.2 = (s32[1]{0:T(128)}, s32[1]{0:T(128)}, u32[]{:S(2)}, u32[]{:S(2)}) collective-permute-start(s32[1]{0:T(128)} %param.5), channel_id=1, source_target_pairs={{0,4},{4,0},{8,12},{12,8},{16,20},{20,16},{24,28},{28,24},{1,5},{5... | collective-permute-start | bytes 20 | tf_op jit(solution)/shard_map/ppermute | solution.py:525
  10.1 0.0 collective-permute-done.4.other2.refs_7_
  10.1 0.0 collective-permute-done.3.other1.refs_6_
  10.1 0.6 copy-done.8
  10.7 0.0 copy-done.9
  10.8 10.5 %lay_upstream.1 = (bf16[256,128,128]{2,1,0:T(8,128)(2,1)}, bf16[16,32,2048]{2,1,0:T(8,128)(2,1)}, bf16[64,2048]{1,0:T(8,128)(2,1)}, bf16[64,2048]{1,0:T(8,128)(2,1)}, bf16[64,2048]{1,0:T(8,128)(2,1)}) custom-call(s32[1]{0:T(128)S(6)} %copy.7.own_turn.refs_0_, bf16[9,32,128]{2,1,0:T(8,128)(2,1)} %bitcast.24, bf16[9,32,128]{2,1,0:T(8,128)(2,1)} %copy-done.9, ...), custom_call_target="tpu_custom_call" | custom-call | flops 4294967296 | bytes 20971520 | tf_op jit(solution)/shard_map/lay_upstream/pallas_call | solution.py:187
  21.2 2.1 %collective-permute-start.9 = (bf16[64,2048]{1,0:T(8,128)(2,1)}, bf16[64,2048]{1,0:T(8,128)(2,1)S(1)}, u32[]{:S(2)}, u32[]{:S(2)}) collective-permute-start(bf16[64,2048]{1,0:T(8,128)(2,1)} %get-tuple-element.19), channel_id=1, source_target_pairs={{0,24},{4,28},{8,0},{12,4},{16,8},{20,12},{24,16},{28,20},{1,25},{... | collective-permute-start | bytes 786440 | tf_op jit(solution)/shard_map/ppermute | solution.py:514
  23.3 0.0 collective-permute-start.10
  23.3 0.0 collective-permute-done.1.west_turn.refs_1_
  23.3 1.5 %collective-permute-start.11 = (bf16[64,2048]{1,0:T(8,128)(2,1)}, bf16[64,2048]{1,0:T(8,128)(2,1)S(1)}, u32[]{:S(2)}, u32[]{:S(2)}) collective-permute-start(bf16[64,2048]{1,0:T(8,128)(2,1)} %get-tuple-element.21), channel_id=1, source_target_pairs={{0,4},{4,0},{8,12},{12,8},{16,20},{20,16},{24,28},{28,24},{1,5},{5... | collective-permute-start | bytes 786440 | tf_op jit(solution)/shard_map/ppermute | solution.py:516
  24.8 0.0 collective-permute-done.east_turn.refs_0_
  24.8 0.0 collective-permute-done.2.across_turn.refs_2_
  24.8 15.6 %lay_field.1 = (bf16[256,128,128]{2,1,0:T(8,128)(2,1)}, bf16[3,16,128,128]{3,2,1,0:T(8,128)(2,1)}, f32[9,32,128]{2,1,0:T(8,128)}, bf16[32,2048]{1,0:T(8,128)(2,1...) custom-call(s32[1]{0:T(128)S(6)} %copy.7.own_turn.refs_0_, s32[1]{0:T(128)} %collective-permute-done.east_turn.refs_0_, ...), custom_call_target="tpu_custom_call" | custom-call | flops 7549747200 | bytes 20971520 | tf_op jit(solution)/shard_map/lay_field/pallas_call | solution.py:309
  40.4 3.9 %collective-permute-start.6 = (bf16[32,2048]{1,0:T(8,128)(2,1)}, bf16[32,2048]{1,0:T(8,128)(2,1)S(1)}, u32[]{:S(2)}, u32[]{:S(2)}) collective-permute-start(bf16[32,2048]{1,0:T(8,128)(2,1)} %get-tuple-element.15), channel_id=1, source_target_pairs={{0,24},{4,28},{8,0},{12,4},{16,8},{20,12},{24,16},{28,20},{1,25},{... | collective-permute-start | bytes 393224 | tf_op jit(solution)/shard_map/ppermute | solution.py:514
  44.3 0.0 collective-permute-start.7
  44.3 0.0 collective-permute-done.9.refs_1_.refs_5_
  44.3 0.6 collective-permute-start.8
  44.9 0.0 collective-permute-done.10.refs_2_.refs_6_
  44.9 0.0 collective-permute-done.11.refs_3_.refs_7_
  44.9 0.0 copy-start.3
  44.9 0.1 copy-done.1
  45.0 0.6 copy-done.2
  45.6 0.1 copy-done.3
  45.7 4.7 %seam_filters.1 = f32[9,32,128]{2,1,0:T(8,128)} custom-call(s32[1]{0:T(128)} %collective-permute-done.east_turn.refs_0_, s32[1]{0:T(128)} %collective-permute-done.1.west_turn.refs_1_, s32[1]{0:T(128)} %collective-permute-done.2.across_turn.refs_2_, bf16[3,16,128,128]{3,2,1,0:T(8,128)(2,1)} %get-tuple-element.23.refs_3_, ...), custom_call_target="tpu_custom_call" | custom-call | flops 150994944 | bytes 1572864 | tf_op jit(solution)/shard_map/seam_filters/pallas_call | solution.py:359
  50.4 1.5 %collective-permute-start.12 = (f32[9,32,128]{2,1,0:T(8,128)}, f32[9,32,128]{2,1,0:T(8,128)S(1)}, u32[]{:S(2)}, u32[]{:S(2)}) collective-permute-start(f32[9,32,128]{2,1,0:T(8,128)} %seam_filters.1), channel_id=1, source_target_pairs={{0,4},{4,0},{8,12},{12,8},{16,20},{20,16},{24,28},{28,24},{1,5},{5... | collective-permute-start | bytes 442376 | tf_op jit(solution)/shard_map/ppermute | solution.py:492
  51.9 12.3 %grad_conv.1.refs_6_ = bf16[256,32,128]{2,1,0:T(8,128)(2,1)} custom-call(s32[1]{0:T(128)S(6)} %copy.7.own_turn.refs_0_, bf16[64,2048]{1,0:T(8,128)(2,1)} %copy-done.1, bf16[64,2048]{1,0:T(8,128)(2,1)} %copy-done.2, bf16[64,2048]{1,0:T(8,128)(2,1)} %copy-done.3, bf16[256,128,128]{2,1,0:T(8,128)(2,1)} %get-tuple-element.22.refs_4_, ...), custom_call_target="tpu_custom_call" | custom-call | flops 10066329600 | bytes 12582912 | tf_op jit(solution)/shard_map/grad_conv/pallas_call | solution.py:463
  64.2 0.0 collective-permute-done.12
  64.3 0.0 copy-done
  64.3 3.8 %collective-permute-start.15 = (f32[9,32,128]{2,1,0:T(8,128)S(1)}, f32[9,32,128]{2,1,0:T(8,128)S(1)}, u32[]{:S(2)}, u32[]{:S(2)}) collective-permute-start(f32[9,32,128]{2,1,0:T(8,128)S(1)} %add.12), channel_id=1, source_target_pairs={{0,24},{4,28},{8,16},{12,20},{16,8},{20,12},{24,0},{28,4},{1,25},{... | collective-permute-start | bytes 442376 | tf_op jit(solution)/shard_map/ppermute | solution.py:492
  68.1 0.0 collective-permute-start.14
  68.1 0.0 collective-permute-done.6.refs_1_
  68.1 0.6 collective-permute-start.13
  68.8 0.0 collective-permute-done.7.refs_2_
  68.8 0.0 collective-permute-done.8.refs_3_
  68.8 0.6 copy-done.5
  69.4 0.0 copy-done.6
  69.5 11.7 %conv.1 = bf16[256,32,128]{2,1,0:T(8,128)(2,1)} custom-call(s32[1]{0:T(128)S(6)} %copy.7.own_turn.refs_0_, bf16[32,2048]{1,0:T(8,128)(2,1)} %copy-done.4, bf16[32,2048]{1,0:T(8,128)(2,1)} %copy-done.5, bf16[32,2048]{1,0:T(8,128)(2,1)} %copy-done.6, bf16[256,128,128]{2,1,0:T(8,128)(2,1)} %get-tuple-element.18.refs_4_, bf16[9,32,128]{2,1,0:T(8,128)(2,1)} %bitcast.27, ...), custom_call_target="tpu_custom_call" | custom-call | flops 10066329600 | bytes 12582912 | tf_op jit(solution)/shard_map/conv/pallas_call | solution.py:463
  81.1 0.0 collective-permute-done.15
  81.2 0.0 collective-permute-done.14
  81.2 0.0 collective-permute-done.13
  81.2 0.7 add_add_fusion
  (11 shorter events, 0.0 us)
Async XLA Ops:
  0.6 7.7 %collective-permute-start.5 = (bf16[9,32,128]{2,1,0:T(8,128)(2,1)}, bf16[9,32,128]{2,1,0:T(8,128)(2,1)S(1)}, u32[]{:S(2)}, u32[]{:S(2)}) collective-permute-start(bf16[9,32,128]{2,1,0:T(8,128)(2,1)} %bitcast.21), channel_id=1, source_target_pairs={{0,3},{1,2},{2,1},{3,0},{4,7},{5,6},{6,5},{7,4},{8,11},{9,10},{10,... | collective-permute-start | bytes 221192 | tf_op jit(solution)/shard_map/ppermute | solution.py:521
  3.1 7.0 %collective-permute-start.4 = (bf16[9,32,128]{2,1,0:T(8,128)(2,1)}, bf16[9,32,128]{2,1,0:T(8,128)(2,1)S(1)}, u32[]{:S(2)}, u32[]{:S(2)}) collective-permute-start(bf16[9,32,128]{2,1,0:T(8,128)(2,1)} %bitcast.22), channel_id=1, source_target_pairs={{0,2},{1,3},{2,0},{3,1},{4,6},{5,7},{6,4},{7,5},{8,10},{9,11},{10,... | collective-permute-start | bytes 221192 | tf_op jit(solution)/shard_map/ppermute | solution.py:521
  3.7 6.4 %collective-permute-start.3 = (bf16[9,32,128]{2,1,0:T(8,128)(2,1)}, bf16[9,32,128]{2,1,0:T(8,128)(2,1)S(1)}, u32[]{:S(2)}, u32[]{:S(2)}) collective-permute-start(bf16[9,32,128]{2,1,0:T(8,128)(2,1)} %bitcast.23), channel_id=1, source_target_pairs={{0,1},{1,0},{2,3},{3,2},{4,5},{5,4},{6,7},{7,6},{8,9},{9,8},{10,11... | collective-permute-start | bytes 221192 | tf_op jit(solution)/shard_map/ppermute | solution.py:521
  3.8 19.5 %collective-permute-start.1 = (s32[1]{0:T(128)}, s32[1]{0:T(128)}, u32[]{:S(2)}, u32[]{:S(2)}) collective-permute-start(s32[1]{0:T(128)} %param.5), channel_id=1, source_target_pairs={{0,8},{4,12},{8,16},{12,20},{16,24},{20,28},{24,0},{28,4},{1,9},{5... | collective-permute-start | bytes 20 | tf_op jit(solution)/shard_map/ppermute | solution.py:525
  5.6 19.2 %collective-permute-start = (s32[1]{0:T(128)}, s32[1]{0:T(128)}, u32[]{:S(2)}, u32[]{:S(2)}) collective-permute-start(s32[1]{0:T(128)} %param.5), channel_id=1, source_target_pairs={{0,24},{4,28},{8,0},{12,4},{16,8},{20,12},{24,16},{28,20},{1,25},{... | collective-permute-start | bytes 20 | tf_op jit(solution)/shard_map/ppermute | solution.py:525
  8.3 1.8 %copy-start.7 = (bf16[9,32,128]{2,1,0:T(8,128)(2,1)}, bf16[9,32,128]{2,1,0:T(8,128)(2,1)S(1)}, u32[]{:S(2)}) copy-start(bf16[9,32,128]{2,1,0:T(8,128)(2,1)S(1)} %collective-permute-done.5.other3.refs_8_) | copy-start | bytes 221188
  8.3 16.5 %collective-permute-start.2 = (s32[1]{0:T(128)}, s32[1]{0:T(128)}, u32[]{:S(2)}, u32[]{:S(2)}) collective-permute-start(s32[1]{0:T(128)} %param.5), channel_id=1, source_target_pairs={{0,4},{4,0},{8,12},{12,8},{16,20},{20,16},{24,28},{28,24},{1,5},{5... | collective-permute-start | bytes 20 | tf_op jit(solution)/shard_map/ppermute | solution.py:525
  10.1 0.6 copy-start.8
  10.1 0.6 copy-start.9
  21.2 23.1 %collective-permute-start.9 = (bf16[64,2048]{1,0:T(8,128)(2,1)}, bf16[64,2048]{1,0:T(8,128)(2,1)S(1)}, u32[]{:S(2)}, u32[]{:S(2)}) collective-permute-start(bf16[64,2048]{1,0:T(8,128)(2,1)} %get-tuple-element.19), channel_id=1, source_target_pairs={{0,24},{4,28},{8,0},{12,4},{16,8},{20,12},{24,16},{28,20},{1,25},{... | collective-permute-start | bytes 786440 | tf_op jit(solution)/shard_map/ppermute | solution.py:514
  23.3 21.6 %collective-permute-start.10 = (bf16[64,2048]{1,0:T(8,128)(2,1)}, bf16[64,2048]{1,0:T(8,128)(2,1)S(1)}, u32[]{:S(2)}, u32[]{:S(2)}) collective-permute-start(bf16[64,2048]{1,0:T(8,128)(2,1)} %get-tuple-element.20), channel_id=1, source_target_pairs={{0,8},{4,12},{8,16},{12,20},{16,24},{20,28},{24,0},{28,4},{1,9},{5... | collective-permute-start | bytes 786440 | tf_op jit(solution)/shard_map/ppermute | solution.py:515
  23.3 21.6 %collective-permute-start.11 = (bf16[64,2048]{1,0:T(8,128)(2,1)}, bf16[64,2048]{1,0:T(8,128)(2,1)S(1)}, u32[]{:S(2)}, u32[]{:S(2)}) collective-permute-start(bf16[64,2048]{1,0:T(8,128)(2,1)} %get-tuple-element.21), channel_id=1, source_target_pairs={{0,4},{4,0},{8,12},{12,8},{16,20},{20,16},{24,28},{28,24},{1,5},{5... | collective-permute-start | bytes 786440 | tf_op jit(solution)/shard_map/ppermute | solution.py:516
  40.4 27.7 %collective-permute-start.6 = (bf16[32,2048]{1,0:T(8,128)(2,1)}, bf16[32,2048]{1,0:T(8,128)(2,1)S(1)}, u32[]{:S(2)}, u32[]{:S(2)}) collective-permute-start(bf16[32,2048]{1,0:T(8,128)(2,1)} %get-tuple-element.15), channel_id=1, source_target_pairs={{0,24},{4,28},{8,0},{12,4},{16,8},{20,12},{24,16},{28,20},{1,25},{... | collective-permute-start | bytes 393224 | tf_op jit(solution)/shard_map/ppermute | solution.py:514
  44.3 24.5 %collective-permute-start.7 = (bf16[32,2048]{1,0:T(8,128)(2,1)}, bf16[32,2048]{1,0:T(8,128)(2,1)S(1)}, u32[]{:S(2)}, u32[]{:S(2)}) collective-permute-start(bf16[32,2048]{1,0:T(8,128)(2,1)} %get-tuple-element.16), channel_id=1, source_target_pairs={{0,8},{4,12},{8,16},{12,20},{16,24},{20,28},{24,0},{28,4},{1,9},{5... | collective-permute-start | bytes 393224 | tf_op jit(solution)/shard_map/ppermute | solution.py:515
  44.3 0.7 copy-start.1
  44.3 24.5 %collective-permute-start.8 = (bf16[32,2048]{1,0:T(8,128)(2,1)}, bf16[32,2048]{1,0:T(8,128)(2,1)S(1)}, u32[]{:S(2)}, u32[]{:S(2)}) collective-permute-start(bf16[32,2048]{1,0:T(8,128)(2,1)} %get-tuple-element.17), channel_id=1, source_target_pairs={{0,4},{4,0},{8,12},{12,8},{16,20},{20,16},{24,28},{28,24},{1,5},{5... | collective-permute-start | bytes 393224 | tf_op jit(solution)/shard_map/ppermute | solution.py:516
  44.9 0.7 copy-start.2
  44.9 0.8 copy-start.3
  50.4 13.8 %collective-permute-start.12 = (f32[9,32,128]{2,1,0:T(8,128)}, f32[9,32,128]{2,1,0:T(8,128)S(1)}, u32[]{:S(2)}, u32[]{:S(2)}) collective-permute-start(f32[9,32,128]{2,1,0:T(8,128)} %seam_filters.1), channel_id=1, source_target_pairs={{0,4},{4,0},{8,12},{12,8},{16,20},{20,16},{24,28},{28,24},{1,5},{5... | collective-permute-start | bytes 442376 | tf_op jit(solution)/shard_map/ppermute | solution.py:492
  51.9 12.4 %copy-start = (f32[9,32,128]{2,1,0:T(8,128)S(1)}, f32[9,32,128]{2,1,0:T(8,128)}, u32[]{:S(2)}) copy-start(f32[9,32,128]{2,1,0:T(8,128)} %seam_filters.1) | copy-start | bytes 442372
  64.3 16.8 %collective-permute-start.15 = (f32[9,32,128]{2,1,0:T(8,128)S(1)}, f32[9,32,128]{2,1,0:T(8,128)S(1)}, u32[]{:S(2)}, u32[]{:S(2)}) collective-permute-start(f32[9,32,128]{2,1,0:T(8,128)S(1)} %add.12), channel_id=1, source_target_pairs={{0,24},{4,28},{8,16},{12,20},{16,8},{20,12},{24,0},{28,4},{1,25},{... | collective-permute-start | bytes 442376 | tf_op jit(solution)/shard_map/ppermute | solution.py:492
  68.1 13.0 %collective-permute-start.14 = (f32[9,32,128]{2,1,0:T(8,128)S(1)}, f32[9,32,128]{2,1,0:T(8,128)S(1)}, u32[]{:S(2)}, u32[]{:S(2)}) collective-permute-start(f32[9,32,128]{2,1,0:T(8,128)S(1)} %add.12), channel_id=1, source_target_pairs={{0,16},{4,20},{8,24},{12,28},{16,0},{20,4},{24,8},{28,12},{1,17},{... | collective-permute-start | bytes 442376 | tf_op jit(solution)/shard_map/ppermute | solution.py:492
  68.1 0.7 copy-start.4
  68.1 13.0 %collective-permute-start.13 = (f32[9,32,128]{2,1,0:T(8,128)S(1)}, f32[9,32,128]{2,1,0:T(8,128)S(1)}, u32[]{:S(2)}, u32[]{:S(2)}) collective-permute-start(f32[9,32,128]{2,1,0:T(8,128)S(1)} %add.12), channel_id=1, source_target_pairs={{0,8},{4,12},{8,0},{12,4},{16,24},{20,28},{24,16},{28,20},{1,9},{5... | collective-permute-start | bytes 442376 | tf_op jit(solution)/shard_map/ppermute | solution.py:492
  68.8 0.7 copy-start.5
  68.8 0.7 copy-start.6

commit v4 on v3

--- a/solution.py
+++ b/solution.py
@@ -8,6 +8,8 @@
 from jax.sharding import PartitionSpec as P
 
 BIG = 56 << 20
+AHEAD = 2
+EXTRA = 128
 FLAT = (((1,), (0,)), ((), ()))
 TURNED = (((1,), (1,)), ((), ()))
 
@@ -119,7 +121,7 @@
     pairs, batch, rows, side, channels = stage.shape
     taps, share, _ = weight.shape
     group = 256 // side
-    for pair in range(pairs):
+    for pair in range(AHEAD):
         pair_in(upstream, stage, in_sems, pair).start()
     to = lax.broadcasted_iota(jnp.int32, (256, 256), 0)
     come = lax.broadcasted_iota(jnp.int32, (256, 256), 1)
@@ -136,6 +138,10 @@
 
     @pl.loop(0, pairs)
     def _(pair):
+        @pl.when(pair + AHEAD < pairs)
+        def _():
+            pair_in(upstream, stage, in_sems, pair + AHEAD).start()
+
         pair_in(upstream, stage, in_sems, pair).wait()
         for start in range(0, batch, group):
             block = jnp.concatenate(
@@ -167,8 +173,10 @@
             axis=0,
         )
         product = dot(filters, edge_pixels(turn, lower, edge, held, side), TURNED)
-        out[0:share] = terms_of(product, share, batch)
-        out[share:] = product[3 * share :].astype(jnp.bfloat16)
+        out[0:share, 0 : side * batch] = terms_of(product, share, batch)
+        out[share:, 0 : side * batch] = product[3 * share :].astype(jnp.bfloat16)
+        code = jnp.full((2 * share, EXTRA), turn, jnp.int32)
+        out[:, side * batch :] = code.astype(jnp.float32).astype(jnp.bfloat16)
     for pair in range(pairs):
         pair_out(held, laid, out_sems, pair, side).wait()
         turned_out(pair).wait()
@@ -183,7 +191,7 @@
     pairs = side // 2
     laid = jax.ShapeDtypeStruct((side * side, batch, channels), jnp.bfloat16)
     turned = jax.ShapeDtypeStruct((side, share, side * batch), jnp.bfloat16)
-    message = jax.ShapeDtypeStruct((2 * share, side * batch), jnp.bfloat16)
+    message = jax.ShapeDtypeStruct((2 * share, side * batch + EXTRA), jnp.bfloat16)
     return pl.pallas_call(
         upstream_kernel,
         in_specs=[smem] + [vmem] * len(weights) + [anywhere],
@@ -209,19 +217,18 @@
 
 
 def field_kernel(
-    own_turn, east_turn, west_turn, across_turn, weight, field, turned,
-    laid, edges, inner, east, west, across,
+    own_turn, field, turned, laid, edges, inner,
     stage, held, padded, total, in_sems, out_sems, turned_sem, edge_sems,
 ):
     pairs, batch, rows, side, channels = stage.shape
-    taps, share, _ = weight.shape
+    share = padded.shape[1]
     width = side * batch
     turned_in = pltpu.make_async_copy(
         turned, padded.at[pl.ds(1, side), :, pl.ds(batch, width)], turned_sem
     )
     pair_in(field, stage, in_sems, 0).start()
     turned_in.start()
-    for pair in range(1, pairs):
+    for pair in range(1, AHEAD):
         pair_in(field, stage, in_sems, pair).start()
     padded[0] = jnp.zeros(padded.shape[1:], padded.dtype)
     padded[side + 1] = jnp.zeros(padded.shape[1:], padded.dtype)
@@ -237,14 +244,8 @@
         pair_out(held, laid, out_sems, pair, side).start()
 
     def add_filters(pair):
-        cols = 4
+        cols = 8
         for start in range(0, side, cols):
-            parts = []
-            for tap in range(3):
-                at = (start + 2 - tap) * batch
-                part = padded[pl.ds(2 * pair, rows + 2), :, at : at + cols * batch]
-                parts.append(part.reshape((rows + 2) * share, cols * batch))
-            left = jnp.concatenate(parts, axis=0)
             right = jnp.concatenate(
                 [
                     held[pl.ds((2 * pair + row) * side + start, cols)].reshape(
@@ -254,13 +255,25 @@
                 ],
                 axis=1,
             )
-            total[...] += dot(left, right, FLAT)
+            parts = []
+            for tap in range(3):
+                at = (start + 2 - tap) * batch
+                for half in range(2):
+                    part = padded[pl.ds(2 * pair + 2 * half, 2), :, at : at + cols * batch]
+                    parts.append(part.reshape(2 * share, cols * batch))
+            for half in range(2):
+                left = jnp.concatenate(parts[3 * half : 3 * half + 3], axis=0)
+                total[6 * share * half : 6 * share * (half + 1)] += dot(left, right, FLAT)
 
     lay(0)
     turned_in.wait()
 
     @pl.loop(1, pairs)
     def _(pair):
+        @pl.when(pair + AHEAD - 1 < pairs)
+        def _():
+            pair_in(field, stage, in_sems, pair + AHEAD - 1).start()
+
         add_filters(pair - 1)
         lay(pair)
 
@@ -272,13 +285,6 @@
             pltpu.make_async_copy(
                 held.at[first + pos * step], edges.at[edge, pos], edge_sems.at[edge]
             ).start()
-    turns = (east_turn[0], west_turn[0], across_turn[0])
-    for edge, out in enumerate((east, west, across)):
-        filters = jnp.concatenate(
-            [weight[edge_tap(turns[edge], lower, edge, d, False)] for d in range(3)], axis=0
-        )
-        product = dot(filters, edge_pixels(turn, lower, edge, held, side), TURNED)
-        out[...] = terms_of(product, share, batch)
     add_filters(pairs - 1)
     for row_tap in range(3):
         for col_tap in range(3):
@@ -295,22 +301,19 @@
         ).wait()
 
 
-def lay_field(turns, weight, field, turned):
+def lay_field(turn, field, turned):
     batch, side, _, channels = field.shape
-    taps, share, _ = weight.shape
-    smem = pl.BlockSpec(memory_space=pltpu.SMEM)
-    vmem = pl.BlockSpec(memory_space=pltpu.VMEM)
+    share = turned.shape[1]
     anywhere = pl.BlockSpec(memory_space=pl.ANY)
     pairs = side // 2
     laid = jax.ShapeDtypeStruct((side * side, batch, channels), jnp.bfloat16)
     edges = jax.ShapeDtypeStruct((3, side, batch, channels), jnp.bfloat16)
-    inner = jax.ShapeDtypeStruct((taps, share, channels), jnp.float32)
-    message = jax.ShapeDtypeStruct((share, side * batch), jnp.bfloat16)
+    inner = jax.ShapeDtypeStruct((9, share, channels), jnp.float32)
     return pl.pallas_call(
         field_kernel,
-        in_specs=[smem] * 4 + [vmem] + [anywhere] * 2,
-        out_specs=[anywhere] * 2 + [vmem] * 4,
-        out_shape=[laid, edges, inner] + [message] * 3,
+        in_specs=[pl.BlockSpec(memory_space=pltpu.SMEM)] + [anywhere] * 2,
+        out_specs=[anywhere] * 2 + [pl.BlockSpec(memory_space=pltpu.VMEM)],
+        out_shape=[laid, edges, inner],
         scratch_shapes=[
             pltpu.VMEM((pairs, batch, 2, side, channels), jnp.bfloat16),
             pltpu.VMEM(laid.shape, jnp.bfloat16),
@@ -326,31 +329,33 @@
             flops=1800 * field.size, bytes_accessed=5 * field.size, transcendentals=0
         ),
         name="lay_field",
-    )(*turns, weight, field, turned)
-
-
-def seam_kernel(
-    scale, east_turn, west_turn, across_turn, edges, inner, east, west, across, out
-):
+    )(turn, field, turned)
+
+
+def seam_kernel(scale, edges, inner, weight, *refs):
+    messages, out, terms_out = refs[:3], refs[3], refs[4:7]
     side, batch, channels = edges.shape[1:]
     share = out.shape[1]
+    width = side * batch
     lower = half_of_band()
-    turns = (east_turn[0], west_turn[0], across_turn[0])
     out[...] = inner[...]
-    for edge, message in enumerate((east, west, across)):
-        turned = message[share:]
+    for edge, message in enumerate(messages):
+        turn = jnp.max(message[0:16, width:].astype(jnp.float32)).astype(jnp.int32)
+        taps = [edge_tap(turn, lower, edge, d, False) for d in range(3)]
+        turned = message[share:, 0:width]
         left = jnp.concatenate([earlier(turned, batch), turned, later(turned, batch)], axis=0)
-        terms = dot(left, edges[edge].reshape(side * batch, channels), FLAT)
+        pixels = edges[edge].reshape(width, channels)
+        terms = dot(left, pixels, FLAT)
         for d in range(3):
-            tap = edge_tap(turns[edge], lower, edge, d, False)
-            out[tap] += terms[d * share : (d + 1) * share]
+            out[taps[d]] += terms[d * share : (d + 1) * share]
+        filters = jnp.concatenate([weight[tap] for tap in taps], axis=0)
+        terms_out[edge][...] = terms_of(dot(filters, pixels, TURNED), share, batch)
     out[...] = out[...] * scale
 
 
-def seam_filters(scale, turns, edges, inner, messages):
+def seam_filters(scale, edges, inner, weight, messages):
     _, side, batch, channels = edges.shape
     share = inner.shape[1]
-    smem = pl.BlockSpec(memory_space=pltpu.SMEM)
     vmem = pl.BlockSpec(memory_space=pltpu.VMEM)
 
     def body(*refs):
@@ -358,46 +363,58 @@
 
     return pl.pallas_call(
         body,
-        in_specs=[smem] * 3 + [vmem] * 5,
-        out_specs=vmem,
-        out_shape=jax.ShapeDtypeStruct(inner.shape, jnp.float32),
+        in_specs=[vmem] * 6,
+        out_specs=[vmem] * 4,
+        out_shape=[jax.ShapeDtypeStruct(inner.shape, jnp.float32)]
+        + [jax.ShapeDtypeStruct((share, side * batch), jnp.bfloat16)] * 3,
         compiler_params=pltpu.CompilerParams(vmem_limit_bytes=BIG),
         cost_estimate=pl.CostEstimate(
-            flops=18 * share * side * batch * channels,
+            flops=36 * share * side * batch * channels,
             bytes_accessed=6 * side * batch * channels,
             transcendentals=0,
         ),
         name="seam_filters",
-    )(*turns[1:], edges, inner, *messages)
-
-
-def conv_kernel(mirrored, own_turn, east, west, across, source, *refs):
-    out, padded, spread, sums, whole, sems = refs[-6:]
-    weights = refs[:-6]
+    )(edges, inner, weight, *messages)
+
+
+def add_messages(turn, messages, sums, offset, share, batch, side):
+    lower = half_of_band()
+    for edge, message in enumerate(messages):
+        first, step = edge_place(turn, lower, edge, side)
+        for pos in range(side):
+            sums[first + pos * step + offset] += message[
+                0:share, pos * batch : (pos + 1) * batch
+            ].astype(jnp.float32)
+
+
+def grad_kernel(own_turn, east, west, across, source, *refs):
+    out, padded, spread, sums, done, whole, sems, out_sems = refs[-8:]
+    weights = refs[:-8]
     side, cols, batch, channels = padded.shape
     cols -= 2
     share = weights[0].shape[1]
+    ahead = 3
 
     def row_copy(row):
         return pltpu.make_async_copy(
             source.at[pl.ds(row * cols, cols)], padded.at[row, pl.ds(1, cols)], sems.at[row]
         )
 
-    for row in range(side):
+    def row_out(row):
+        pixels = pl.ds(row * cols, cols)
+        return pltpu.make_async_copy(done.at[pixels], out.at[pixels], out_sems.at[row])
+
+    for row in range(ahead):
         row_copy(row).start()
     tile = jnp.zeros((batch, channels), padded.dtype)
     for row in range(side):
         padded[row, 0] = tile
         padded[row, cols + 1] = tile
 
-    if mirrored:
-        gather_filters(weights, whole)
-        pick = one_hot(share, channels)
+    gather_filters(weights, whole)
+    pick = one_hot(share, channels)
     empty = jnp.zeros((share, channels), spread.dtype)
-    blocks = [
-        dot(pick, whole[8 - tap], TURNED).astype(jnp.bfloat16) if mirrored else weights[0][tap]
-        for tap in range(9)
-    ]
+    blocks = [dot(pick, whole[8 - tap], TURNED).astype(jnp.bfloat16) for tap in range(9)]
     for row in range(3):
         for out_col in range(2):
             for in_col in range(4):
@@ -408,17 +425,9 @@
                     blocks[row * 3 + tap] if 0 <= tap <= 2 else empty
                 )
     sums[...] = jnp.zeros_like(sums)
-    lower = half_of_band()
-    for edge, message in enumerate((east, west, across)):
-        first, step = edge_place(own_turn[0], lower, edge, side)
-        for pos in range(side):
-            sums[first + pos * step + cols] += message[
-                0:share, pos * batch : (pos + 1) * batch
-            ].astype(jnp.float32)
-
-    @pl.loop(0, side, unroll=4)
-    def _(row):
-        row_copy(row).wait()
+    add_messages(own_turn[0], (east, west, across), sums, cols, share, batch, side)
+
+    def add_row(row):
         for start in range(0, cols, 4):
             right = jnp.concatenate(
                 [
@@ -432,7 +441,6 @@
             terms = dot(spread[...], right, TURNED)
             for half in (0, 2):
                 for col in range(2):
-                    at = start + half + col
                     part = [
                         terms[
                             (k * 2 + col) * share : (k * 2 + col + 1) * share,
@@ -440,47 +448,205 @@
                         ]
                         for k in range(3)
                     ]
+                    at = start + half + col
                     pixel = row * cols + at
                     sums[pixel + 2 * cols] += part[0]
                     sums[pixel + cols] += part[1]
-                    done = jnp.maximum(pixel - cols, at)
-                    out[done] = (sums[pixel] + part[2]).astype(out.dtype)
+                    done[jnp.maximum(pixel - cols, at)] = (sums[pixel] + part[2]).astype(
+                        done.dtype
+                    )
+
+    row_copy(0).wait()
+    row_copy(ahead).start()
+    add_row(0)
+
+    @pl.loop(1, side, unroll=3)
+    def _(row):
+        @pl.when(row + ahead < side)
+        def _():
+            row_copy(row + ahead).start()
+
+        row_copy(row).wait()
+        add_row(row)
+        row_out(row - 1).start()
 
     for at in range(cols):
-        out[(side - 1) * cols + at] = sums[side * cols + at].astype(out.dtype)
-
-
-def convolved(mirrored, turn, messages, source, weights, *after):
+        done[(side - 1) * cols + at] = sums[side * cols + at].astype(done.dtype)
+    row_out(side - 1).start()
+    for row in range(side):
+        row_out(row).wait()
+
+
+def grad_conv(turn, messages, source, weights):
     pixels, batch, channels = source.shape
     taps, share, _ = weights[0].shape
     side = math.isqrt(pixels)
-    smem = pl.BlockSpec(memory_space=pltpu.SMEM)
     vmem = pl.BlockSpec(memory_space=pltpu.VMEM)
-
-    def body(*refs):
-        conv_kernel(mirrored, *refs)
-
+    anywhere = pl.BlockSpec(memory_space=pl.ANY)
     return pl.pallas_call(
-        body,
-        in_specs=[smem] + [vmem] * 3
-        + [pl.BlockSpec(memory_space=pl.ANY)]
-        + [vmem] * len(weights)
-        + [pl.BlockSpec(memory_space=pl.ANY)] * len(after),
-        out_specs=vmem,
+        grad_kernel,
+        in_specs=[pl.BlockSpec(memory_space=pltpu.SMEM)]
+        + [vmem] * 3
+        + [anywhere]
+        + [vmem] * len(weights),
+        out_specs=anywhere,
         out_shape=jax.ShapeDtypeStruct((pixels, share, batch), jnp.bfloat16),
         scratch_shapes=[
             pltpu.VMEM((side, side + 2, batch, channels), jnp.bfloat16),
             pltpu.VMEM((6 * share, 4 * channels), jnp.bfloat16),
             pltpu.VMEM((pixels + 2 * side, share, batch), jnp.float32),
+            pltpu.VMEM((pixels, share, batch), jnp.bfloat16),
             pltpu.VMEM((taps, channels, channels), jnp.bfloat16),
+            pltpu.SemaphoreType.DMA((side,)),
             pltpu.SemaphoreType.DMA((side,)),
         ],
         compiler_params=pltpu.CompilerParams(vmem_limit_bytes=BIG),
         cost_estimate=pl.CostEstimate(
             flops=2400 * source.size, bytes_accessed=3 * source.size, transcendentals=0
         ),
-        name="grad_conv" if mirrored else "conv",
-    )(turn, *messages, source, *weights, *after)
+        name="grad_conv",
+    )(turn, *messages, source, *weights)
+
+
+def conv_kernel(
+    own_turn, east, west, across, source, weight, after,
+    out, padded, spread, sums, done, sems, out_sems,
+):
+    rows, cols, batch, channels = padded.shape
+    rows -= 2
+    cols -= 2
+    share = weight.shape[1]
+    blocks = rows // 2
+    ahead = 2
+
+    def pair_copy(pair):
+        row = 2 * pair + 1
+        return [
+            pltpu.make_async_copy(
+                source.at[pl.ds((row + k) * cols, cols)],
+                padded.at[row + k + 1, pl.ds(1, cols)],
+                sems.at[row + k],
+            )
+            for k in range(2)
+        ]
+
+    def first_copy():
+        return pltpu.make_async_copy(
+            source.at[pl.ds(0, cols)], padded.at[1, pl.ds(1, cols)], sems.at[0]
+        )
+
+    def last_copy():
+        return pltpu.make_async_copy(
+            source.at[pl.ds((rows - 1) * cols, cols)],
+            padded.at[rows, pl.ds(1, cols)],
+            sems.at[rows - 1],
+        )
+
+    def block_out(block):
+        pixels = pl.ds(2 * block * cols, 2 * cols)
+        return pltpu.make_async_copy(done.at[pixels], out.at[pixels], out_sems.at[block])
+
+    first_copy().start()
+    for pair in range(ahead):
+        for copy in pair_copy(pair):
+            copy.start()
+    tile = jnp.zeros((batch, channels), padded.dtype)
+    for row in range(rows + 2):
+        padded[row, 0] = tile
+        padded[row, cols + 1] = tile
+    for col in range(cols):
+        padded[0, col + 1] = tile
+        padded[rows + 1, col + 1] = tile
+
+    spread[...] = jnp.zeros_like(spread)
+    for tap in range(9):
+        value = weight[tap]
+        for row in range(2):
+            for col in range(2):
+                to = (row * 2 + col) * share
+                at = ((row + tap // 3) * 4 + col + tap % 3) * channels
+                spread[to : to + share, at : at + channels] = value
+    sums[...] = jnp.zeros_like(sums)
+    add_messages(own_turn[0], (east, west, across), sums, 0, share, batch, rows)
+
+    def add_block(block):
+        for start in range(0, cols, 4):
+            right = jnp.concatenate(
+                [
+                    jnp.concatenate(
+                        [
+                            padded[2 * block + row, start + half + col]
+                            for row in range(4)
+                            for col in range(4)
+                        ],
+                        axis=1,
+                    )
+                    for half in (0, 2)
+                ],
+                axis=0,
+            )
+            terms = dot(spread[...], right, TURNED)
+            for half in (0, 2):
+                for row in range(2):
+                    for col in range(2):
+                        part = terms[
+                            (row * 2 + col) * share : (row * 2 + col + 1) * share,
+                            half // 2 * batch : (half // 2 + 1) * batch,
+                        ]
+                        pixel = (2 * block + row) * cols + start + half + col
+                        done[pixel] = (sums[pixel] + part).astype(done.dtype)
+        block_out(block).start()
+
+    first_copy().wait()
+
+    @pl.loop(0, blocks - 1)
+    def _(block):
+        @pl.when(block + ahead < blocks - 1)
+        def _():
+            for copy in pair_copy(block + ahead):
+                copy.start()
+
+        @pl.when(block + ahead == blocks - 1)
+        def _():
+            last_copy().start()
+
+        for copy in pair_copy(block):
+            copy.wait()
+        add_block(block)
+
+    last_copy().wait()
+    add_block(blocks - 1)
+    for block in range(blocks):
+        block_out(block).wait()
+
+
+def convolved(turn, messages, source, weight, after):
+    pixels, batch, channels = source.shape
+    taps, share, _ = weight.shape
+    side = math.isqrt(pixels)
+    vmem = pl.BlockSpec(memory_space=pltpu.VMEM)
+    anywhere = pl.BlockSpec(memory_space=pl.ANY)
+    return pl.pallas_call(
+        conv_kernel,
+        in_specs=[pl.BlockSpec(memory_space=pltpu.SMEM)]
+        + [vmem] * 3
+        + [anywhere, vmem, anywhere],
+        out_specs=anywhere,
+        out_shape=jax.ShapeDtypeStruct((pixels, share, batch), jnp.bfloat16),
+        scratch_shapes=[
+            pltpu.VMEM((side + 2, side + 2, batch, channels), jnp.bfloat16),
+            pltpu.VMEM((4 * share, 16 * channels), jnp.bfloat16),
+            pltpu.VMEM((pixels, share, batch), jnp.float32),
+            pltpu.VMEM((pixels, share, batch), jnp.bfloat16),
+            pltpu.SemaphoreType.DMA((side,)),
+            pltpu.SemaphoreType.DMA((side // 2,)),
+        ],
+        compiler_params=pltpu.CompilerParams(vmem_limit_bytes=BIG),
+        cost_estimate=pl.CostEstimate(
+            flops=2400 * source.size, bytes_accessed=3 * source.size, transcendentals=0
+        ),
+        name="conv",
+    )(turn, *messages, source, weight, after)
 
 
 def sum_over_tiles(total, count):
@@ -521,18 +687,14 @@
         lax.ppermute(own, "chan", [(i, i ^ flip) for i in range(channels // share)])
         for flip in range(1, channels // share)
     ]
-    turns = [orientation] + [
-        lax.ppermute(orientation, "tile", pairs)
-        for pairs in (westward, eastward, acrossward)
-    ]
     upstream, turned, *sends = lay_upstream(orientation, weights, grad_out[0])
     grad_messages = exchanged(sends)
-    field, edges, inner, *sends = lay_field(turns, own, tiles[0], turned)
+    field, edges, inner = lay_field(orientation, tiles[0], turned)
+    scale = 1.0 / math.sqrt(count * batch * side * side)
+    total, *sends = seam_filters(scale, edges, inner, own, grad_messages)
     conv_messages = exchanged(sends)
-    scale = 1.0 / math.sqrt(count * batch * side * side)
-    total = seam_filters(scale, turns, edges, inner, grad_messages)
-    grad = convolved(True, orientation, grad_messages, upstream, weights)
-    conv = convolved(False, orientation, conv_messages, field, weights[:1], grad)
+    grad = grad_conv(orientation, grad_messages, upstream, weights)
+    conv = convolved(orientation, conv_messages, field, own, grad)
     total = sum_over_tiles(total, count)
     shape = (side, side, share, batch)
     conv_out = conv.reshape(shape).transpose(3, 0, 1, 2)[None]

time: 82.2 us -> 79.7 us (0.970)
  waiting for transfers between devices: 0.04 us -> 4.18 us
  starting transfers between devices: 22.8 us -> 18.7 us
  Pallas kernels: 54.8 us -> 52.2 us
    ppermute x3 -> x0, starting transfers between devices: 5.6 us -> none  [per_device(): lax.ppermute(orientation, 'tile', pairs)]
    ppermute x3, waiting for transfers between devices: 0.01 us -> 3.73 us  [per_device(): lax.ppermute(own, 'chan', [(i, i ^ flip) for i in range(channels // share)])]
    pallas_call x4, Pallas kernels: 44.3 us -> 41.7 us  [the longest x1 15.2 us: convolved(): pl.pallas_call(conv_kernel, in_specs=[pl.BlockSpec(memory_space=pltpu.SME...]
    ppermute x2, starting transfers between devices: 5.93 us -> 7.47 us  [exchanged(): lax.ppermute(sends[1], 'tile', westward)]
  transfers between devices with their start and end apart: 16 -> 13, of which waited for: 0 -> 3; matrix products, arithmetic and copies ran while one was open for 0% -> 0% of each run, Pallas kernels for 67% -> 48%
where the time goes in v4:
time: 79.7 us; the launch traced here: 79.3 us
  Pallas kernels  52.2 us (65%)
  starting transfers between devices  18.7 us (23%)
  waiting for transfers between devices  4.18 us (5%)
  local copies, waits for them, and re-layouts  2.11 us (3%)
  between operations  1.42 us (2%)
    pallas_call x1, Pallas kernels, convolved(): pl.pallas_call(conv_kernel, in_specs=[pl.BlockSpec(memory_space=pltpu.SME...  15.2 us
    pallas_call x1, Pallas kernels, grad_conv(): pl.pallas_call(grad_kernel, in_specs=[pl.BlockSpec(memory_space=pltpu.SME...  11.9 us
    pallas_call x1, Pallas kernels, lay_field(): pl.pallas_call(field_kernel, in_specs=[pl.BlockSpec(memory_space=pltpu.SM...  11.3 us
    pallas_call x1, Pallas kernels, lay_upstream(): pl.pallas_call(upstream_kernel, in_specs=[smem] + [vmem] * len(weights) +...  10.5 us
    ppermute x2, starting transfers between devices, exchanged(): lax.ppermute(sends[1], 'tile', westward)  7.47 us
    ppermute x4, starting transfers between devices, other(): return lax.ppermute(total, 'tile', [(i, i ^ flip) for i in range(count)])  6.02 us
    ppermute x3, waiting for transfers between devices, per_device(): lax.ppermute(own, 'chan', [(i, i ^ flip) for i in range(channels // share)])  3.73 us
    pallas_call x1, Pallas kernels, seam_filters(): pl.pallas_call(body, in_specs=[vmem] * 6, out_specs=[vmem] * 4, out_shape...  3.34 us
  transfers between devices with their start and end apart: 13, of which 3 were waited for; matrix products, arithmetic and copies ran while one was open for 0% of the time, Pallas kernels for 48%

profile of v4, /device:TPU:0, one launch (start us, length us, event | category | flops | bytes accessed | tf_op | source)
XLA Modules:
  0.0 79.3 jit_solution(17739341138442936019)
XLA Ops:
  0.6 2.5 %collective-permute-start.2 = (bf16[9,32,128]{2,1,0:T(8,128)(2,1)}, bf16[9,32,128]{2,1,0:T(8,128)(2,1)S(1)}, u32[]{:S(2)}, u32[]{:S(2)}) collective-permute-start(bf16[9,32,128]{2,1,0:T(8,128)(2,1)} %bitcast.19), channel_id=1, source_target_pairs={{0,3},{1,2},{2,1},{3,0},{4,7},{5,6},{6,5},{7,4},{8,11},{9,10},{10,... | collective-permute-start | bytes 221192 | tf_op jit(solution)/shard_map/ppermute | solution.py:687
  3.1 0.6 collective-permute-start.1
  3.7 0.0 collective-permute-start
  4.4 1.6 %collective-permute-done.2.other3.refs_3_ = bf16[9,32,128]{2,1,0:T(8,128)(2,1)S(1)} collective-permute-done((bf16[9,32,128]{2,1,0:T(8,128)(2,1)}, bf16[9,32,128]{2,1,0:T(8,128)(2,1)S(1)}, u32[]{:S(2)}, u32[]{:S(2)}) %collective-permute-start.2) | collective-permute-done | bytes 73760 | tf_op jit(solution)/shard_map/ppermute | solution.py:687
  6.1 0.0 copy-start.7
  6.1 2.1 %collective-permute-done.1.other2.refs_2_ = bf16[9,32,128]{2,1,0:T(8,128)(2,1)S(1)} collective-permute-done((bf16[9,32,128]{2,1,0:T(8,128)(2,1)}, bf16[9,32,128]{2,1,0:T(8,128)(2,1)S(1)}, u32[]{:S(2)}, u32[]{:S(2)}) %collective-permute-start.1) | collective-permute-done | bytes 73760 | tf_op jit(solution)/shard_map/ppermute | solution.py:687
  8.2 0.0 copy-start.8
  8.2 0.0 collective-permute-done.other1.refs_1_
  8.2 0.0 copy-start.9
  8.2 0.0 copy-done.7
  8.2 0.6 copy-done.8
  8.8 0.0 copy-done.9
  8.8 10.5 %lay_upstream.1 = (bf16[256,128,128]{2,1,0:T(8,128)(2,1)}, bf16[16,32,2048]{2,1,0:T(8,128)(2,1)}, bf16[64,2176]{1,0:T(8,128)(2,1)}, bf16[64,2176]{1,0:T(8,128)(2,1)}, bf16[64,2176]{1,0:T(8,128)(2,1)}) custom-call(s32[1]{0:T(128)S(6)} %copy.7.own_turn, bf16[9,32,128]{2,1,0:T(8,128)(2,1)} %bitcast.22, bf16[9,32,128]{2,1,0:T(8,128)(2,1)} %copy-done.9, ...), custom_call_target="tpu_custom_call" | custom-call | flops 4294967296 | bytes 20971520 | tf_op jit(solution)/shard_map/lay_upstream/pallas_call | solution.py:195
  19.3 4.0 %collective-permute-start.3 = (bf16[64,2176]{1,0:T(8,128)(2,1)}, bf16[64,2176]{1,0:T(8,128)(2,1)S(1)}, u32[]{:S(2)}, u32[]{:S(2)}) collective-permute-start(bf16[64,2176]{1,0:T(8,128)(2,1)} %get-tuple-element.18), channel_id=1, source_target_pairs={{0,24},{4,28},{8,0},{12,4},{16,8},{20,12},{24,16},{28,20},{1,25},{... | collective-permute-start | bytes 835592 | tf_op jit(solution)/shard_map/ppermute | solution.py:680
  23.3 0.0 collective-permute-start.4
  23.3 1.5 %collective-permute-start.5 = (bf16[64,2176]{1,0:T(8,128)(2,1)}, bf16[64,2176]{1,0:T(8,128)(2,1)S(1)}, u32[]{:S(2)}, u32[]{:S(2)}) collective-permute-start(bf16[64,2176]{1,0:T(8,128)(2,1)} %get-tuple-element.20), channel_id=1, source_target_pairs={{0,4},{4,0},{8,12},{12,8},{16,20},{20,16},{24,28},{28,24},{1,5},{5... | collective-permute-start | bytes 835592 | tf_op jit(solution)/shard_map/ppermute | solution.py:682
  24.8 11.3 %lay_field.1 = (bf16[256,128,128]{2,1,0:T(8,128)(2,1)}, bf16[3,16,128,128]{3,2,1,0:T(8,128)(2,1)}, f32[9,32,128]{2,1,0:T(8,128)}) custom-call(s32[1]{0:T(128)S(6)} %copy.7.own_turn, bf16[128,16,16,128]{3,2,1,0:T(8,128)(2,1)} %bitcast.27, bf16[16,32,2048]{2,1,0:T(8,128)(2,1)} %get-tuple-element.15.turned), custom_call_target="tpu_custom_call" | custom-call | flops 7549747200 | bytes 20971520 | tf_op jit(solution)/shard_map/lay_field/pallas_call | solution.py:312
  36.0 0.0 collective-permute-done.3.refs_3_.east
  36.0 0.0 copy-start
  36.1 0.4 collective-permute-done.4.refs_4_.west
  36.5 0.0 copy-start.1
  36.5 0.0 collective-permute-done.5.refs_5_.across
  36.5 0.3 copy-done
  36.8 0.4 copy-done.1
  37.2 0.1 copy-done.2
  37.3 3.3 %seam_filters.1 = (f32[9,32,128]{2,1,0:T(8,128)}, bf16[32,2048]{1,0:T(8,128)(2,1)}, bf16[32,2048]{1,0:T(8,128)(2,1)}, bf16[32,2048]{1,0:T(8,128)(2,1)}) custom-call(bf16[3,16,128,128]{3,2,1,0:T(8,128)(2,1)} %get-tuple-element.16.refs_0_, f32[9,32,128]{2,1,0:T(8,128)} %get-tuple-element.17.refs_1_, bf16[9,32,128]{2,1,0:T(8,128)(2,1)} %bitcast.23, ...), custom_call_target="tpu_custom_call" | custom-call | flops 301989888 | bytes 1572864 | tf_op jit(solution)/shard_map/seam_filters/pallas_call | solution.py:364
  40.6 3.5 %collective-permute-start.6 = (bf16[32,2048]{1,0:T(8,128)(2,1)}, bf16[32,2048]{1,0:T(8,128)(2,1)S(1)}, u32[]{:S(2)}, u32[]{:S(2)}) collective-permute-start(bf16[32,2048]{1,0:T(8,128)(2,1)} %get-tuple-element.21), channel_id=1, source_target_pairs={{0,24},{4,28},{8,0},{12,4},{16,8},{20,12},{24,16},{28,20},{1,25},{... | collective-permute-start | bytes 393224 | tf_op jit(solution)/shard_map/ppermute | solution.py:680
  44.1 0.0 collective-permute-start.7
  44.1 0.5 collective-permute-start.8
  44.6 1.5 %collective-permute-start.9 = (f32[9,32,128]{2,1,0:T(8,128)}, f32[9,32,128]{2,1,0:T(8,128)S(1)}, u32[]{:S(2)}, u32[]{:S(2)}) collective-permute-start(f32[9,32,128]{2,1,0:T(8,128)} %get-tuple-element.26), channel_id=1, source_target_pairs={{0,4},{4,0},{8,12},{12,8},{16,20},{20,16},{24,28},{28,24},{1,5},{5... | collective-permute-start | bytes 442376 | tf_op jit(solution)/shard_map/ppermute | solution.py:658
  46.1 11.9 %grad_conv.1.after = bf16[256,32,128]{2,1,0:T(8,128)(2,1)} custom-call(s32[1]{0:T(128)S(6)} %copy.7.own_turn, bf16[64,2176]{1,0:T(8,128)(2,1)} %copy-done, bf16[64,2176]{1,0:T(8,128)(2,1)} %copy-done.1, bf16[64,2176]{1,0:T(8,128)(2,1)} %copy-done.2, bf16[256,128,128]{2,1,0:T(8,128)(2,1)} %get-tuple-element.25.source, bf16[9,32,128]{2,1,0:T(8,128)(2,1)} %bitcast.24, ...), custom_call_target="tpu_custom_call" | custom-call | flops 10066329600 | bytes 12582912 | tf_op jit(solution)/shard_map/grad_conv/pallas_call | solution.py:486
  58.0 0.0 collective-permute-done.9
  58.0 0.0 copy-done.3
  58.1 3.9 %collective-permute-start.12 = (f32[9,32,128]{2,1,0:T(8,128)S(1)}, f32[9,32,128]{2,1,0:T(8,128)S(1)}, u32[]{:S(2)}, u32[]{:S(2)}) collective-permute-start(f32[9,32,128]{2,1,0:T(8,128)S(1)} %add.12), channel_id=1, source_target_pairs={{0,24},{4,28},{8,16},{12,20},{16,8},{20,12},{24,0},{28,4},{1,25},{... | collective-permute-start | bytes 442376 | tf_op jit(solution)/shard_map/ppermute | solution.py:658
  62.0 0.0 collective-permute-start.11
  62.0 0.0 collective-permute-done.6.east
  62.0 0.6 collective-permute-start.10
  62.6 0.0 collective-permute-done.7.west
  62.6 0.0 collective-permute-done.8.across
  62.6 0.0 copy-start.6
  62.6 0.0 copy-done.4
  62.7 0.6 copy-done.5
  63.3 0.0 copy-done.6
  63.3 15.2 %conv.1 = bf16[256,32,128]{2,1,0:T(8,128)(2,1)} custom-call(s32[1]{0:T(128)S(6)} %copy.7.own_turn, bf16[32,2048]{1,0:T(8,128)(2,1)} %copy-done.4, bf16[32,2048]{1,0:T(8,128)(2,1)} %copy-done.5, bf16[32,2048]{1,0:T(8,128)(2,1)} %copy-done.6, bf16[256,128,128]{2,1,0:T(8,128)(2,1)} %get-tuple-element.24.source, bf16[9,32,128]{2,1,0:T(8,128)(2,1)} %bitcast.25, ...), custom_call_target="tpu_custom_call" | custom-call | flops 10066329600 | bytes 12582912 | tf_op jit(solution)/shard_map/conv/pallas_call | solution.py:629
  78.5 0.0 collective-permute-done.12
  78.5 0.0 collective-permute-done.11
  78.5 0.0 collective-permute-done.10
  78.6 0.7 add_add_fusion
  (5 shorter events, 0.0 us)
Async XLA Ops:
  0.6 5.4 %collective-permute-start.2 = (bf16[9,32,128]{2,1,0:T(8,128)(2,1)}, bf16[9,32,128]{2,1,0:T(8,128)(2,1)S(1)}, u32[]{:S(2)}, u32[]{:S(2)}) collective-permute-start(bf16[9,32,128]{2,1,0:T(8,128)(2,1)} %bitcast.19), channel_id=1, source_target_pairs={{0,3},{1,2},{2,1},{3,0},{4,7},{5,6},{6,5},{7,4},{8,11},{9,10},{10,... | collective-permute-start | bytes 221192 | tf_op jit(solution)/shard_map/ppermute | solution.py:687
  3.1 5.1 %collective-permute-start.1 = (bf16[9,32,128]{2,1,0:T(8,128)(2,1)}, bf16[9,32,128]{2,1,0:T(8,128)(2,1)S(1)}, u32[]{:S(2)}, u32[]{:S(2)}) collective-permute-start(bf16[9,32,128]{2,1,0:T(8,128)(2,1)} %bitcast.20), channel_id=1, source_target_pairs={{0,2},{1,3},{2,0},{3,1},{4,6},{5,7},{6,4},{7,5},{8,10},{9,11},{10,... | collective-permute-start | bytes 221192 | tf_op jit(solution)/shard_map/ppermute | solution.py:687
  3.7 4.4 %collective-permute-start = (bf16[9,32,128]{2,1,0:T(8,128)(2,1)}, bf16[9,32,128]{2,1,0:T(8,128)(2,1)S(1)}, u32[]{:S(2)}, u32[]{:S(2)}) collective-permute-start(bf16[9,32,128]{2,1,0:T(8,128)(2,1)} %bitcast.21), channel_id=1, source_target_pairs={{0,1},{1,0},{2,3},{3,2},{4,5},{5,4},{6,7},{7,6},{8,9},{9,8},{10,11... | collective-permute-start | bytes 221192 | tf_op jit(solution)/shard_map/ppermute | solution.py:687
  6.1 2.1 %copy-start.7 = (bf16[9,32,128]{2,1,0:T(8,128)(2,1)}, bf16[9,32,128]{2,1,0:T(8,128)(2,1)S(1)}, u32[]{:S(2)}) copy-start(bf16[9,32,128]{2,1,0:T(8,128)(2,1)S(1)} %collective-permute-done.2.other3.refs_3_) | copy-start | bytes 221188
  8.2 0.6 copy-start.8
  8.2 0.6 copy-start.9
  19.3 16.8 %collective-permute-start.3 = (bf16[64,2176]{1,0:T(8,128)(2,1)}, bf16[64,2176]{1,0:T(8,128)(2,1)S(1)}, u32[]{:S(2)}, u32[]{:S(2)}) collective-permute-start(bf16[64,2176]{1,0:T(8,128)(2,1)} %get-tuple-element.18), channel_id=1, source_target_pairs={{0,24},{4,28},{8,0},{12,4},{16,8},{20,12},{24,16},{28,20},{1,25},{... | collective-permute-start | bytes 835592 | tf_op jit(solution)/shard_map/ppermute | solution.py:680
  23.3 13.2 %collective-permute-start.4 = (bf16[64,2176]{1,0:T(8,128)(2,1)}, bf16[64,2176]{1,0:T(8,128)(2,1)S(1)}, u32[]{:S(2)}, u32[]{:S(2)}) collective-permute-start(bf16[64,2176]{1,0:T(8,128)(2,1)} %get-tuple-element.19), channel_id=1, source_target_pairs={{0,8},{4,12},{8,16},{12,20},{16,24},{20,28},{24,0},{28,4},{1,9},{5... | collective-permute-start | bytes 835592 | tf_op jit(solution)/shard_map/ppermute | solution.py:681
  23.3 13.2 %collective-permute-start.5 = (bf16[64,2176]{1,0:T(8,128)(2,1)}, bf16[64,2176]{1,0:T(8,128)(2,1)S(1)}, u32[]{:S(2)}, u32[]{:S(2)}) collective-permute-start(bf16[64,2176]{1,0:T(8,128)(2,1)} %get-tuple-element.20), channel_id=1, source_target_pairs={{0,4},{4,0},{8,12},{12,8},{16,20},{20,16},{24,28},{28,24},{1,5},{5... | collective-permute-start | bytes 835592 | tf_op jit(solution)/shard_map/ppermute | solution.py:682
  36.0 0.7 copy-start
  36.5 0.7 copy-start.1
  36.5 0.8 %copy-start.2 = (bf16[64,2176]{1,0:T(8,128)(2,1)}, bf16[64,2176]{1,0:T(8,128)(2,1)S(1)}, u32[]{:S(2)}) copy-start(bf16[64,2176]{1,0:T(8,128)(2,1)S(1)} %collective-permute-done.5.refs_5_.across) | copy-start | bytes 835588
  40.6 21.4 %collective-permute-start.6 = (bf16[32,2048]{1,0:T(8,128)(2,1)}, bf16[32,2048]{1,0:T(8,128)(2,1)S(1)}, u32[]{:S(2)}, u32[]{:S(2)}) collective-permute-start(bf16[32,2048]{1,0:T(8,128)(2,1)} %get-tuple-element.21), channel_id=1, source_target_pairs={{0,24},{4,28},{8,0},{12,4},{16,8},{20,12},{24,16},{28,20},{1,25},{... | collective-permute-start | bytes 393224 | tf_op jit(solution)/shard_map/ppermute | solution.py:680
  44.1 18.5 %collective-permute-start.7 = (bf16[32,2048]{1,0:T(8,128)(2,1)}, bf16[32,2048]{1,0:T(8,128)(2,1)S(1)}, u32[]{:S(2)}, u32[]{:S(2)}) collective-permute-start(bf16[32,2048]{1,0:T(8,128)(2,1)} %get-tuple-element.22), channel_id=1, source_target_pairs={{0,8},{4,12},{8,16},{12,20},{16,24},{20,28},{24,0},{28,4},{1,9},{5... | collective-permute-start | bytes 393224 | tf_op jit(solution)/shard_map/ppermute | solution.py:681
  44.1 18.5 %collective-permute-start.8 = (bf16[32,2048]{1,0:T(8,128)(2,1)}, bf16[32,2048]{1,0:T(8,128)(2,1)S(1)}, u32[]{:S(2)}, u32[]{:S(2)}) collective-permute-start(bf16[32,2048]{1,0:T(8,128)(2,1)} %get-tuple-element.23), channel_id=1, source_target_pairs={{0,4},{4,0},{8,12},{12,8},{16,20},{20,16},{24,28},{28,24},{1,5},{5... | collective-permute-start | bytes 393224 | tf_op jit(solution)/shard_map/ppermute | solution.py:682
  44.6 13.4 %collective-permute-start.9 = (f32[9,32,128]{2,1,0:T(8,128)}, f32[9,32,128]{2,1,0:T(8,128)S(1)}, u32[]{:S(2)}, u32[]{:S(2)}) collective-permute-start(f32[9,32,128]{2,1,0:T(8,128)} %get-tuple-element.26), channel_id=1, source_target_pairs={{0,4},{4,0},{8,12},{12,8},{16,20},{20,16},{24,28},{28,24},{1,5},{5... | collective-permute-start | bytes 442376 | tf_op jit(solution)/shard_map/ppermute | solution.py:658
  46.1 11.9 %copy-start.3 = (f32[9,32,128]{2,1,0:T(8,128)S(1)}, f32[9,32,128]{2,1,0:T(8,128)}, u32[]{:S(2)}) copy-start(f32[9,32,128]{2,1,0:T(8,128)} %get-tuple-element.26) | copy-start | bytes 442372
  58.1 20.4 %collective-permute-start.12 = (f32[9,32,128]{2,1,0:T(8,128)S(1)}, f32[9,32,128]{2,1,0:T(8,128)S(1)}, u32[]{:S(2)}, u32[]{:S(2)}) collective-permute-start(f32[9,32,128]{2,1,0:T(8,128)S(1)} %add.12), channel_id=1, source_target_pairs={{0,24},{4,28},{8,16},{12,20},{16,8},{20,12},{24,0},{28,4},{1,25},{... | collective-permute-start | bytes 442376 | tf_op jit(solution)/shard_map/ppermute | solution.py:658
  62.0 16.6 %collective-permute-start.11 = (f32[9,32,128]{2,1,0:T(8,128)S(1)}, f32[9,32,128]{2,1,0:T(8,128)S(1)}, u32[]{:S(2)}, u32[]{:S(2)}) collective-permute-start(f32[9,32,128]{2,1,0:T(8,128)S(1)} %add.12), channel_id=1, source_target_pairs={{0,16},{4,20},{8,24},{12,28},{16,0},{20,4},{24,8},{28,12},{1,17},{... | collective-permute-start | bytes 442376 | tf_op jit(solution)/shard_map/ppermute | solution.py:658
  62.0 0.7 copy-start.4
  62.0 16.6 %collective-permute-start.10 = (f32[9,32,128]{2,1,0:T(8,128)S(1)}, f32[9,32,128]{2,1,0:T(8,128)S(1)}, u32[]{:S(2)}, u32[]{:S(2)}) collective-permute-start(f32[9,32,128]{2,1,0:T(8,128)S(1)} %add.12), channel_id=1, source_target_pairs={{0,8},{4,12},{8,0},{12,4},{16,24},{20,28},{24,16},{28,20},{1,9},{5... | collective-permute-start | bytes 442376 | tf_op jit(solution)/shard_map/ppermute | solution.py:658
  62.6 0.6 copy-start.5
  62.6 0.7 copy-start.6

commit v5 on v4

--- a/solution.py
+++ b/solution.py
@@ -80,11 +80,6 @@
     return jnp.concatenate([value[:, width:], empty], axis=1)
 
 
-def edge_pixels(turn, lower, edge, held, side):
-    first, step = edge_place(turn, lower, edge, side)
-    return jnp.concatenate([held[first + pos * step] for pos in range(side)], axis=0)
-
-
 def terms_of(product, share, batch):
     return (
         later(product[:share], batch)
@@ -108,15 +103,25 @@
     )
 
 
-def pair_out(held, laid, sems, pair, side):
-    pixels = pl.ds(2 * pair * side, 2 * side)
-    return pltpu.make_async_copy(held.at[pixels], laid.at[pixels], sems.at[pair])
+def edge_columns(turn, lower, edge, flat, side, batch):
+    first, step = edge_place(turn, lower, edge, side)
+    parts = []
+    for pos in range(side):
+        pixel = first + pos * step
+        col = pl.multiple_of(lax.rem(pixel, side) * batch, batch)
+        parts.append(flat[lax.div(pixel, side), :, pl.ds(col, batch)])
+    return jnp.concatenate(parts, axis=1)
+
+
+def turned_out(flat, turned, sems, pair):
+    part = pl.ds(2 * pair, 2)
+    return pltpu.make_async_copy(flat.at[part], turned.at[part], sems.at[pair])
 
 
 def upstream_kernel(
     own_turn, weight, other1, other2, other3, upstream,
-    laid, turned, east, west, across,
-    stage, held, flat, whole, rowed, shuffle, in_sems, out_sems, turned_sems,
+    turned, east, west, across,
+    stage, held, flat, whole, rowed, shuffle, same, in_sems, turned_sems,
 ):
     pairs, batch, rows, side, channels = stage.shape
     taps, share, _ = weight.shape
@@ -125,16 +130,15 @@
         pair_in(upstream, stage, in_sems, pair).start()
     to = lax.broadcasted_iota(jnp.int32, (256, 256), 0)
     come = lax.broadcasted_iota(jnp.int32, (256, 256), 1)
-    same = (to // group == come % side) & (to % group == come // side)
-    shuffle[...] = jnp.where(same, 1.0, 0.0).astype(jnp.bfloat16)
+    moves = (to // group == come % side) & (to % group == come // side)
+    shuffle[...] = jnp.where(moves, 1.0, 0.0).astype(jnp.bfloat16)
+    to = lax.broadcasted_iota(jnp.int32, (channels, channels), 0)
+    come = lax.broadcasted_iota(jnp.int32, (channels, channels), 1)
+    same[...] = jnp.where(to == come, 1.0, 0.0).astype(jnp.bfloat16)
     pick = one_hot(share, channels)
     gather_filters((weight, other1, other2, other3), whole)
     for tap in range(taps):
         rowed[tap] = dot(pick, whole[tap], TURNED).astype(jnp.bfloat16)
-
-    def turned_out(pair):
-        part = pl.ds(2 * pair, 2)
-        return pltpu.make_async_copy(flat.at[part], turned.at[part], turned_sems.at[pair])
 
     @pl.loop(0, pairs)
     def _(pair):
@@ -153,17 +157,16 @@
             )
             moved = dot(shuffle[...], block, FLAT).astype(jnp.bfloat16)
             for row in range(rows):
-                pixels = pl.ds((2 * pair + row) * side, side)
-                held[pixels, start : start + group] = moved[
+                held[row * side : (row + 1) * side, start : start + group] = moved[
                     :, row * channels : (row + 1) * channels
                 ].reshape(side, group, channels)
-        pair_out(held, laid, out_sems, pair, side).start()
         for row in range(rows):
-            pixels = pl.ds((2 * pair + row) * side, side)
             flat[2 * pair + row] = dot(
-                pick, held[pixels].reshape(side * batch, channels), TURNED
+                same[...],
+                held[row * side : (row + 1) * side].reshape(side * batch, channels),
+                TURNED,
             ).astype(jnp.bfloat16)
-        turned_out(pair).start()
+        turned_out(flat, turned, turned_sems, pair).start()
 
     lower = half_of_band()
     turn = own_turn[0]
@@ -172,14 +175,13 @@
             [rowed[edge_tap(turn, lower, edge, 2 - d, True)] for d in range(3)] + [pick],
             axis=0,
         )
-        product = dot(filters, edge_pixels(turn, lower, edge, held, side), TURNED)
+        product = dot(filters, edge_columns(turn, lower, edge, flat, side, batch), FLAT)
         out[0:share, 0 : side * batch] = terms_of(product, share, batch)
         out[share:, 0 : side * batch] = product[3 * share :].astype(jnp.bfloat16)
         code = jnp.full((2 * share, EXTRA), turn, jnp.int32)
         out[:, side * batch :] = code.astype(jnp.float32).astype(jnp.bfloat16)
     for pair in range(pairs):
-        pair_out(held, laid, out_sems, pair, side).wait()
-        turned_out(pair).wait()
+        turned_out(flat, turned, turned_sems, pair).wait()
 
 
 def lay_upstream(turn, weights, upstream):
@@ -189,28 +191,27 @@
     vmem = pl.BlockSpec(memory_space=pltpu.VMEM)
     anywhere = pl.BlockSpec(memory_space=pl.ANY)
     pairs = side // 2
-    laid = jax.ShapeDtypeStruct((side * side, batch, channels), jnp.bfloat16)
-    turned = jax.ShapeDtypeStruct((side, share, side * batch), jnp.bfloat16)
+    turned = jax.ShapeDtypeStruct((side, channels, side * batch), jnp.bfloat16)
     message = jax.ShapeDtypeStruct((2 * share, side * batch + EXTRA), jnp.bfloat16)
     return pl.pallas_call(
         upstream_kernel,
         in_specs=[smem] + [vmem] * len(weights) + [anywhere],
-        out_specs=[anywhere] * 2 + [vmem] * 3,
-        out_shape=[laid, turned] + [message] * 3,
+        out_specs=[anywhere] + [vmem] * 3,
+        out_shape=[turned] + [message] * 3,
         scratch_shapes=[
             pltpu.VMEM((pairs, batch, 2, side, channels), jnp.bfloat16),
-            pltpu.VMEM(laid.shape, jnp.bfloat16),
+            pltpu.VMEM((2 * side, batch, channels), jnp.bfloat16),
             pltpu.VMEM(turned.shape, jnp.bfloat16),
             pltpu.VMEM((taps, channels, channels), jnp.bfloat16),
             pltpu.VMEM((taps, share, channels), jnp.bfloat16),
             pltpu.VMEM((256, 256), jnp.bfloat16),
-            pltpu.SemaphoreType.DMA((pairs,)),
+            pltpu.VMEM((channels, channels), jnp.bfloat16),
             pltpu.SemaphoreType.DMA((pairs,)),
             pltpu.SemaphoreType.DMA((pairs,)),
         ],
         compiler_params=pltpu.CompilerParams(vmem_limit_bytes=BIG),
         cost_estimate=pl.CostEstimate(
-            flops=1024 * upstream.size, bytes_accessed=5 * upstream.size, transcendentals=0
+            flops=1024 * upstream.size, bytes_accessed=4 * upstream.size, transcendentals=0
         ),
         name="lay_upstream",
     )(turn, *weights, upstream)
@@ -218,13 +219,15 @@
 
 def field_kernel(
     own_turn, field, turned, laid, edges, inner,
-    stage, held, padded, total, in_sems, out_sems, turned_sem, edge_sems,
+    stage, held, flat, padded, total, in_sems, out_sems, turned_sem, edge_sems,
 ):
     pairs, batch, rows, side, channels = stage.shape
     share = padded.shape[1]
     width = side * batch
+    chan = lax.axis_index("chan").astype(jnp.int32)
+    own = pl.ds(pl.multiple_of(chan * share, share), share)
     turned_in = pltpu.make_async_copy(
-        turned, padded.at[pl.ds(1, side), :, pl.ds(batch, width)], turned_sem
+        turned.at[:, own], padded.at[pl.ds(1, side), :, pl.ds(batch, width)], turned_sem
     )
     pair_in(field, stage, in_sems, 0).start()
     turned_in.start()
@@ -240,8 +243,11 @@
     def lay(pair):
         pair_in(field, stage, in_sems, pair).wait()
         for row in range(rows):
-            held[pl.ds((2 * pair + row) * side, side)] = jnp.swapaxes(stage[pair, :, row], 0, 1)
-        pair_out(held, laid, out_sems, pair, side).start()
+            block = jnp.swapaxes(stage[pair, :, row], 0, 1)
+            held[pl.ds((2 * pair + row) * side, side)] = block
+            for col in range(side):
+                flat[2 * pair + row, :, col * batch : (col + 1) * batch] = block[col].T
+        turned_out(flat, laid, out_sems, pair).start()
 
     def add_filters(pair):
         cols = 8
@@ -294,19 +300,18 @@
                 value += total[start : start + share, row * channels : (row + 1) * channels]
             inner[row_tap * 3 + col_tap] = value
     for pair in range(pairs):
-        pair_out(held, laid, out_sems, pair, side).wait()
+        turned_out(flat, laid, out_sems, pair).wait()
     for edge in range(3):
         pltpu.make_async_copy(
             held.at[pl.ds(0, side)], edges.at[edge], edge_sems.at[edge]
         ).wait()
 
 
-def lay_field(turn, field, turned):
+def lay_field(turn, field, turned, share):
     batch, side, _, channels = field.shape
-    share = turned.shape[1]
     anywhere = pl.BlockSpec(memory_space=pl.ANY)
     pairs = side // 2
-    laid = jax.ShapeDtypeStruct((side * side, batch, channels), jnp.bfloat16)
+    laid = jax.ShapeDtypeStruct((side, channels, side * batch), jnp.bfloat16)
     edges = jax.ShapeDtypeStruct((3, side, batch, channels), jnp.bfloat16)
     inner = jax.ShapeDtypeStruct((9, share, channels), jnp.float32)
     return pl.pallas_call(
@@ -316,6 +321,7 @@
         out_shape=[laid, edges, inner],
         scratch_shapes=[
             pltpu.VMEM((pairs, batch, 2, side, channels), jnp.bfloat16),
+            pltpu.VMEM((side * side, batch, channels), jnp.bfloat16),
             pltpu.VMEM(laid.shape, jnp.bfloat16),
             pltpu.VMEM((side + 2, share, (side + 2) * batch), jnp.bfloat16),
             pltpu.VMEM((12 * share, 2 * channels), jnp.float32),
@@ -387,17 +393,17 @@
             ].astype(jnp.float32)
 
 
-def grad_kernel(own_turn, east, west, across, source, *refs):
+def conv_kernel(mirrored, own_turn, east, west, across, source, *refs):
     out, padded, spread, sums, done, whole, sems, out_sems = refs[-8:]
     weights = refs[:-8]
-    side, cols, batch, channels = padded.shape
-    cols -= 2
-    share = weights[0].shape[1]
+    side, channels, lanes = padded.shape
+    share, batch = done.shape[1:]
+    cols = lanes // batch - 2
     ahead = 3
 
     def row_copy(row):
         return pltpu.make_async_copy(
-            source.at[pl.ds(row * cols, cols)], padded.at[row, pl.ds(1, cols)], sems.at[row]
+            source.at[row], padded.at[row, :, pl.ds(batch, cols * batch)], sems.at[row]
         )
 
     def row_out(row):
@@ -406,15 +412,18 @@
 
     for row in range(ahead):
         row_copy(row).start()
-    tile = jnp.zeros((batch, channels), padded.dtype)
+    tile = jnp.zeros((channels, batch), padded.dtype)
     for row in range(side):
-        padded[row, 0] = tile
-        padded[row, cols + 1] = tile
-
-    gather_filters(weights, whole)
-    pick = one_hot(share, channels)
+        padded[row, :, 0:batch] = tile
+        padded[row, :, lanes - batch :] = tile
+
+    if mirrored:
+        gather_filters(weights, whole)
+        pick = one_hot(share, channels)
+        blocks = [dot(pick, whole[8 - tap], TURNED).astype(jnp.bfloat16) for tap in range(9)]
+    else:
+        blocks = [weights[0][tap] for tap in range(9)]
     empty = jnp.zeros((share, channels), spread.dtype)
-    blocks = [dot(pick, whole[8 - tap], TURNED).astype(jnp.bfloat16) for tap in range(9)]
     for row in range(3):
         for out_col in range(2):
             for in_col in range(4):
@@ -432,13 +441,21 @@
             right = jnp.concatenate(
                 [
                     jnp.concatenate(
-                        [padded[row, start + half + col] for col in range(4)], axis=1
+                        [
+                            padded[
+                                row,
+                                :,
+                                (start + half + col) * batch : (start + half + col + 1) * batch,
+                            ]
+                            for half in (0, 2)
+                        ],
+                        axis=1,
                     )
-                    for half in (0, 2)
+                    for col in range(4)
                 ],
                 axis=0,
             )
-            terms = dot(spread[...], right, TURNED)
+            terms = dot(spread[...], right, FLAT)
             for half in (0, 2):
                 for col in range(2):
                     part = [
@@ -477,22 +494,28 @@
         row_out(row).wait()
 
 
-def grad_conv(turn, messages, source, weights):
-    pixels, batch, channels = source.shape
+def convolved(mirrored, turn, messages, source, weights, *after):
+    side, channels, width = source.shape
     taps, share, _ = weights[0].shape
-    side = math.isqrt(pixels)
+    batch = width // side
+    pixels = side * side
     vmem = pl.BlockSpec(memory_space=pltpu.VMEM)
     anywhere = pl.BlockSpec(memory_space=pl.ANY)
+
+    def body(*refs):
+        conv_kernel(mirrored, *refs)
+
     return pl.pallas_call(
-        grad_kernel,
+        body,
         in_specs=[pl.BlockSpec(memory_space=pltpu.SMEM)]
         + [vmem] * 3
         + [anywhere]
-        + [vmem] * len(weights),
+        + [vmem] * len(weights)
+        + [anywhere] * len(after),
         out_specs=anywhere,
         out_shape=jax.ShapeDtypeStruct((pixels, share, batch), jnp.bfloat16),
         scratch_shapes=[
-            pltpu.VMEM((side, side + 2, batch, channels), jnp.bfloat16),
+            pltpu.VMEM((side, channels, width + 2 * batch), jnp.bfloat16),
             pltpu.VMEM((6 * share, 4 * channels), jnp.bfloat16),
             pltpu.VMEM((pixels + 2 * side, share, batch), jnp.float32),
             pltpu.VMEM((pixels, share, batch), jnp.bfloat16),
@@ -504,149 +527,8 @@
         cost_estimate=pl.CostEstimate(
             flops=2400 * source.size, bytes_accessed=3 * source.size, transcendentals=0
         ),
-        name="grad_conv",
-    )(turn, *messages, source, *weights)
-
-
-def conv_kernel(
-    own_turn, east, west, across, source, weight, after,
-    out, padded, spread, sums, done, sems, out_sems,
-):
-    rows, cols, batch, channels = padded.shape
-    rows -= 2
-    cols -= 2
-    share = weight.shape[1]
-    blocks = rows // 2
-    ahead = 2
-
-    def pair_copy(pair):
-        row = 2 * pair + 1
-        return [
-            pltpu.make_async_copy(
-                source.at[pl.ds((row + k) * cols, cols)],
-                padded.at[row + k + 1, pl.ds(1, cols)],
-                sems.at[row + k],
-            )
-            for k in range(2)
-        ]
-
-    def first_copy():
-        return pltpu.make_async_copy(
-            source.at[pl.ds(0, cols)], padded.at[1, pl.ds(1, cols)], sems.at[0]
-        )
-
-    def last_copy():
-        return pltpu.make_async_copy(
-            source.at[pl.ds((rows - 1) * cols, cols)],
-            padded.at[rows, pl.ds(1, cols)],
-            sems.at[rows - 1],
-        )
-
-    def block_out(block):
-        pixels = pl.ds(2 * block * cols, 2 * cols)
-        return pltpu.make_async_copy(done.at[pixels], out.at[pixels], out_sems.at[block])
-
-    first_copy().start()
-    for pair in range(ahead):
-        for copy in pair_copy(pair):
-            copy.start()
-    tile = jnp.zeros((batch, channels), padded.dtype)
-    for row in range(rows + 2):
-        padded[row, 0] = tile
-        padded[row, cols + 1] = tile
-    for col in range(cols):
-        padded[0, col + 1] = tile
-        padded[rows + 1, col + 1] = tile
-
-    spread[...] = jnp.zeros_like(spread)
-    for tap in range(9):
-        value = weight[tap]
-        for row in range(2):
-            for col in range(2):
-                to = (row * 2 + col) * share
-                at = ((row + tap // 3) * 4 + col + tap % 3) * channels
-                spread[to : to + share, at : at + channels] = value
-    sums[...] = jnp.zeros_like(sums)
-    add_messages(own_turn[0], (east, west, across), sums, 0, share, batch, rows)
-
-    def add_block(block):
-        for start in range(0, cols, 4):
-            right = jnp.concatenate(
-                [
-                    jnp.concatenate(
-                        [
-                            padded[2 * block + row, start + half + col]
-                            for row in range(4)
-                            for col in range(4)
-                        ],
-                        axis=1,
-                    )
-                    for half in (0, 2)
-                ],
-                axis=0,
-            )
-            terms = dot(spread[...], right, TURNED)
-            for half in (0, 2):
-                for row in range(2):
-                    for col in range(2):
-                        part = terms[
-                            (row * 2 + col) * share : (row * 2 + col + 1) * share,
-                            half // 2 * batch : (half // 2 + 1) * batch,
-                        ]
-                        pixel = (2 * block + row) * cols + start + half + col
-                        done[pixel] = (sums[pixel] + part).astype(done.dtype)
-        block_out(block).start()
-
-    first_copy().wait()
-
-    @pl.loop(0, blocks - 1)
-    def _(block):
-        @pl.when(block + ahead < blocks - 1)
-        def _():
-            for copy in pair_copy(block + ahead):
-                copy.start()
-
-        @pl.when(block + ahead == blocks - 1)
-        def _():
-            last_copy().start()
-
-        for copy in pair_copy(block):
-            copy.wait()
-        add_block(block)
-
-    last_copy().wait()
-    add_block(blocks - 1)
-    for block in range(blocks):
-        block_out(block).wait()
-
-
-def convolved(turn, messages, source, weight, after):
-    pixels, batch, channels = source.shape
-    taps, share, _ = weight.shape
-    side = math.isqrt(pixels)
-    vmem = pl.BlockSpec(memory_space=pltpu.VMEM)
-    anywhere = pl.BlockSpec(memory_space=pl.ANY)
-    return pl.pallas_call(
-        conv_kernel,
-        in_specs=[pl.BlockSpec(memory_space=pltpu.SMEM)]
-        + [vmem] * 3
-        + [anywhere, vmem, anywhere],
-        out_specs=anywhere,
-        out_shape=jax.ShapeDtypeStruct((pixels, share, batch), jnp.bfloat16),
-        scratch_shapes=[
-            pltpu.VMEM((side + 2, side + 2, batch, channels), jnp.bfloat16),
-            pltpu.VMEM((4 * share, 16 * channels), jnp.bfloat16),
-            pltpu.VMEM((pixels, share, batch), jnp.float32),
-            pltpu.VMEM((pixels, share, batch), jnp.bfloat16),
-            pltpu.SemaphoreType.DMA((side,)),
-            pltpu.SemaphoreType.DMA((side // 2,)),
-        ],
-        compiler_params=pltpu.CompilerParams(vmem_limit_bytes=BIG),
-        cost_estimate=pl.CostEstimate(
-            flops=2400 * source.size, bytes_accessed=3 * source.size, transcendentals=0
-        ),
-        name="conv",
-    )(turn, *messages, source, weight, after)
+        name="grad_conv" if mirrored else "conv",
+    )(turn, *messages, source, *weights, *after)
 
 
 def sum_over_tiles(total, count):
@@ -687,14 +569,14 @@
         lax.ppermute(own, "chan", [(i, i ^ flip) for i in range(channels // share)])
         for flip in range(1, channels // share)
     ]
-    upstream, turned, *sends = lay_upstream(orientation, weights, grad_out[0])
+    upstream, *sends = lay_upstream(orientation, weights, grad_out[0])
     grad_messages = exchanged(sends)
-    field, edges, inner = lay_field(orientation, tiles[0], turned)
+    field, edges, inner = lay_field(orientation, tiles[0], upstream, share)
     scale = 1.0 / math.sqrt(count * batch * side * side)
     total, *sends = seam_filters(scale, edges, inner, own, grad_messages)
     conv_messages = exchanged(sends)
-    grad = grad_conv(orientation, grad_messages, upstream, weights)
-    conv = convolved(orientation, conv_messages, field, own, grad)
+    grad = convolved(True, orientation, grad_messages, upstream, weights)
+    conv = convolved(False, orientation, conv_messages, field, weights[:1], grad)
     total = sum_over_tiles(total, count)
     shape = (side, side, share, batch)
     conv_out = conv.reshape(shape).transpose(3, 0, 1, 2)[None]

time: 79.7 us -> 73.2 us (0.918)
  Pallas kernels: 52.2 us -> 45.4 us
    pallas_call x2, Pallas kernels: 27.1 us -> 19.3 us  [convolved(): pl.pallas_call(body, in_specs=[pl.BlockSpec(memory_space=pltpu.SMEM)] + [...]
  transfers between devices with their start and end apart: 13 -> 13, of which waited for: 3 -> 2; matrix products, arithmetic and copies ran while one was open for 0% -> 0% of each run, Pallas kernels for 48% -> 43%
where the time goes in v5:
time: 73.2 us; the launch traced here: 72.4 us
  Pallas kernels  45.4 us (62%)
  starting transfers between devices  18.9 us (26%)
  waiting for transfers between devices  3.72 us (5%)
  local copies, waits for them, and re-layouts  2.17 us (3%)
  between operations  1.45 us (2%)
    pallas_call x2, Pallas kernels, convolved(): pl.pallas_call(body, in_specs=[pl.BlockSpec(memory_space=pltpu.SMEM)] + [...  19.3 us
    pallas_call x1, Pallas kernels, lay_field(): pl.pallas_call(field_kernel, in_specs=[pl.BlockSpec(memory_space=pltpu.SM...  11.9 us
    pallas_call x1, Pallas kernels, lay_upstream(): pl.pallas_call(upstream_kernel, in_specs=[smem] + [vmem] * len(weights) +...  10.9 us
    ppermute x2, starting transfers between devices, exchanged(): lax.ppermute(sends[1], 'tile', westward)  7.69 us
    ppermute x4, starting transfers between devices, other(): return lax.ppermute(total, 'tile', [(i, i ^ flip) for i in range(count)])  6.01 us
    ppermute x3, waiting for transfers between devices, per_device(): lax.ppermute(own, 'chan', [(i, i ^ flip) for i in range(channels // share)])  3.69 us
    pallas_call x1, Pallas kernels, seam_filters(): pl.pallas_call(body, in_specs=[vmem] * 6, out_specs=[vmem] * 4, out_shape...  3.34 us
    ppermute x3, starting transfers between devices, per_device(): lax.ppermute(own, 'chan', [(i, i ^ flip) for i in range(channels // share)])  3.18 us
  transfers between devices with their start and end apart: 13, of which 2 were waited for; matrix products, arithmetic and copies ran while one was open for 0% of the time, Pallas kernels for 43%

profile of v5, /device:TPU:0, one launch (start us, length us, event | category | flops | bytes accessed | tf_op | source)
XLA Modules:
  0.0 72.4 jit_solution(10796764665218140567)
XLA Ops:
  0.6 0.5 collective-permute-start
  1.1 2.6 %collective-permute-start.1 = (bf16[9,32,128]{2,1,0:T(8,128)(2,1)}, bf16[9,32,128]{2,1,0:T(8,128)(2,1)S(1)}, u32[]{:S(2)}, u32[]{:S(2)}) collective-permute-start(bf16[9,32,128]{2,1,0:T(8,128)(2,1)} %bitcast.20), channel_id=1, source_target_pairs={{0,2},{1,3},{2,0},{3,1},{4,6},{5,7},{6,4},{7,5},{8,10},{9,11},{10,... | collective-permute-start | bytes 221192 | tf_op jit(solution)/shard_map/ppermute | solution.py:569
  3.7 0.1 collective-permute-start.2
  4.5 0.0 collective-permute-done.other1.refs_6_
  4.5 0.0 copy-start.7
  4.5 2.3 %collective-permute-done.1.other2.refs_7_ = bf16[9,32,128]{2,1,0:T(8,128)(2,1)S(1)} collective-permute-done((bf16[9,32,128]{2,1,0:T(8,128)(2,1)}, bf16[9,32,128]{2,1,0:T(8,128)(2,1)S(1)}, u32[]{:S(2)}, u32[]{:S(2)}) %collective-permute-start.1) | collective-permute-done | bytes 73760 | tf_op jit(solution)/shard_map/ppermute | solution.py:569
  6.8 0.0 copy-start.8
  6.8 1.4 %collective-permute-done.2.other3.refs_8_ = bf16[9,32,128]{2,1,0:T(8,128)(2,1)S(1)} collective-permute-done((bf16[9,32,128]{2,1,0:T(8,128)(2,1)}, bf16[9,32,128]{2,1,0:T(8,128)(2,1)S(1)}, u32[]{:S(2)}, u32[]{:S(2)}) %collective-permute-start.2) | collective-permute-done | bytes 73760 | tf_op jit(solution)/shard_map/ppermute | solution.py:569
  8.2 0.0 copy-done.7
  8.2 0.0 copy-done.8
  8.2 0.6 copy-done.9
  8.8 10.9 %lay_upstream.1 = (bf16[16,128,2048]{2,1,0:T(8,128)(2,1)}, bf16[64,2176]{1,0:T(8,128)(2,1)}, bf16[64,2176]{1,0:T(8,128)(2,1)}, bf16[64,2176]{1,0:T(8,128)(2,1)}) custom-call(s32[1]{0:T(128)S(6)} %copy.7.own_turn.refs_0_, bf16[9,32,128]{2,1,0:T(8,128)(2,1)} %bitcast.22, bf16[9,32,128]{2,1,0:T(8,128)(2,1)} %copy-done.7, bf16[9,32,128]{2,1,0:T(8,128)(2,1)} %copy-done.8, ...), custom_call_target="tpu_custom_call" | custom-call | flops 4294967296 | bytes 16777216 | tf_op jit(solution)/shard_map/lay_upstream/pallas_call | solution.py:196
  19.7 3.9 %collective-permute-start.3 = (bf16[64,2176]{1,0:T(8,128)(2,1)}, bf16[64,2176]{1,0:T(8,128)(2,1)S(1)}, u32[]{:S(2)}, u32[]{:S(2)}) collective-permute-start(bf16[64,2176]{1,0:T(8,128)(2,1)} %get-tuple-element.17), channel_id=1, source_target_pairs={{0,24},{4,28},{8,0},{12,4},{16,8},{20,12},{24,16},{28,20},{1,25},{... | collective-permute-start | bytes 835592 | tf_op jit(solution)/shard_map/ppermute | solution.py:562
  23.6 0.0 collective-permute-start.4
  23.6 1.5 %collective-permute-start.5 = (bf16[64,2176]{1,0:T(8,128)(2,1)}, bf16[64,2176]{1,0:T(8,128)(2,1)S(1)}, u32[]{:S(2)}, u32[]{:S(2)}) collective-permute-start(bf16[64,2176]{1,0:T(8,128)(2,1)} %get-tuple-element.19), channel_id=1, source_target_pairs={{0,4},{4,0},{8,12},{12,8},{16,20},{20,16},{24,28},{28,24},{1,5},{5... | collective-permute-start | bytes 835592 | tf_op jit(solution)/shard_map/ppermute | solution.py:564
  25.1 11.9 %lay_field.1 = (bf16[16,128,2048]{2,1,0:T(8,128)(2,1)}, bf16[3,16,128,128]{3,2,1,0:T(8,128)(2,1)}, f32[9,32,128]{2,1,0:T(8,128)}) custom-call(s32[1]{0:T(128)S(6)} %copy.7.own_turn.refs_0_, bf16[128,16,16,128]{3,2,1,0:T(8,128)(2,1)} %bitcast.27, bf16[16,128,2048]{2,1,0:T(8,128)(2,1)} %get-tuple-element.14.turned.refs_4_), custom_call_target="tpu_custom_call" | custom-call | flops 7549747200 | bytes 20971520 | tf_op jit(solution)/shard_map/lay_field/pallas_call | solution.py:317
  36.9 0.0 collective-permute-done.3.refs_3_.refs_1_
  36.9 0.0 copy-start
  37.0 0.0 collective-permute-done.4.refs_4_.refs_2_
  37.0 0.0 copy-start.1
  37.0 0.0 collective-permute-done.5.refs_5_.refs_3_
  37.0 0.0 copy-start.2
  37.0 0.7 copy-done
  37.7 0.1 copy-done.1
  37.8 0.1 copy-done.2
  37.9 3.3 %seam_filters.1 = (f32[9,32,128]{2,1,0:T(8,128)}, bf16[32,2048]{1,0:T(8,128)(2,1)}, bf16[32,2048]{1,0:T(8,128)(2,1)}, bf16[32,2048]{1,0:T(8,128)(2,1)}) custom-call(bf16[3,16,128,128]{3,2,1,0:T(8,128)(2,1)} %get-tuple-element.15.refs_0_, f32[9,32,128]{2,1,0:T(8,128)} %get-tuple-element.16.refs_1_, bf16[9,32,128]{2,1,0:T(8,128)(2,1)} %bitcast.23, ...), custom_call_target="tpu_custom_call" | custom-call | flops 301989888 | bytes 1572864 | tf_op jit(solution)/shard_map/seam_filters/pallas_call | solution.py:370
  41.2 3.8 %collective-permute-start.6 = (bf16[32,2048]{1,0:T(8,128)(2,1)}, bf16[32,2048]{1,0:T(8,128)(2,1)S(1)}, u32[]{:S(2)}, u32[]{:S(2)}) collective-permute-start(bf16[32,2048]{1,0:T(8,128)(2,1)} %get-tuple-element.20), channel_id=1, source_target_pairs={{0,24},{4,28},{8,0},{12,4},{16,8},{20,12},{24,16},{28,20},{1,25},{... | collective-permute-start | bytes 393224 | tf_op jit(solution)/shard_map/ppermute | solution.py:562
  45.0 0.0 collective-permute-start.7
  45.0 0.5 collective-permute-start.8
  45.6 1.5 %collective-permute-start.9 = (f32[9,32,128]{2,1,0:T(8,128)}, f32[9,32,128]{2,1,0:T(8,128)S(1)}, u32[]{:S(2)}, u32[]{:S(2)}) collective-permute-start(f32[9,32,128]{2,1,0:T(8,128)} %get-tuple-element.24), channel_id=1, source_target_pairs={{0,4},{4,0},{8,12},{12,8},{16,20},{20,16},{24,28},{28,24},{1,5},{5... | collective-permute-start | bytes 442376 | tf_op jit(solution)/shard_map/ppermute | solution.py:540
  47.1 10.0 %grad_conv.1.refs_6_ = bf16[256,32,128]{2,1,0:T(8,128)(2,1)} custom-call(s32[1]{0:T(128)S(6)} %copy.7.own_turn.refs_0_, bf16[64,2176]{1,0:T(8,128)(2,1)} %copy-done, bf16[64,2176]{1,0:T(8,128)(2,1)} %copy-done.1, bf16[64,2176]{1,0:T(8,128)(2,1)} %copy-done.2, bf16[16,128,2048]{2,1,0:T(8,128)(2,1)} %get-tuple-element.14.turned.refs_4_, ...), custom_call_target="tpu_custom_call" | custom-call | flops 10066329600 | bytes 12582912 | tf_op jit(solution)/shard_map/grad_conv/pallas_call | solution.py:508
  57.1 0.0 collective-permute-done.9
  57.1 0.0 copy-done.3
  57.1 0.6 collective-permute-start.11
  57.7 3.3 %collective-permute-start.12 = (f32[9,32,128]{2,1,0:T(8,128)S(1)}, f32[9,32,128]{2,1,0:T(8,128)S(1)}, u32[]{:S(2)}, u32[]{:S(2)}) collective-permute-start(f32[9,32,128]{2,1,0:T(8,128)S(1)} %add.12), channel_id=1, source_target_pairs={{0,24},{4,28},{8,16},{12,20},{16,8},{20,12},{24,0},{28,4},{1,25},{... | collective-permute-start | bytes 442376 | tf_op jit(solution)/shard_map/ppermute | solution.py:540
  61.1 0.0 collective-permute-done.6.refs_1_
  61.1 0.6 collective-permute-start.10
  61.6 0.0 collective-permute-done.7.refs_2_
  61.6 0.0 collective-permute-done.8.refs_3_
  61.6 0.0 copy-start.6
  61.7 0.1 copy-done.4
  61.7 0.6 copy-done.5
  62.3 0.0 copy-done.6
  62.3 9.3 %conv.1 = bf16[256,32,128]{2,1,0:T(8,128)(2,1)} custom-call(s32[1]{0:T(128)S(6)} %copy.7.own_turn.refs_0_, bf16[32,2048]{1,0:T(8,128)(2,1)} %copy-done.4, bf16[32,2048]{1,0:T(8,128)(2,1)} %copy-done.5, bf16[32,2048]{1,0:T(8,128)(2,1)} %copy-done.6, bf16[16,128,2048]{2,1,0:T(8,128)(2,1)} %get-tuple-element.23.refs_4_, bf16[9,32,128]{2,1,0:T(8,128)(2,1)} %bitcast.25, ...), custom_call_target="tpu_custom_call" | custom-call | flops 10066329600 | bytes 12582912 | tf_op jit(solution)/shard_map/conv/pallas_call | solution.py:508
  71.6 0.0 collective-permute-done.11
  71.6 0.0 collective-permute-done.12
  71.6 0.0 collective-permute-done.10
  71.7 0.7 add_add_fusion
  (5 shorter events, 0.0 us)
Async XLA Ops:
  0.6 3.8 %collective-permute-start = (bf16[9,32,128]{2,1,0:T(8,128)(2,1)}, bf16[9,32,128]{2,1,0:T(8,128)(2,1)S(1)}, u32[]{:S(2)}, u32[]{:S(2)}) collective-permute-start(bf16[9,32,128]{2,1,0:T(8,128)(2,1)} %bitcast.19), channel_id=1, source_target_pairs={{0,1},{1,0},{2,3},{3,2},{4,5},{5,4},{6,7},{7,6},{8,9},{9,8},{10,11... | collective-permute-start | bytes 221192 | tf_op jit(solution)/shard_map/ppermute | solution.py:569
  1.1 5.7 %collective-permute-start.1 = (bf16[9,32,128]{2,1,0:T(8,128)(2,1)}, bf16[9,32,128]{2,1,0:T(8,128)(2,1)S(1)}, u32[]{:S(2)}, u32[]{:S(2)}) collective-permute-start(bf16[9,32,128]{2,1,0:T(8,128)(2,1)} %bitcast.20), channel_id=1, source_target_pairs={{0,2},{1,3},{2,0},{3,1},{4,6},{5,7},{6,4},{7,5},{8,10},{9,11},{10,... | collective-permute-start | bytes 221192 | tf_op jit(solution)/shard_map/ppermute | solution.py:569
  3.7 4.4 %collective-permute-start.2 = (bf16[9,32,128]{2,1,0:T(8,128)(2,1)}, bf16[9,32,128]{2,1,0:T(8,128)(2,1)S(1)}, u32[]{:S(2)}, u32[]{:S(2)}) collective-permute-start(bf16[9,32,128]{2,1,0:T(8,128)(2,1)} %bitcast.21), channel_id=1, source_target_pairs={{0,3},{1,2},{2,1},{3,0},{4,7},{5,6},{6,5},{7,4},{8,11},{9,10},{10,... | collective-permute-start | bytes 221192 | tf_op jit(solution)/shard_map/ppermute | solution.py:569
  4.5 3.7 %copy-start.7 = (bf16[9,32,128]{2,1,0:T(8,128)(2,1)}, bf16[9,32,128]{2,1,0:T(8,128)(2,1)S(1)}, u32[]{:S(2)}) copy-start(bf16[9,32,128]{2,1,0:T(8,128)(2,1)S(1)} %collective-permute-done.other1.refs_6_) | copy-start | bytes 221188
  6.8 1.4 %copy-start.8 = (bf16[9,32,128]{2,1,0:T(8,128)(2,1)}, bf16[9,32,128]{2,1,0:T(8,128)(2,1)S(1)}, u32[]{:S(2)}) copy-start(bf16[9,32,128]{2,1,0:T(8,128)(2,1)S(1)} %collective-permute-done.1.other2.refs_7_) | copy-start | bytes 221188
  8.2 0.6 copy-start.9
  19.7 17.2 %collective-permute-start.3 = (bf16[64,2176]{1,0:T(8,128)(2,1)}, bf16[64,2176]{1,0:T(8,128)(2,1)S(1)}, u32[]{:S(2)}, u32[]{:S(2)}) collective-permute-start(bf16[64,2176]{1,0:T(8,128)(2,1)} %get-tuple-element.17), channel_id=1, source_target_pairs={{0,24},{4,28},{8,0},{12,4},{16,8},{20,12},{24,16},{28,20},{1,25},{... | collective-permute-start | bytes 835592 | tf_op jit(solution)/shard_map/ppermute | solution.py:562
  23.6 13.4 %collective-permute-start.4 = (bf16[64,2176]{1,0:T(8,128)(2,1)}, bf16[64,2176]{1,0:T(8,128)(2,1)S(1)}, u32[]{:S(2)}, u32[]{:S(2)}) collective-permute-start(bf16[64,2176]{1,0:T(8,128)(2,1)} %get-tuple-element.18), channel_id=1, source_target_pairs={{0,8},{4,12},{8,16},{12,20},{16,24},{20,28},{24,0},{28,4},{1,9},{5... | collective-permute-start | bytes 835592 | tf_op jit(solution)/shard_map/ppermute | solution.py:563
  23.6 13.4 %collective-permute-start.5 = (bf16[64,2176]{1,0:T(8,128)(2,1)}, bf16[64,2176]{1,0:T(8,128)(2,1)S(1)}, u32[]{:S(2)}, u32[]{:S(2)}) collective-permute-start(bf16[64,2176]{1,0:T(8,128)(2,1)} %get-tuple-element.19), channel_id=1, source_target_pairs={{0,4},{4,0},{8,12},{12,8},{16,20},{20,16},{24,28},{28,24},{1,5},{5... | collective-permute-start | bytes 835592 | tf_op jit(solution)/shard_map/ppermute | solution.py:564
  36.9 0.7 copy-start
  37.0 0.8 %copy-start.1 = (bf16[64,2176]{1,0:T(8,128)(2,1)}, bf16[64,2176]{1,0:T(8,128)(2,1)S(1)}, u32[]{:S(2)}) copy-start(bf16[64,2176]{1,0:T(8,128)(2,1)S(1)} %collective-permute-done.4.refs_4_.refs_2_) | copy-start | bytes 835588
  37.0 0.9 %copy-start.2 = (bf16[64,2176]{1,0:T(8,128)(2,1)}, bf16[64,2176]{1,0:T(8,128)(2,1)S(1)}, u32[]{:S(2)}) copy-start(bf16[64,2176]{1,0:T(8,128)(2,1)S(1)} %collective-permute-done.5.refs_5_.refs_3_) | copy-start | bytes 835588
  41.2 19.9 %collective-permute-start.6 = (bf16[32,2048]{1,0:T(8,128)(2,1)}, bf16[32,2048]{1,0:T(8,128)(2,1)S(1)}, u32[]{:S(2)}, u32[]{:S(2)}) collective-permute-start(bf16[32,2048]{1,0:T(8,128)(2,1)} %get-tuple-element.20), channel_id=1, source_target_pairs={{0,24},{4,28},{8,0},{12,4},{16,8},{20,12},{24,16},{28,20},{1,25},{... | collective-permute-start | bytes 393224 | tf_op jit(solution)/shard_map/ppermute | solution.py:562
  45.0 16.6 %collective-permute-start.7 = (bf16[32,2048]{1,0:T(8,128)(2,1)}, bf16[32,2048]{1,0:T(8,128)(2,1)S(1)}, u32[]{:S(2)}, u32[]{:S(2)}) collective-permute-start(bf16[32,2048]{1,0:T(8,128)(2,1)} %get-tuple-element.21), channel_id=1, source_target_pairs={{0,8},{4,12},{8,16},{12,20},{16,24},{20,28},{24,0},{28,4},{1,9},{5... | collective-permute-start | bytes 393224 | tf_op jit(solution)/shard_map/ppermute | solution.py:563
  45.0 16.6 %collective-permute-start.8 = (bf16[32,2048]{1,0:T(8,128)(2,1)}, bf16[32,2048]{1,0:T(8,128)(2,1)S(1)}, u32[]{:S(2)}, u32[]{:S(2)}) collective-permute-start(bf16[32,2048]{1,0:T(8,128)(2,1)} %get-tuple-element.22), channel_id=1, source_target_pairs={{0,4},{4,0},{8,12},{12,8},{16,20},{20,16},{24,28},{28,24},{1,5},{5... | collective-permute-start | bytes 393224 | tf_op jit(solution)/shard_map/ppermute | solution.py:564
  45.6 11.5 %copy-start.3 = (f32[9,32,128]{2,1,0:T(8,128)S(1)}, f32[9,32,128]{2,1,0:T(8,128)}, u32[]{:S(2)}) copy-start(f32[9,32,128]{2,1,0:T(8,128)} %get-tuple-element.24) | copy-start | bytes 442372
  45.6 11.5 %collective-permute-start.9 = (f32[9,32,128]{2,1,0:T(8,128)}, f32[9,32,128]{2,1,0:T(8,128)S(1)}, u32[]{:S(2)}, u32[]{:S(2)}) collective-permute-start(f32[9,32,128]{2,1,0:T(8,128)} %get-tuple-element.24), channel_id=1, source_target_pairs={{0,4},{4,0},{8,12},{12,8},{16,20},{20,16},{24,28},{28,24},{1,5},{5... | collective-permute-start | bytes 442376 | tf_op jit(solution)/shard_map/ppermute | solution.py:540
  57.1 14.5 %collective-permute-start.11 = (f32[9,32,128]{2,1,0:T(8,128)S(1)}, f32[9,32,128]{2,1,0:T(8,128)S(1)}, u32[]{:S(2)}, u32[]{:S(2)}) collective-permute-start(f32[9,32,128]{2,1,0:T(8,128)S(1)} %add.12), channel_id=1, source_target_pairs={{0,16},{4,20},{8,24},{12,28},{16,0},{20,4},{24,8},{28,12},{1,17},{... | collective-permute-start | bytes 442376 | tf_op jit(solution)/shard_map/ppermute | solution.py:540
  57.7 13.9 %collective-permute-start.12 = (f32[9,32,128]{2,1,0:T(8,128)S(1)}, f32[9,32,128]{2,1,0:T(8,128)S(1)}, u32[]{:S(2)}, u32[]{:S(2)}) collective-permute-start(f32[9,32,128]{2,1,0:T(8,128)S(1)} %add.12), channel_id=1, source_target_pairs={{0,24},{4,28},{8,16},{12,20},{16,8},{20,12},{24,0},{28,4},{1,25},{... | collective-permute-start | bytes 442376 | tf_op jit(solution)/shard_map/ppermute | solution.py:540
  61.1 0.7 copy-start.4
  61.1 10.6 %collective-permute-start.10 = (f32[9,32,128]{2,1,0:T(8,128)S(1)}, f32[9,32,128]{2,1,0:T(8,128)S(1)}, u32[]{:S(2)}, u32[]{:S(2)}) collective-permute-start(f32[9,32,128]{2,1,0:T(8,128)S(1)} %add.12), channel_id=1, source_target_pairs={{0,8},{4,12},{8,0},{12,4},{16,24},{20,28},{24,16},{28,20},{1,9},{5... | collective-permute-start | bytes 442376 | tf_op jit(solution)/shard_map/ppermute | solution.py:540
  61.6 0.6 copy-start.5
  61.6 0.7 copy-start.6

commit v6 on v5

--- a/solution.py
+++ b/solution.py
@@ -103,42 +103,29 @@
     )
 
 
-def edge_columns(turn, lower, edge, flat, side, batch):
-    first, step = edge_place(turn, lower, edge, side)
-    parts = []
-    for pos in range(side):
-        pixel = first + pos * step
-        col = pl.multiple_of(lax.rem(pixel, side) * batch, batch)
-        parts.append(flat[lax.div(pixel, side), :, pl.ds(col, batch)])
-    return jnp.concatenate(parts, axis=1)
-
-
 def turned_out(flat, turned, sems, pair):
     part = pl.ds(2 * pair, 2)
     return pltpu.make_async_copy(flat.at[part], turned.at[part], sems.at[pair])
 
 
+def lay_pair(stage, held, flat, pair):
+    _, batch, rows, side, _ = stage.shape
+    for row in range(rows):
+        block = jnp.swapaxes(stage[pair, :, row], 0, 1)
+        if held is not None:
+            held[pl.ds((2 * pair + row) * side, side)] = block
+        for col in range(side):
+            flat[2 * pair + row, :, col * batch : (col + 1) * batch] = block[col].T
+
+
 def upstream_kernel(
-    own_turn, weight, other1, other2, other3, upstream,
-    turned, east, west, across,
-    stage, held, flat, whole, rowed, shuffle, same, in_sems, turned_sems,
+    own_turn, upstream, turned, edges, east, west, across,
+    stage, flat, in_sems, turned_sems, edge_sems,
 ):
     pairs, batch, rows, side, channels = stage.shape
-    taps, share, _ = weight.shape
-    group = 256 // side
+    share = east.shape[0]
     for pair in range(AHEAD):
         pair_in(upstream, stage, in_sems, pair).start()
-    to = lax.broadcasted_iota(jnp.int32, (256, 256), 0)
-    come = lax.broadcasted_iota(jnp.int32, (256, 256), 1)
-    moves = (to // group == come % side) & (to % group == come // side)
-    shuffle[...] = jnp.where(moves, 1.0, 0.0).astype(jnp.bfloat16)
-    to = lax.broadcasted_iota(jnp.int32, (channels, channels), 0)
-    come = lax.broadcasted_iota(jnp.int32, (channels, channels), 1)
-    same[...] = jnp.where(to == come, 1.0, 0.0).astype(jnp.bfloat16)
-    pick = one_hot(share, channels)
-    gather_filters((weight, other1, other2, other3), whole)
-    for tap in range(taps):
-        rowed[tap] = dot(pick, whole[tap], TURNED).astype(jnp.bfloat16)
 
     @pl.loop(0, pairs)
     def _(pair):
@@ -147,79 +134,63 @@
             pair_in(upstream, stage, in_sems, pair + AHEAD).start()
 
         pair_in(upstream, stage, in_sems, pair).wait()
-        for start in range(0, batch, group):
-            block = jnp.concatenate(
-                [
-                    stage[pair, start : start + group, row].reshape(256, channels)
-                    for row in range(rows)
-                ],
-                axis=1,
-            )
-            moved = dot(shuffle[...], block, FLAT).astype(jnp.bfloat16)
-            for row in range(rows):
-                held[row * side : (row + 1) * side, start : start + group] = moved[
-                    :, row * channels : (row + 1) * channels
-                ].reshape(side, group, channels)
-        for row in range(rows):
-            flat[2 * pair + row] = dot(
-                same[...],
-                held[row * side : (row + 1) * side].reshape(side * batch, channels),
-                TURNED,
-            ).astype(jnp.bfloat16)
+        lay_pair(stage, None, flat, pair)
         turned_out(flat, turned, turned_sems, pair).start()
 
+    chan = lax.axis_index("chan").astype(jnp.int32)
+    own = pl.ds(pl.multiple_of(chan * share, share), share)
     lower = half_of_band()
     turn = own_turn[0]
     for edge, out in enumerate((east, west, across)):
-        filters = jnp.concatenate(
-            [rowed[edge_tap(turn, lower, edge, 2 - d, True)] for d in range(3)] + [pick],
-            axis=0,
-        )
-        product = dot(filters, edge_columns(turn, lower, edge, flat, side, batch), FLAT)
-        out[0:share, 0 : side * batch] = terms_of(product, share, batch)
-        out[share:, 0 : side * batch] = product[3 * share :].astype(jnp.bfloat16)
-        code = jnp.full((2 * share, EXTRA), turn, jnp.int32)
+        first, step = edge_place(turn, lower, edge, side)
+        for pos in range(side):
+            pixel = first + pos * step
+            row = lax.div(pixel, side)
+            col = pl.ds(pl.multiple_of(lax.rem(pixel, side) * batch, batch), batch)
+            lanes = pl.ds(pos * batch, batch)
+            pltpu.make_async_copy(
+                flat.at[row, :, col], edges.at[edge, :, lanes], edge_sems.at[edge]
+            ).start()
+            out[:, lanes] = flat[row, own, col]
+        code = jnp.full((share, EXTRA), turn, jnp.int32)
         out[:, side * batch :] = code.astype(jnp.float32).astype(jnp.bfloat16)
     for pair in range(pairs):
         turned_out(flat, turned, turned_sems, pair).wait()
-
-
-def lay_upstream(turn, weights, upstream):
+    for edge in range(3):
+        pltpu.make_async_copy(flat.at[0], edges.at[edge], edge_sems.at[edge]).wait()
+
+
+def lay_upstream(turn, upstream, share):
     batch, side, _, channels = upstream.shape
-    taps, share, _ = weights[0].shape
-    smem = pl.BlockSpec(memory_space=pltpu.SMEM)
     vmem = pl.BlockSpec(memory_space=pltpu.VMEM)
     anywhere = pl.BlockSpec(memory_space=pl.ANY)
     pairs = side // 2
     turned = jax.ShapeDtypeStruct((side, channels, side * batch), jnp.bfloat16)
-    message = jax.ShapeDtypeStruct((2 * share, side * batch + EXTRA), jnp.bfloat16)
+    edges = jax.ShapeDtypeStruct((3, channels, side * batch), jnp.bfloat16)
+    message = jax.ShapeDtypeStruct((share, side * batch + EXTRA), jnp.bfloat16)
     return pl.pallas_call(
         upstream_kernel,
-        in_specs=[smem] + [vmem] * len(weights) + [anywhere],
-        out_specs=[anywhere] + [vmem] * 3,
-        out_shape=[turned] + [message] * 3,
+        in_specs=[pl.BlockSpec(memory_space=pltpu.SMEM), anywhere],
+        out_specs=[anywhere] * 2 + [vmem] * 3,
+        out_shape=[turned, edges] + [message] * 3,
         scratch_shapes=[
             pltpu.VMEM((pairs, batch, 2, side, channels), jnp.bfloat16),
-            pltpu.VMEM((2 * side, batch, channels), jnp.bfloat16),
             pltpu.VMEM(turned.shape, jnp.bfloat16),
-            pltpu.VMEM((taps, channels, channels), jnp.bfloat16),
-            pltpu.VMEM((taps, share, channels), jnp.bfloat16),
-            pltpu.VMEM((256, 256), jnp.bfloat16),
-            pltpu.VMEM((channels, channels), jnp.bfloat16),
             pltpu.SemaphoreType.DMA((pairs,)),
             pltpu.SemaphoreType.DMA((pairs,)),
+            pltpu.SemaphoreType.DMA((3,)),
         ],
         compiler_params=pltpu.CompilerParams(vmem_limit_bytes=BIG),
         cost_estimate=pl.CostEstimate(
             flops=1024 * upstream.size, bytes_accessed=4 * upstream.size, transcendentals=0
         ),
         name="lay_upstream",
-    )(turn, *weights, upstream)
+    )(turn, upstream)
 
 
 def field_kernel(
-    own_turn, field, turned, laid, edges, inner,
-    stage, held, flat, padded, total, in_sems, out_sems, turned_sem, edge_sems,
+    own_turn, weight, other1, other2, other3, field, turned, laid, edges, inner, rowed,
+    stage, held, flat, padded, total, whole, in_sems, out_sems, turned_sem, edge_sems,
 ):
     pairs, batch, rows, side, channels = stage.shape
     share = padded.shape[1]
@@ -242,11 +213,7 @@
 
     def lay(pair):
         pair_in(field, stage, in_sems, pair).wait()
-        for row in range(rows):
-            block = jnp.swapaxes(stage[pair, :, row], 0, 1)
-            held[pl.ds((2 * pair + row) * side, side)] = block
-            for col in range(side):
-                flat[2 * pair + row, :, col * batch : (col + 1) * batch] = block[col].T
+        lay_pair(stage, held, flat, pair)
         turned_out(flat, laid, out_sems, pair).start()
 
     def add_filters(pair):
@@ -271,6 +238,10 @@
                 left = jnp.concatenate(parts[3 * half : 3 * half + 3], axis=0)
                 total[6 * share * half : 6 * share * (half + 1)] += dot(left, right, FLAT)
 
+    gather_filters((weight, other1, other2, other3), whole)
+    pick = one_hot(share, channels)
+    for tap in range(9):
+        rowed[tap] = dot(pick, whole[tap], TURNED).astype(jnp.bfloat16)
     lay(0)
     turned_in.wait()
 
@@ -307,7 +278,9 @@
         ).wait()
 
 
-def lay_field(turn, field, turned, share):
+def lay_field(turn, weights, field, turned):
+    share = weights[0].shape[1]
+    vmem = pl.BlockSpec(memory_space=pltpu.VMEM)
     batch, side, _, channels = field.shape
     anywhere = pl.BlockSpec(memory_space=pl.ANY)
     pairs = side // 2
@@ -316,15 +289,18 @@
     inner = jax.ShapeDtypeStruct((9, share, channels), jnp.float32)
     return pl.pallas_call(
         field_kernel,
-        in_specs=[pl.BlockSpec(memory_space=pltpu.SMEM)] + [anywhere] * 2,
-        out_specs=[anywhere] * 2 + [pl.BlockSpec(memory_space=pltpu.VMEM)],
-        out_shape=[laid, edges, inner],
+        in_specs=[pl.BlockSpec(memory_space=pltpu.SMEM)]
+        + [vmem] * len(weights)
+        + [anywhere] * 2,
+        out_specs=[anywhere] * 2 + [vmem] * 2,
+        out_shape=[laid, edges, inner, jax.ShapeDtypeStruct(inner.shape, jnp.bfloat16)],
         scratch_shapes=[
             pltpu.VMEM((pairs, batch, 2, side, channels), jnp.bfloat16),
             pltpu.VMEM((side * side, batch, channels), jnp.bfloat16),
             pltpu.VMEM(laid.shape, jnp.bfloat16),
             pltpu.VMEM((side + 2, share, (side + 2) * batch), jnp.bfloat16),
             pltpu.VMEM((12 * share, 2 * channels), jnp.float32),
+            pltpu.VMEM((9, channels, channels), jnp.bfloat16),
             pltpu.SemaphoreType.DMA((pairs,)),
             pltpu.SemaphoreType.DMA((pairs,)),
             pltpu.SemaphoreType.DMA,
@@ -335,10 +311,10 @@
             flops=1800 * field.size, bytes_accessed=5 * field.size, transcendentals=0
         ),
         name="lay_field",
-    )(turn, field, turned)
-
-
-def seam_kernel(scale, edges, inner, weight, *refs):
+    )(turn, *weights, field, turned)
+
+
+def seam_kernel(scale, own_turn, edges, upstream_edges, inner, weight, rowed, *refs):
     messages, out, terms_out = refs[:3], refs[3], refs[4:7]
     side, batch, channels = edges.shape[1:]
     share = out.shape[1]
@@ -348,18 +324,24 @@
     for edge, message in enumerate(messages):
         turn = jnp.max(message[0:16, width:].astype(jnp.float32)).astype(jnp.int32)
         taps = [edge_tap(turn, lower, edge, d, False) for d in range(3)]
-        turned = message[share:, 0:width]
+        turned = message[:, 0:width]
         left = jnp.concatenate([earlier(turned, batch), turned, later(turned, batch)], axis=0)
         pixels = edges[edge].reshape(width, channels)
         terms = dot(left, pixels, FLAT)
         for d in range(3):
             out[taps[d]] += terms[d * share : (d + 1) * share]
         filters = jnp.concatenate([weight[tap] for tap in taps], axis=0)
-        terms_out[edge][...] = terms_of(dot(filters, pixels, TURNED), share, batch)
+        terms_out[edge][0:share] = terms_of(dot(filters, pixels, TURNED), share, batch)
+        filters = jnp.concatenate(
+            [rowed[edge_tap(own_turn[0], lower, edge, 2 - d, True)] for d in range(3)], axis=0
+        )
+        terms_out[edge][share:] = terms_of(
+            dot(filters, upstream_edges[edge], FLAT), share, batch
+        )
     out[...] = out[...] * scale
 
 
-def seam_filters(scale, edges, inner, weight, messages):
+def seam_filters(scale, turn, edges, upstream_edges, inner, weight, rowed, messages):
     _, side, batch, channels = edges.shape
     share = inner.shape[1]
     vmem = pl.BlockSpec(memory_space=pltpu.VMEM)
@@ -369,33 +351,53 @@
 
     return pl.pallas_call(
         body,
-        in_specs=[vmem] * 6,
+        in_specs=[pl.BlockSpec(memory_space=pltpu.SMEM)] + [vmem] * 8,
         out_specs=[vmem] * 4,
         out_shape=[jax.ShapeDtypeStruct(inner.shape, jnp.float32)]
-        + [jax.ShapeDtypeStruct((share, side * batch), jnp.bfloat16)] * 3,
+        + [jax.ShapeDtypeStruct((2 * share, side * batch), jnp.bfloat16)] * 3,
         compiler_params=pltpu.CompilerParams(vmem_limit_bytes=BIG),
         cost_estimate=pl.CostEstimate(
-            flops=36 * share * side * batch * channels,
-            bytes_accessed=6 * side * batch * channels,
+            flops=54 * share * side * batch * channels,
+            bytes_accessed=12 * side * batch * channels,
             transcendentals=0,
         ),
         name="seam_filters",
-    )(edges, inner, weight, *messages)
-
-
-def add_messages(turn, messages, sums, offset, share, batch, side):
-    lower = half_of_band()
-    for edge, message in enumerate(messages):
-        first, step = edge_place(turn, lower, edge, side)
-        for pos in range(side):
-            sums[first + pos * step + offset] += message[
-                0:share, pos * batch : (pos + 1) * batch
-            ].astype(jnp.float32)
-
-
-def conv_kernel(mirrored, own_turn, east, west, across, source, *refs):
-    out, padded, spread, sums, done, whole, sems, out_sems = refs[-8:]
-    weights = refs[:-8]
+    )(turn, edges, upstream_edges, inner, weight, rowed, *messages)
+
+
+def border_rows(cols, rows, source, target, sems):
+    copies = []
+    for index, row in enumerate((0, rows - 1)):
+        where = pl.ds(row * cols, cols)
+        copies.append(
+            pltpu.make_async_copy(source.at[where], target.at[where], sems.at[index])
+        )
+    return copies
+
+
+def start_border(cols, rows, source, target, sems):
+    for copy in border_rows(cols, rows, source, target, sems):
+        copy.start()
+    for row in range(1, rows - 1):
+        for col in (0, cols - 1):
+            where = pl.ds(row * cols + col, 1)
+            pltpu.make_async_copy(source.at[where], target.at[where], sems.at[2]).start()
+
+
+def wait_border(cols, rows, source, target, sems):
+    for copy in border_rows(cols, rows, source, target, sems):
+        copy.wait()
+    between = pl.ds(cols, 2 * (rows - 2))
+    pltpu.make_async_copy(source.at[between], target.at[between], sems.at[2]).wait()
+
+
+def conv_kernel(last, *refs):
+    if last:
+        own_turn, east, west, across, source, weight, other_in = refs[:7]
+        out, other_out, padded, spread, sums, done, sems, out_sems = refs[7:15]
+        other, other_sems, back_sems = refs[15:]
+    else:
+        source, weight, out, padded, spread, sums, done, sems, out_sems = refs
     side, channels, lanes = padded.shape
     share, batch = done.shape[1:]
     cols = lanes // batch - 2
@@ -417,12 +419,7 @@
         padded[row, :, 0:batch] = tile
         padded[row, :, lanes - batch :] = tile
 
-    if mirrored:
-        gather_filters(weights, whole)
-        pick = one_hot(share, channels)
-        blocks = [dot(pick, whole[8 - tap], TURNED).astype(jnp.bfloat16) for tap in range(9)]
-    else:
-        blocks = [weights[0][tap] for tap in range(9)]
+    blocks = [weight[tap if last else 8 - tap] for tap in range(9)]
     empty = jnp.zeros((share, channels), spread.dtype)
     for row in range(3):
         for out_col in range(2):
@@ -434,7 +431,21 @@
                     blocks[row * 3 + tap] if 0 <= tap <= 2 else empty
                 )
     sums[...] = jnp.zeros_like(sums)
-    add_messages(own_turn[0], (east, west, across), sums, cols, share, batch, side)
+    if last:
+        start_border(cols, side, other_in, other, other_sems)
+        lower = half_of_band()
+        wait_border(cols, side, other_in, other, other_sems)
+        for edge, message in enumerate((east, west, across)):
+            first, step = edge_place(own_turn[0], lower, edge, side)
+            for pos in range(side):
+                pixel = first + pos * step
+                place = slice(pos * batch, (pos + 1) * batch)
+                sums[pixel + cols] += message[0:share, place].astype(jnp.float32)
+                other[pixel] = (
+                    other[pixel].astype(jnp.float32)
+                    + message[share:, place].astype(jnp.float32)
+                ).astype(other.dtype)
+        start_border(cols, side, other, other_out, back_sems)
 
     def add_row(row):
         for start in range(0, cols, 4):
@@ -492,43 +503,52 @@
     row_out(side - 1).start()
     for row in range(side):
         row_out(row).wait()
-
-
-def convolved(mirrored, turn, messages, source, weights, *after):
+    if last:
+        wait_border(cols, side, other, other_out, back_sems)
+
+
+def convolved(source, weight, turn=None, messages=(), other=None):
     side, channels, width = source.shape
-    taps, share, _ = weights[0].shape
+    share = weight.shape[1]
     batch = width // side
     pixels = side * side
+    last = other is not None
     vmem = pl.BlockSpec(memory_space=pltpu.VMEM)
+    smem = pl.BlockSpec(memory_space=pltpu.SMEM)
     anywhere = pl.BlockSpec(memory_space=pl.ANY)
+    shape = jax.ShapeDtypeStruct((pixels, share, batch), jnp.bfloat16)
+    scratch = [
+        pltpu.VMEM((side, channels, width + 2 * batch), jnp.bfloat16),
+        pltpu.VMEM((6 * share, 4 * channels), jnp.bfloat16),
+        pltpu.VMEM((pixels + 2 * side, share, batch), jnp.float32),
+        pltpu.VMEM((pixels, share, batch), jnp.bfloat16),
+        pltpu.SemaphoreType.DMA((side,)),
+        pltpu.SemaphoreType.DMA((side,)),
+    ]
+    if last:
+        scratch += [
+            pltpu.VMEM((pixels, share, batch), jnp.bfloat16),
+            pltpu.SemaphoreType.DMA((3,)),
+            pltpu.SemaphoreType.DMA((3,)),
+        ]
 
     def body(*refs):
-        conv_kernel(mirrored, *refs)
-
-    return pl.pallas_call(
+        conv_kernel(last, *refs)
+
+    call = pl.pallas_call(
         body,
-        in_specs=[pl.BlockSpec(memory_space=pltpu.SMEM)]
-        + [vmem] * 3
-        + [anywhere]
-        + [vmem] * len(weights)
-        + [anywhere] * len(after),
-        out_specs=anywhere,
-        out_shape=jax.ShapeDtypeStruct((pixels, share, batch), jnp.bfloat16),
-        scratch_shapes=[
-            pltpu.VMEM((side, channels, width + 2 * batch), jnp.bfloat16),
-            pltpu.VMEM((6 * share, 4 * channels), jnp.bfloat16),
-            pltpu.VMEM((pixels + 2 * side, share, batch), jnp.float32),
-            pltpu.VMEM((pixels, share, batch), jnp.bfloat16),
-            pltpu.VMEM((taps, channels, channels), jnp.bfloat16),
-            pltpu.SemaphoreType.DMA((side,)),
-            pltpu.SemaphoreType.DMA((side,)),
-        ],
+        in_specs=[smem] + [vmem] * 3 + [anywhere, vmem, anywhere] if last else [anywhere, vmem],
+        out_specs=[anywhere] * 2 if last else anywhere,
+        out_shape=[shape] * 2 if last else shape,
+        scratch_shapes=scratch,
+        input_output_aliases={6: 1} if last else {},
         compiler_params=pltpu.CompilerParams(vmem_limit_bytes=BIG),
         cost_estimate=pl.CostEstimate(
             flops=2400 * source.size, bytes_accessed=3 * source.size, transcendentals=0
         ),
-        name="grad_conv" if mirrored else "conv",
-    )(turn, *messages, source, *weights, *after)
+        name="conv" if last else "grad_conv",
+    )
+    return call(turn, *messages, source, weight, other) if last else call(source, weight)
 
 
 def sum_over_tiles(total, count):
@@ -569,14 +589,16 @@
         lax.ppermute(own, "chan", [(i, i ^ flip) for i in range(channels // share)])
         for flip in range(1, channels // share)
     ]
-    upstream, *sends = lay_upstream(orientation, weights, grad_out[0])
-    grad_messages = exchanged(sends)
-    field, edges, inner = lay_field(orientation, tiles[0], upstream, share)
+    upstream, upstream_edges, *sends = lay_upstream(orientation, grad_out[0], share)
+    messages = exchanged(sends)
+    field, edges, inner, rowed = lay_field(orientation, weights, tiles[0], upstream)
     scale = 1.0 / math.sqrt(count * batch * side * side)
-    total, *sends = seam_filters(scale, edges, inner, own, grad_messages)
-    conv_messages = exchanged(sends)
-    grad = convolved(True, orientation, grad_messages, upstream, weights)
-    conv = convolved(False, orientation, conv_messages, field, weights[:1], grad)
+    total, *sends = seam_filters(
+        scale, orientation, edges, upstream_edges, inner, own, rowed, messages
+    )
+    messages = exchanged(sends)
+    grad = convolved(upstream, rowed)
+    conv, grad = convolved(field, own, orientation, messages, grad)
     total = sum_over_tiles(total, count)
     shape = (side, side, share, batch)
     conv_out = conv.reshape(shape).transpose(3, 0, 1, 2)[None]

time: 73.2 us -> 70.2 us (0.959)
  waiting for transfers between devices: 3.72 us -> 0.03 us
    ppermute x3, waiting for transfers between devices: 3.69 us -> 0.01 us  [per_device(): lax.ppermute(own, 'chan', [(i, i ^ flip) for i in range(channels // share)])]
    ppermute x2, starting transfers between devices: 2.03 us -> 3.06 us  [exchanged(): lax.ppermute(sends[2], 'tile', acrossward)]
    ppermute x4, starting transfers between devices: 6.01 us -> 4.99 us  [other(): return lax.ppermute(total, 'tile', [(i, i ^ flip) for i in range(count)])]
    pallas_call x1, Pallas kernels: 11.9 us -> 12.9 us  [lay_field(): pl.pallas_call(field_kernel, in_specs=[pl.BlockSpec(memory_space=pltpu.SM...]
  transfers between devices with their start and end apart: 13 -> 13, of which waited for: 2 -> 0; matrix products, arithmetic and copies ran while one was open for 0% -> 0% of each run, Pallas kernels for 43% -> 61%
where the time goes in v6:
time: 70.2 us; the launch traced here: 69.4 us
  Pallas kernels  46 us (66%)
  starting transfers between devices  18.8 us (27%)
  local copies, waits for them, and re-layouts  2.31 us (3%)
  between operations  1.49 us (2%)
  other arithmetic  0.73 us (1%)
    pallas_call x1, Pallas kernels, lay_field(): pl.pallas_call(field_kernel, in_specs=[pl.BlockSpec(memory_space=pltpu.SM...  12.9 us
    pallas_call x1, Pallas kernels, convolved(): call(turn, *messages, source, weight, other)  10.2 us
    pallas_call x1, Pallas kernels, lay_upstream(): pl.pallas_call(upstream_kernel, in_specs=[pl.BlockSpec(memory_space=pltpu...  9.78 us
    pallas_call x1, Pallas kernels, convolved(): call(source, weight)  9.09 us
    ppermute x2, starting transfers between devices, exchanged(): lax.ppermute(sends[1], 'tile', westward)  7.6 us
    ppermute x4, starting transfers between devices, other(): return lax.ppermute(total, 'tile', [(i, i ^ flip) for i in range(count)])  4.99 us
    pallas_call x1, Pallas kernels, seam_filters(): pl.pallas_call(body, in_specs=[pl.BlockSpec(memory_space=pltpu.SMEM)] + [...  4.05 us
    ppermute x3, starting transfers between devices, per_device(): lax.ppermute(own, 'chan', [(i, i ^ flip) for i in range(channels // share)])  3.18 us
  transfers between devices with their start and end apart: 13, of which 0 were waited for; matrix products, arithmetic and copies ran while one was open for 0% of the time, Pallas kernels for 61%

profile of v6, /device:TPU:0, one launch (start us, length us, event | category | flops | bytes accessed | tf_op | source)
XLA Modules:
  0.0 69.4 jit_solution(12177482004527157220)
XLA Ops:
  0.6 0.5 collective-permute-start
  1.1 2.6 %collective-permute-start.1 = (bf16[9,32,128]{2,1,0:T(8,128)(2,1)}, bf16[9,32,128]{2,1,0:T(8,128)(2,1)S(1)}, u32[]{:S(2)}, u32[]{:S(2)}) collective-permute-start(bf16[9,32,128]{2,1,0:T(8,128)(2,1)} %bitcast.20), channel_id=1, source_target_pairs={{0,2},{1,3},{2,0},{3,1},{4,6},{5,7},{6,4},{7,5},{8,10},{9,11},{10,... | collective-permute-start | bytes 221192 | tf_op jit(solution)/shard_map/ppermute | solution.py:589
  3.7 0.1 collective-permute-start.2
  4.5 9.8 %lay_upstream.1 = (bf16[16,128,2048]{2,1,0:T(8,128)(2,1)}, bf16[3,128,2048]{2,1,0:T(8,128)(2,1)}, bf16[32,2176]{1,0:T(8,128)(2,1)}, bf16[32,2176]{1,0:T(8,128)(2,1)}, bf16[32,2176]{1,0:T(8,128)(2,1)}) custom-call(s32[1]{0:T(128)S(6)} %copy.9.own_turn.refs_0_, bf16[128,16,16,128]{3,2,1,0:T(8,128)(2,1)} %bitcast.25), custom_call_target="tpu_custom_call" | custom-call | flops 4294967296 | bytes 16777216 | tf_op jit(solution)/shard_map/lay_upstream/pallas_call | solution.py:171
  14.3 3.9 %collective-permute-start.3 = (bf16[32,2176]{1,0:T(8,128)(2,1)}, bf16[32,2176]{1,0:T(8,128)(2,1)S(1)}, u32[]{:S(2)}, u32[]{:S(2)}) collective-permute-start(bf16[32,2176]{1,0:T(8,128)(2,1)} %get-tuple-element.23), channel_id=1, source_target_pairs={{0,24},{4,28},{8,0},{12,4},{16,8},{20,12},{24,16},{28,20},{1,25},{... | collective-permute-start | bytes 417800 | tf_op jit(solution)/shard_map/ppermute | solution.py:582
  18.1 0.0 collective-permute-start.4
  18.1 0.0 collective-permute-done.other1
  18.1 1.6 %collective-permute-start.5 = (bf16[32,2176]{1,0:T(8,128)(2,1)}, bf16[32,2176]{1,0:T(8,128)(2,1)S(1)}, u32[]{:S(2)}, u32[]{:S(2)}) collective-permute-start(bf16[32,2176]{1,0:T(8,128)(2,1)} %get-tuple-element.25), channel_id=1, source_target_pairs={{0,4},{4,0},{8,12},{12,8},{16,20},{20,16},{24,28},{28,24},{1,5},{5... | collective-permute-start | bytes 417800 | tf_op jit(solution)/shard_map/ppermute | solution.py:584
  19.7 0.0 collective-permute-done.1.other2
  19.7 0.0 collective-permute-done.2.other3
  19.7 0.0 copy-start.9
  19.7 0.0 copy-done.7
  19.7 0.6 copy-done.8
  20.3 0.0 copy-done.9
  20.3 12.9 %lay_field.1 = (bf16[16,128,2048]{2,1,0:T(8,128)(2,1)}, bf16[3,16,128,128]{3,2,1,0:T(8,128)(2,1)}, f32[9,32,128]{2,1,0:T(8,128)}, bf16[9,32,128]{2,1,0:T(8,128)(2,1)}) custom-call(s32[1]{0:T(128)S(6)} %copy.9.own_turn.refs_0_, bf16[9,32,128]{2,1,0:T(8,128)(2,1)} %bitcast.22, bf16[9,32,128]{2,1,0:T(8,128)(2,1)} %copy-done.7, bf16[9,32,128]{2,1,0:T(8,128)(2,1)} %copy-done.8, ...), custom_call_target="tpu_custom_call" | custom-call | flops 7549747200 | bytes 20971520 | tf_op jit(solution)/shard_map/lay_field/pallas_call | solution.py:290
  33.2 0.0 collective-permute-done.3.refs_6_
  33.2 0.0 copy-start.1
  33.3 0.0 collective-permute-done.4.refs_7_
  33.3 0.0 copy-start.2
  33.3 0.0 collective-permute-done.5.refs_8_
  33.3 0.0 copy-start.3
  33.3 0.6 copy-done.1
  33.9 0.1 copy-done.2
  34.0 0.0 copy-done.3
  34.0 4.0 %seam_filters.1 = (f32[9,32,128]{2,1,0:T(8,128)}, bf16[64,2048]{1,0:T(8,128)(2,1)}, bf16[64,2048]{1,0:T(8,128)(2,1)}, bf16[64,2048]{1,0:T(8,128)(2,1)}) custom-call(s32[1]{0:T(128)S(6)} %copy.9.own_turn.refs_0_, bf16[3,16,128,128]{3,2,1,0:T(8,128)(2,1)} %get-tuple-element.19.refs_1_, bf16[3,128,2048]{2,1,0:T(8,128)(2,1)} %get-tuple-element.20.refs_2_, ...), custom_call_target="tpu_custom_call" | custom-call | flops 452984832 | bytes 3145728 | tf_op jit(solution)/shard_map/seam_filters/pallas_call | solution.py:352
  38.1 0.5 collective-permute-start.9
  38.6 3.7 %collective-permute-start.6 = (bf16[64,2048]{1,0:T(8,128)(2,1)}, bf16[64,2048]{1,0:T(8,128)(2,1)S(1)}, u32[]{:S(2)}, u32[]{:S(2)}) collective-permute-start(bf16[64,2048]{1,0:T(8,128)(2,1)} %get-tuple-element.26), channel_id=1, source_target_pairs={{0,24},{4,28},{8,0},{12,4},{16,8},{20,12},{24,16},{28,20},{1,25},{... | collective-permute-start | bytes 786440 | tf_op jit(solution)/shard_map/ppermute | solution.py:582
  42.3 0.0 collective-permute-start.7
  42.3 1.5 %collective-permute-start.8 = (bf16[64,2048]{1,0:T(8,128)(2,1)}, bf16[64,2048]{1,0:T(8,128)(2,1)S(1)}, u32[]{:S(2)}, u32[]{:S(2)}) collective-permute-start(bf16[64,2048]{1,0:T(8,128)(2,1)} %get-tuple-element.28), channel_id=1, source_target_pairs={{0,4},{4,0},{8,12},{12,8},{16,20},{20,16},{24,28},{28,24},{1,5},{5... | collective-permute-start | bytes 786440 | tf_op jit(solution)/shard_map/ppermute | solution.py:584
  43.8 9.1 %grad_conv.1.refs_6_ = bf16[256,32,128]{2,1,0:T(8,128)(2,1)} custom-call(bf16[16,128,2048]{2,1,0:T(8,128)(2,1)} %get-tuple-element.18.turned.refs_0_, bf16[9,32,128]{2,1,0:T(8,128)(2,1)} %get-tuple-element.22.refs_5_.refs_1_), custom_call_target="tpu_custom_call" | custom-call | flops 10066329600 | bytes 12582912 | tf_op jit(solution)/shard_map/grad_conv/pallas_call | solution.py:551
  53.0 0.0 collective-permute-done.9
  53.0 0.0 copy-done
  53.0 0.1 collective-permute-start.10
  53.1 4.4 %collective-permute-start.11 = (f32[9,32,128]{2,1,0:T(8,128)S(1)}, f32[9,32,128]{2,1,0:T(8,128)S(1)}, u32[]{:S(2)}, u32[]{:S(2)}) collective-permute-start(f32[9,32,128]{2,1,0:T(8,128)S(1)} %add.12), channel_id=1, source_target_pairs={{0,16},{4,20},{8,24},{12,28},{16,0},{20,4},{24,8},{28,12},{1,17},{... | collective-permute-start | bytes 442376 | tf_op jit(solution)/shard_map/ppermute | solution.py:560
  57.5 0.0 collective-permute-done.6.refs_1_
  57.5 0.0 collective-permute-start.12
  57.5 0.0 collective-permute-done.7.refs_2_
  57.5 0.0 copy-start.5
  57.5 0.0 collective-permute-done.8.refs_3_
  57.5 0.0 copy-start.6
  57.5 0.7 copy-done.4
  58.2 0.1 copy-done.5
  58.3 0.1 copy-done.6
  58.4 10.2 %conv.1 = (bf16[256,32,128]{2,1,0:T(8,128)(2,1)}, bf16[256,32,128]{2,1,0:T(8,128)(2,1)}) custom-call(s32[1]{0:T(128)S(6)} %copy.9.own_turn.refs_0_, bf16[64,2048]{1,0:T(8,128)(2,1)} %copy-done.4, bf16[64,2048]{1,0:T(8,128)(2,1)} %copy-done.5, bf16[64,2048]{1,0:T(8,128)(2,1)} %copy-done.6, ...), custom_call_target="tpu_custom_call", output_to_operand_aliasing={{1}: (6, {})} | custom-call | flops 10066329600 | bytes 12582912 | tf_op jit(solution)/shard_map/conv/pallas_call | solution.py:551
  68.7 0.0 collective-permute-done.10
  68.7 0.0 collective-permute-done.11
  68.7 0.0 collective-permute-done.12
  68.7 0.7 %add_add_fusion = f32[9,32,128]{2,1,0:T(8,128)} fusion(f32[9,32,128]{2,1,0:T(8,128)S(1)} %collective-permute-done.11, f32[9,32,128]{2,1,0:T(8,128)S(1)} %collective-permute-done.12, f32[9,32,128]{2,1,0:T(8,128)S(1)} %add.12, f32[9,32,128]{2,1,0:T(8,128)S(1)} %collective-permute-done.10), kind=kLoop, calls=%fused_computation | loop fusion | flops 110592 | bytes 737280 | tf_op jit(solution)/shard_map/add | solution.py:564
  (5 shorter events, 0.0 us)
Async XLA Ops:
  0.6 17.5 %collective-permute-start = (bf16[9,32,128]{2,1,0:T(8,128)(2,1)}, bf16[9,32,128]{2,1,0:T(8,128)(2,1)S(1)}, u32[]{:S(2)}, u32[]{:S(2)}) collective-permute-start(bf16[9,32,128]{2,1,0:T(8,128)(2,1)} %bitcast.19), channel_id=1, source_target_pairs={{0,1},{1,0},{2,3},{3,2},{4,5},{5,4},{6,7},{7,6},{8,9},{9,8},{10,11... | collective-permute-start | bytes 221192 | tf_op jit(solution)/shard_map/ppermute | solution.py:589
  1.1 18.5 %collective-permute-start.1 = (bf16[9,32,128]{2,1,0:T(8,128)(2,1)}, bf16[9,32,128]{2,1,0:T(8,128)(2,1)S(1)}, u32[]{:S(2)}, u32[]{:S(2)}) collective-permute-start(bf16[9,32,128]{2,1,0:T(8,128)(2,1)} %bitcast.20), channel_id=1, source_target_pairs={{0,2},{1,3},{2,0},{3,1},{4,6},{5,7},{6,4},{7,5},{8,10},{9,11},{10,... | collective-permute-start | bytes 221192 | tf_op jit(solution)/shard_map/ppermute | solution.py:589
  3.7 15.9 %collective-permute-start.2 = (bf16[9,32,128]{2,1,0:T(8,128)(2,1)}, bf16[9,32,128]{2,1,0:T(8,128)(2,1)S(1)}, u32[]{:S(2)}, u32[]{:S(2)}) collective-permute-start(bf16[9,32,128]{2,1,0:T(8,128)(2,1)} %bitcast.21), channel_id=1, source_target_pairs={{0,3},{1,2},{2,1},{3,0},{4,7},{5,6},{6,5},{7,4},{8,11},{9,10},{10,... | collective-permute-start | bytes 221192 | tf_op jit(solution)/shard_map/ppermute | solution.py:589
  14.3 19.0 %collective-permute-start.3 = (bf16[32,2176]{1,0:T(8,128)(2,1)}, bf16[32,2176]{1,0:T(8,128)(2,1)S(1)}, u32[]{:S(2)}, u32[]{:S(2)}) collective-permute-start(bf16[32,2176]{1,0:T(8,128)(2,1)} %get-tuple-element.23), channel_id=1, source_target_pairs={{0,24},{4,28},{8,0},{12,4},{16,8},{20,12},{24,16},{28,20},{1,25},{... | collective-permute-start | bytes 417800 | tf_op jit(solution)/shard_map/ppermute | solution.py:582
  18.1 15.1 %collective-permute-start.4 = (bf16[32,2176]{1,0:T(8,128)(2,1)}, bf16[32,2176]{1,0:T(8,128)(2,1)S(1)}, u32[]{:S(2)}, u32[]{:S(2)}) collective-permute-start(bf16[32,2176]{1,0:T(8,128)(2,1)} %get-tuple-element.24), channel_id=1, source_target_pairs={{0,8},{4,12},{8,16},{12,20},{16,24},{20,28},{24,0},{28,4},{1,9},{5... | collective-permute-start | bytes 417800 | tf_op jit(solution)/shard_map/ppermute | solution.py:583
  18.1 1.6 %copy-start.7 = (bf16[9,32,128]{2,1,0:T(8,128)(2,1)}, bf16[9,32,128]{2,1,0:T(8,128)(2,1)S(1)}, u32[]{:S(2)}) copy-start(bf16[9,32,128]{2,1,0:T(8,128)(2,1)S(1)} %collective-permute-done.other1) | copy-start | bytes 221188
  18.1 15.1 %collective-permute-start.5 = (bf16[32,2176]{1,0:T(8,128)(2,1)}, bf16[32,2176]{1,0:T(8,128)(2,1)S(1)}, u32[]{:S(2)}, u32[]{:S(2)}) collective-permute-start(bf16[32,2176]{1,0:T(8,128)(2,1)} %get-tuple-element.25), channel_id=1, source_target_pairs={{0,4},{4,0},{8,12},{12,8},{16,20},{20,16},{24,28},{28,24},{1,5},{5... | collective-permute-start | bytes 417800 | tf_op jit(solution)/shard_map/ppermute | solution.py:584
  19.7 0.6 copy-start.8
  19.7 0.7 copy-start.9
  33.2 0.7 copy-start.1
  33.3 0.7 %copy-start.2 = (bf16[32,2176]{1,0:T(8,128)(2,1)}, bf16[32,2176]{1,0:T(8,128)(2,1)S(1)}, u32[]{:S(2)}) copy-start(bf16[32,2176]{1,0:T(8,128)(2,1)S(1)} %collective-permute-done.4.refs_7_) | copy-start | bytes 417796
  33.3 0.7 %copy-start.3 = (bf16[32,2176]{1,0:T(8,128)(2,1)}, bf16[32,2176]{1,0:T(8,128)(2,1)S(1)}, u32[]{:S(2)}) copy-start(bf16[32,2176]{1,0:T(8,128)(2,1)S(1)} %collective-permute-done.5.refs_8_) | copy-start | bytes 417796
  38.1 14.9 %collective-permute-start.9 = (f32[9,32,128]{2,1,0:T(8,128)}, f32[9,32,128]{2,1,0:T(8,128)S(1)}, u32[]{:S(2)}, u32[]{:S(2)}) collective-permute-start(f32[9,32,128]{2,1,0:T(8,128)} %get-tuple-element.32), channel_id=1, source_target_pairs={{0,4},{4,0},{8,12},{12,8},{16,20},{20,16},{24,28},{28,24},{1,5},{5... | collective-permute-start | bytes 442376 | tf_op jit(solution)/shard_map/ppermute | solution.py:560
  38.6 18.9 %collective-permute-start.6 = (bf16[64,2048]{1,0:T(8,128)(2,1)}, bf16[64,2048]{1,0:T(8,128)(2,1)S(1)}, u32[]{:S(2)}, u32[]{:S(2)}) collective-permute-start(bf16[64,2048]{1,0:T(8,128)(2,1)} %get-tuple-element.26), channel_id=1, source_target_pairs={{0,24},{4,28},{8,0},{12,4},{16,8},{20,12},{24,16},{28,20},{1,25},{... | collective-permute-start | bytes 786440 | tf_op jit(solution)/shard_map/ppermute | solution.py:582
  42.3 15.1 %collective-permute-start.7 = (bf16[64,2048]{1,0:T(8,128)(2,1)}, bf16[64,2048]{1,0:T(8,128)(2,1)S(1)}, u32[]{:S(2)}, u32[]{:S(2)}) collective-permute-start(bf16[64,2048]{1,0:T(8,128)(2,1)} %get-tuple-element.27), channel_id=1, source_target_pairs={{0,8},{4,12},{8,16},{12,20},{16,24},{20,28},{24,0},{28,4},{1,9},{5... | collective-permute-start | bytes 786440 | tf_op jit(solution)/shard_map/ppermute | solution.py:583
  42.3 10.6 %copy-start = (f32[9,32,128]{2,1,0:T(8,128)S(1)}, f32[9,32,128]{2,1,0:T(8,128)}, u32[]{:S(2)}) copy-start(f32[9,32,128]{2,1,0:T(8,128)} %get-tuple-element.32) | copy-start | bytes 442372
  42.3 15.1 %collective-permute-start.8 = (bf16[64,2048]{1,0:T(8,128)(2,1)}, bf16[64,2048]{1,0:T(8,128)(2,1)S(1)}, u32[]{:S(2)}, u32[]{:S(2)}) collective-permute-start(bf16[64,2048]{1,0:T(8,128)(2,1)} %get-tuple-element.28), channel_id=1, source_target_pairs={{0,4},{4,0},{8,12},{12,8},{16,20},{20,16},{24,28},{28,24},{1,5},{5... | collective-permute-start | bytes 786440 | tf_op jit(solution)/shard_map/ppermute | solution.py:584
  53.0 15.7 %collective-permute-start.10 = (f32[9,32,128]{2,1,0:T(8,128)S(1)}, f32[9,32,128]{2,1,0:T(8,128)S(1)}, u32[]{:S(2)}, u32[]{:S(2)}) collective-permute-start(f32[9,32,128]{2,1,0:T(8,128)S(1)} %add.12), channel_id=1, source_target_pairs={{0,8},{4,12},{8,0},{12,4},{16,24},{20,28},{24,16},{28,20},{1,9},{5... | collective-permute-start | bytes 442376 | tf_op jit(solution)/shard_map/ppermute | solution.py:560
  53.1 15.6 %collective-permute-start.11 = (f32[9,32,128]{2,1,0:T(8,128)S(1)}, f32[9,32,128]{2,1,0:T(8,128)S(1)}, u32[]{:S(2)}, u32[]{:S(2)}) collective-permute-start(f32[9,32,128]{2,1,0:T(8,128)S(1)} %add.12), channel_id=1, source_target_pairs={{0,16},{4,20},{8,24},{12,28},{16,0},{20,4},{24,8},{28,12},{1,17},{... | collective-permute-start | bytes 442376 | tf_op jit(solution)/shard_map/ppermute | solution.py:560
  57.5 0.7 %copy-start.4 = (bf16[64,2048]{1,0:T(8,128)(2,1)}, bf16[64,2048]{1,0:T(8,128)(2,1)S(1)}, u32[]{:S(2)}) copy-start(bf16[64,2048]{1,0:T(8,128)(2,1)S(1)} %collective-permute-done.6.refs_1_) | copy-start | bytes 786436
  57.5 11.3 %collective-permute-start.12 = (f32[9,32,128]{2,1,0:T(8,128)S(1)}, f32[9,32,128]{2,1,0:T(8,128)S(1)}, u32[]{:S(2)}, u32[]{:S(2)}) collective-permute-start(f32[9,32,128]{2,1,0:T(8,128)S(1)} %add.12), channel_id=1, source_target_pairs={{0,24},{4,28},{8,16},{12,20},{16,8},{20,12},{24,0},{28,4},{1,25},{... | collective-permute-start | bytes 442376 | tf_op jit(solution)/shard_map/ppermute | solution.py:560
  57.5 0.8 %copy-start.5 = (bf16[64,2048]{1,0:T(8,128)(2,1)}, bf16[64,2048]{1,0:T(8,128)(2,1)S(1)}, u32[]{:S(2)}) copy-start(bf16[64,2048]{1,0:T(8,128)(2,1)S(1)} %collective-permute-done.7.refs_2_) | copy-start | bytes 786436
  57.5 0.9 %copy-start.6 = (bf16[64,2048]{1,0:T(8,128)(2,1)}, bf16[64,2048]{1,0:T(8,128)(2,1)S(1)}, u32[]{:S(2)}) copy-start(bf16[64,2048]{1,0:T(8,128)(2,1)S(1)} %collective-permute-done.8.refs_3_) | copy-start | bytes 786436

commit v7 on v6

--- a/solution.py
+++ b/solution.py
@@ -112,30 +112,66 @@
     _, batch, rows, side, _ = stage.shape
     for row in range(rows):
         block = jnp.swapaxes(stage[pair, :, row], 0, 1)
-        if held is not None:
-            held[pl.ds((2 * pair + row) * side, side)] = block
+        held[pl.ds((2 * pair + row) * side, side)] = block
         for col in range(side):
             flat[2 * pair + row, :, col * batch : (col + 1) * batch] = block[col].T
 
 
 def upstream_kernel(
     own_turn, upstream, turned, edges, east, west, across,
-    stage, flat, in_sems, turned_sems, edge_sems,
+    stage, even, odd, flat, shuffle, in_sems, turned_sems, edge_sems,
 ):
     pairs, batch, rows, side, channels = stage.shape
     share = east.shape[0]
+    group = 256 // side
     for pair in range(AHEAD):
         pair_in(upstream, stage, in_sems, pair).start()
-
-    @pl.loop(0, pairs)
-    def _(pair):
+    to = lax.broadcasted_iota(jnp.int32, (256, 256), 0)
+    come = lax.broadcasted_iota(jnp.int32, (256, 256), 1)
+    moves = (to // group == come % side) & (to % group == come // side)
+    shuffle[...] = jnp.where(moves, 1.0, 0.0).astype(jnp.bfloat16)
+
+    def permute(pair, held):
         @pl.when(pair + AHEAD < pairs)
         def _():
             pair_in(upstream, stage, in_sems, pair + AHEAD).start()
 
         pair_in(upstream, stage, in_sems, pair).wait()
-        lay_pair(stage, None, flat, pair)
+        for start in range(0, batch, group):
+            block = jnp.concatenate(
+                [
+                    stage[pair, start : start + group, row].reshape(256, channels)
+                    for row in range(rows)
+                ],
+                axis=1,
+            )
+            moved = dot(shuffle[...], block, FLAT).astype(jnp.bfloat16)
+            for row in range(rows):
+                held[row * side : (row + 1) * side, start : start + group] = moved[
+                    :, row * channels : (row + 1) * channels
+                ].reshape(side, group, channels)
+
+    def turn_pair(pair, held):
+        for row in range(rows):
+            for col in range(side):
+                flat[2 * pair + row, :, col * batch : (col + 1) * batch] = held[
+                    row * side + col
+                ].T
         turned_out(flat, turned, turned_sems, pair).start()
+
+    permute(jnp.int32(0), even)
+
+    @pl.loop(0, pairs // 2 - 1)
+    def _(step):
+        pair = 2 * step
+        permute(pair + 1, odd)
+        turn_pair(pair, even)
+        permute(pair + 2, even)
+        turn_pair(pair + 1, odd)
+
+    permute(jnp.int32(pairs - 1), odd)
+    turn_pair(pairs - 2, even)
+    turn_pair(pairs - 1, odd)
 
     chan = lax.axis_index("chan").astype(jnp.int32)
     own = pl.ds(pl.multiple_of(chan * share, share), share)
@@ -175,7 +211,10 @@
         out_shape=[turned, edges] + [message] * 3,
         scratch_shapes=[
             pltpu.VMEM((pairs, batch, 2, side, channels), jnp.bfloat16),
+            pltpu.VMEM((2 * side, batch, channels), jnp.bfloat16),
+            pltpu.VMEM((2 * side, batch, channels), jnp.bfloat16),
             pltpu.VMEM(turned.shape, jnp.bfloat16),
+            pltpu.VMEM((256, 256), jnp.bfloat16),
             pltpu.SemaphoreType.DMA((pairs,)),
             pltpu.SemaphoreType.DMA((pairs,)),
             pltpu.SemaphoreType.DMA((3,)),
@@ -314,8 +353,21 @@
     )(turn, *weights, field, turned)
 
 
-def seam_kernel(scale, own_turn, edges, upstream_edges, inner, weight, rowed, *refs):
+def seam_kernel(scale, own_turn, edges_in, upstream_in, inner, weight, rowed, *refs):
     messages, out, terms_out = refs[:3], refs[3], refs[4:7]
+    edges, upstream_edges, sems = refs[7:]
+
+    def edge_in(edge):
+        return (
+            pltpu.make_async_copy(edges_in.at[edge], edges.at[edge], sems.at[0, edge]),
+            pltpu.make_async_copy(
+                upstream_in.at[edge], upstream_edges.at[edge], sems.at[1, edge]
+            ),
+        )
+
+    for edge in range(3):
+        for copy in edge_in(edge):
+            copy.start()
     side, batch, channels = edges.shape[1:]
     share = out.shape[1]
     width = side * batch
@@ -325,6 +377,8 @@
         turn = jnp.max(message[0:16, width:].astype(jnp.float32)).astype(jnp.int32)
         taps = [edge_tap(turn, lower, edge, d, False) for d in range(3)]
         turned = message[:, 0:width]
+        for copy in edge_in(edge):
+            copy.wait()
         left = jnp.concatenate([earlier(turned, batch), turned, later(turned, batch)], axis=0)
         pixels = edges[edge].reshape(width, channels)
         terms = dot(left, pixels, FLAT)
@@ -351,8 +405,15 @@
 
     return pl.pallas_call(
         body,
-        in_specs=[pl.BlockSpec(memory_space=pltpu.SMEM)] + [vmem] * 8,
+        in_specs=[pl.BlockSpec(memory_space=pltpu.SMEM)]
+        + [pl.BlockSpec(memory_space=pl.ANY)] * 2
+        + [vmem] * 6,
         out_specs=[vmem] * 4,
+        scratch_shapes=[
+            pltpu.VMEM(edges.shape, jnp.bfloat16),
+            pltpu.VMEM(upstream_edges.shape, jnp.bfloat16),
+            pltpu.SemaphoreType.DMA((2, 3)),
+        ],
         out_shape=[jax.ShapeDtypeStruct(inner.shape, jnp.float32)]
         + [jax.ShapeDtypeStruct((2 * share, side * batch), jnp.bfloat16)] * 3,
         compiler_params=pltpu.CompilerParams(vmem_limit_bytes=BIG),
@@ -434,13 +495,16 @@
     if last:
         start_border(cols, side, other_in, other, other_sems)
         lower = half_of_band()
+        edges = [edge_place(own_turn[0], lower, edge, side) for edge in range(3)]
+        for (first, step), message in zip(edges, (east, west, across)):
+            for pos in range(side):
+                place = slice(pos * batch, (pos + 1) * batch)
+                sums[first + pos * step + cols] += message[0:share, place].astype(jnp.float32)
         wait_border(cols, side, other_in, other, other_sems)
-        for edge, message in enumerate((east, west, across)):
-            first, step = edge_place(own_turn[0], lower, edge, side)
+        for (first, step), message in zip(edges, (east, west, across)):
             for pos in range(side):
                 pixel = first + pos * step
                 place = slice(pos * batch, (pos + 1) * batch)
-                sums[pixel + cols] += message[0:share, place].astype(jnp.float32)
                 other[pixel] = (
                     other[pixel].astype(jnp.float32)
                     + message[share:, place].astype(jnp.float32)

time: 70.2 us -> 70.4 us (level)
    pallas_call x1, Pallas kernels: 4.05 us -> 4.77 us  [seam_filters(): pl.pallas_call(body, in_specs=[pl.BlockSpec(memory_space=pltpu.SMEM)] + [...]
  transfers between devices with their start and end apart: 13 -> 13, of which waited for: 0 -> 0; matrix products, arithmetic and copies ran while one was open for 0% -> 0% of each run, Pallas kernels for 61% -> 59%
where the time goes in v7:
time: 70.4 us; the launch traced here: 69.6 us
  Pallas kernels  46.2 us (66%)
  starting transfers between devices  18.9 us (27%)
  local copies, waits for them, and re-layouts  2.31 us (3%)
  between operations  1.49 us (2%)
  other arithmetic  0.73 us (1%)
    pallas_call x1, Pallas kernels, lay_field(): pl.pallas_call(field_kernel, in_specs=[pl.BlockSpec(memory_space=pltpu.SM...  12.9 us
    pallas_call x1, Pallas kernels, convolved(): call(turn, *messages, source, weight, other)  10.2 us
    pallas_call x1, Pallas kernels, lay_upstream(): pl.pallas_call(upstream_kernel, in_specs=[pl.BlockSpec(memory_space=pltpu...  9.28 us
    pallas_call x1, Pallas kernels, convolved(): call(source, weight)  9.09 us
    ppermute x2, starting transfers between devices, exchanged(): lax.ppermute(sends[1], 'tile', westward)  7.6 us
    ppermute x4, starting transfers between devices, other(): return lax.ppermute(total, 'tile', [(i, i ^ flip) for i in range(count)])  5.02 us
    pallas_call x1, Pallas kernels, seam_filters(): pl.pallas_call(body, in_specs=[pl.BlockSpec(memory_space=pltpu.SMEM)] + [...  4.77 us
    ppermute x3, starting transfers between devices, per_device(): lax.ppermute(own, 'chan', [(i, i ^ flip) for i in range(channels // share)])  3.18 us
  transfers between devices with their start and end apart: 13, of which 0 were waited for; matrix products, arithmetic and copies ran while one was open for 0% of the time, Pallas kernels for 59%

profile of v7, /device:TPU:0, one launch (start us, length us, event | category | flops | bytes accessed | tf_op | source)
XLA Modules:
  0.0 69.6 jit_solution(7520369826254822988)
XLA Ops:
  0.6 0.5 collective-permute-start
  1.1 2.6 %collective-permute-start.1 = (bf16[9,32,128]{2,1,0:T(8,128)(2,1)}, bf16[9,32,128]{2,1,0:T(8,128)(2,1)S(1)}, u32[]{:S(2)}, u32[]{:S(2)}) collective-permute-start(bf16[9,32,128]{2,1,0:T(8,128)(2,1)} %bitcast.20), channel_id=1, source_target_pairs={{0,2},{1,3},{2,0},{3,1},{4,6},{5,7},{6,4},{7,5},{8,10},{9,11},{10,... | collective-permute-start | bytes 221192 | tf_op jit(solution)/shard_map/ppermute | solution.py:653
  3.7 0.1 collective-permute-start.2
  4.5 9.3 %lay_upstream.1 = (bf16[16,128,2048]{2,1,0:T(8,128)(2,1)}, bf16[3,128,2048]{2,1,0:T(8,128)(2,1)}, bf16[32,2176]{1,0:T(8,128)(2,1)}, bf16[32,2176]{1,0:T(8,128)(2,1)}, bf16[32,2176]{1,0:T(8,128)(2,1)}) custom-call(s32[1]{0:T(128)S(6)} %copy.9.own_turn.refs_0_, bf16[128,16,16,128]{3,2,1,0:T(8,128)(2,1)} %bitcast.25), custom_call_target="tpu_custom_call" | custom-call | flops 4294967296 | bytes 16777216 | tf_op jit(solution)/shard_map/lay_upstream/pallas_call | solution.py:207
  13.8 3.8 %collective-permute-start.3 = (bf16[32,2176]{1,0:T(8,128)(2,1)}, bf16[32,2176]{1,0:T(8,128)(2,1)S(1)}, u32[]{:S(2)}, u32[]{:S(2)}) collective-permute-start(bf16[32,2176]{1,0:T(8,128)(2,1)} %get-tuple-element.23), channel_id=1, source_target_pairs={{0,24},{4,28},{8,0},{12,4},{16,8},{20,12},{24,16},{28,20},{1,25},{... | collective-permute-start | bytes 417800 | tf_op jit(solution)/shard_map/ppermute | solution.py:646
  17.6 0.0 collective-permute-start.4
  17.6 0.0 collective-permute-done.other1
  17.6 1.6 %collective-permute-start.5 = (bf16[32,2176]{1,0:T(8,128)(2,1)}, bf16[32,2176]{1,0:T(8,128)(2,1)S(1)}, u32[]{:S(2)}, u32[]{:S(2)}) collective-permute-start(bf16[32,2176]{1,0:T(8,128)(2,1)} %get-tuple-element.25), channel_id=1, source_target_pairs={{0,4},{4,0},{8,12},{12,8},{16,20},{20,16},{24,28},{28,24},{1,5},{5... | collective-permute-start | bytes 417800 | tf_op jit(solution)/shard_map/ppermute | solution.py:648
  19.2 0.0 collective-permute-done.1.other2
  19.2 0.0 collective-permute-done.2.other3
  19.2 0.0 copy-start.9
  19.2 0.0 copy-done.7
  19.2 0.6 copy-done.8
  19.8 0.0 copy-done.9
  19.9 12.9 %lay_field.1 = (bf16[16,128,2048]{2,1,0:T(8,128)(2,1)}, bf16[3,16,128,128]{3,2,1,0:T(8,128)(2,1)}, f32[9,32,128]{2,1,0:T(8,128)}, bf16[9,32,128]{2,1,0:T(8,128)(2,1)}) custom-call(s32[1]{0:T(128)S(6)} %copy.9.own_turn.refs_0_, bf16[9,32,128]{2,1,0:T(8,128)(2,1)} %bitcast.22, bf16[9,32,128]{2,1,0:T(8,128)(2,1)} %copy-done.7, bf16[9,32,128]{2,1,0:T(8,128)(2,1)} %copy-done.8, ...), custom_call_target="tpu_custom_call" | custom-call | flops 7549747200 | bytes 20971520 | tf_op jit(solution)/shard_map/lay_field/pallas_call | solution.py:329
  32.7 0.0 collective-permute-done.3.refs_6_
  32.7 0.0 copy-start.1
  32.8 0.0 collective-permute-done.4.refs_7_
  32.8 0.0 copy-start.2
  32.8 0.0 collective-permute-done.5.refs_8_
  32.8 0.0 copy-start.3
  32.8 0.6 copy-done.1
  33.4 0.1 copy-done.2
  33.5 0.0 copy-done.3
  33.5 4.8 %seam_filters.1 = (f32[9,32,128]{2,1,0:T(8,128)}, bf16[64,2048]{1,0:T(8,128)(2,1)}, bf16[64,2048]{1,0:T(8,128)(2,1)}, bf16[64,2048]{1,0:T(8,128)(2,1)}) custom-call(s32[1]{0:T(128)S(6)} %copy.9.own_turn.refs_0_, bf16[3,16,128,128]{3,2,1,0:T(8,128)(2,1)} %get-tuple-element.19.refs_1_, bf16[3,128,2048]{2,1,0:T(8,128)(2,1)} %get-tuple-element.20.refs_2_, ...), custom_call_target="tpu_custom_call" | custom-call | flops 452984832 | bytes 3145728 | tf_op jit(solution)/shard_map/seam_filters/pallas_call | solution.py:406
  38.3 0.6 collective-permute-start.9
  38.9 3.8 %collective-permute-start.6 = (bf16[64,2048]{1,0:T(8,128)(2,1)}, bf16[64,2048]{1,0:T(8,128)(2,1)S(1)}, u32[]{:S(2)}, u32[]{:S(2)}) collective-permute-start(bf16[64,2048]{1,0:T(8,128)(2,1)} %get-tuple-element.26), channel_id=1, source_target_pairs={{0,24},{4,28},{8,0},{12,4},{16,8},{20,12},{24,16},{28,20},{1,25},{... | collective-permute-start | bytes 786440 | tf_op jit(solution)/shard_map/ppermute | solution.py:646
  42.6 0.0 collective-permute-start.7
  42.6 1.5 %collective-permute-start.8 = (bf16[64,2048]{1,0:T(8,128)(2,1)}, bf16[64,2048]{1,0:T(8,128)(2,1)S(1)}, u32[]{:S(2)}, u32[]{:S(2)}) collective-permute-start(bf16[64,2048]{1,0:T(8,128)(2,1)} %get-tuple-element.28), channel_id=1, source_target_pairs={{0,4},{4,0},{8,12},{12,8},{16,20},{20,16},{24,28},{28,24},{1,5},{5... | collective-permute-start | bytes 786440 | tf_op jit(solution)/shard_map/ppermute | solution.py:648
  44.1 9.1 %grad_conv.1.refs_6_ = bf16[256,32,128]{2,1,0:T(8,128)(2,1)} custom-call(bf16[16,128,2048]{2,1,0:T(8,128)(2,1)} %get-tuple-element.18.turned.refs_0_, bf16[9,32,128]{2,1,0:T(8,128)(2,1)} %get-tuple-element.22.refs_5_.refs_1_), custom_call_target="tpu_custom_call" | custom-call | flops 10066329600 | bytes 12582912 | tf_op jit(solution)/shard_map/grad_conv/pallas_call | solution.py:615
  53.2 0.0 collective-permute-done.9
  53.3 0.0 copy-done
  53.3 0.1 collective-permute-start.10
  53.4 4.4 %collective-permute-start.11 = (f32[9,32,128]{2,1,0:T(8,128)S(1)}, f32[9,32,128]{2,1,0:T(8,128)S(1)}, u32[]{:S(2)}, u32[]{:S(2)}) collective-permute-start(f32[9,32,128]{2,1,0:T(8,128)S(1)} %add.12), channel_id=1, source_target_pairs={{0,16},{4,20},{8,24},{12,28},{16,0},{20,4},{24,8},{28,12},{1,17},{... | collective-permute-start | bytes 442376 | tf_op jit(solution)/shard_map/ppermute | solution.py:624
  57.7 0.0 collective-permute-done.6.refs_1_
  57.8 0.0 collective-permute-start.12
  57.8 0.0 collective-permute-done.7.refs_2_
  57.8 0.0 copy-start.5
  57.8 0.0 collective-permute-done.8.refs_3_
  57.8 0.0 copy-start.6
  57.8 0.7 copy-done.4
  58.5 0.1 copy-done.5
  58.6 0.1 copy-done.6
  58.7 10.2 %conv.1 = (bf16[256,32,128]{2,1,0:T(8,128)(2,1)}, bf16[256,32,128]{2,1,0:T(8,128)(2,1)}) custom-call(s32[1]{0:T(128)S(6)} %copy.9.own_turn.refs_0_, bf16[64,2048]{1,0:T(8,128)(2,1)} %copy-done.4, bf16[64,2048]{1,0:T(8,128)(2,1)} %copy-done.5, bf16[64,2048]{1,0:T(8,128)(2,1)} %copy-done.6, ...), custom_call_target="tpu_custom_call", output_to_operand_aliasing={{1}: (6, {})} | custom-call | flops 10066329600 | bytes 12582912 | tf_op jit(solution)/shard_map/conv/pallas_call | solution.py:615
  68.9 0.0 collective-permute-done.10
  68.9 0.0 collective-permute-done.11
  68.9 0.0 collective-permute-done.12
  68.9 0.7 %add_add_fusion = f32[9,32,128]{2,1,0:T(8,128)} fusion(f32[9,32,128]{2,1,0:T(8,128)S(1)} %collective-permute-done.11, f32[9,32,128]{2,1,0:T(8,128)S(1)} %collective-permute-done.12, f32[9,32,128]{2,1,0:T(8,128)S(1)} %add.12, f32[9,32,128]{2,1,0:T(8,128)S(1)} %collective-permute-done.10), kind=kLoop, calls=%fused_computation | loop fusion | flops 110592 | bytes 737280 | tf_op jit(solution)/shard_map/add | solution.py:628
  (5 shorter events, 0.0 us)
Async XLA Ops:
  0.6 17.0 %collective-permute-start = (bf16[9,32,128]{2,1,0:T(8,128)(2,1)}, bf16[9,32,128]{2,1,0:T(8,128)(2,1)S(1)}, u32[]{:S(2)}, u32[]{:S(2)}) collective-permute-start(bf16[9,32,128]{2,1,0:T(8,128)(2,1)} %bitcast.19), channel_id=1, source_target_pairs={{0,1},{1,0},{2,3},{3,2},{4,5},{5,4},{6,7},{7,6},{8,9},{9,8},{10,11... | collective-permute-start | bytes 221192 | tf_op jit(solution)/shard_map/ppermute | solution.py:653
  1.1 18.0 %collective-permute-start.1 = (bf16[9,32,128]{2,1,0:T(8,128)(2,1)}, bf16[9,32,128]{2,1,0:T(8,128)(2,1)S(1)}, u32[]{:S(2)}, u32[]{:S(2)}) collective-permute-start(bf16[9,32,128]{2,1,0:T(8,128)(2,1)} %bitcast.20), channel_id=1, source_target_pairs={{0,2},{1,3},{2,0},{3,1},{4,6},{5,7},{6,4},{7,5},{8,10},{9,11},{10,... | collective-permute-start | bytes 221192 | tf_op jit(solution)/shard_map/ppermute | solution.py:653
  3.7 15.5 %collective-permute-start.2 = (bf16[9,32,128]{2,1,0:T(8,128)(2,1)}, bf16[9,32,128]{2,1,0:T(8,128)(2,1)S(1)}, u32[]{:S(2)}, u32[]{:S(2)}) collective-permute-start(bf16[9,32,128]{2,1,0:T(8,128)(2,1)} %bitcast.21), channel_id=1, source_target_pairs={{0,3},{1,2},{2,1},{3,0},{4,7},{5,6},{6,5},{7,4},{8,11},{9,10},{10,... | collective-permute-start | bytes 221192 | tf_op jit(solution)/shard_map/ppermute | solution.py:653
  13.8 19.0 %collective-permute-start.3 = (bf16[32,2176]{1,0:T(8,128)(2,1)}, bf16[32,2176]{1,0:T(8,128)(2,1)S(1)}, u32[]{:S(2)}, u32[]{:S(2)}) collective-permute-start(bf16[32,2176]{1,0:T(8,128)(2,1)} %get-tuple-element.23), channel_id=1, source_target_pairs={{0,24},{4,28},{8,0},{12,4},{16,8},{20,12},{24,16},{28,20},{1,25},{... | collective-permute-start | bytes 417800 | tf_op jit(solution)/shard_map/ppermute | solution.py:646
  17.6 15.2 %collective-permute-start.4 = (bf16[32,2176]{1,0:T(8,128)(2,1)}, bf16[32,2176]{1,0:T(8,128)(2,1)S(1)}, u32[]{:S(2)}, u32[]{:S(2)}) collective-permute-start(bf16[32,2176]{1,0:T(8,128)(2,1)} %get-tuple-element.24), channel_id=1, source_target_pairs={{0,8},{4,12},{8,16},{12,20},{16,24},{20,28},{24,0},{28,4},{1,9},{5... | collective-permute-start | bytes 417800 | tf_op jit(solution)/shard_map/ppermute | solution.py:647
  17.6 1.6 %copy-start.7 = (bf16[9,32,128]{2,1,0:T(8,128)(2,1)}, bf16[9,32,128]{2,1,0:T(8,128)(2,1)S(1)}, u32[]{:S(2)}) copy-start(bf16[9,32,128]{2,1,0:T(8,128)(2,1)S(1)} %collective-permute-done.other1) | copy-start | bytes 221188
  17.6 15.2 %collective-permute-start.5 = (bf16[32,2176]{1,0:T(8,128)(2,1)}, bf16[32,2176]{1,0:T(8,128)(2,1)S(1)}, u32[]{:S(2)}, u32[]{:S(2)}) collective-permute-start(bf16[32,2176]{1,0:T(8,128)(2,1)} %get-tuple-element.25), channel_id=1, source_target_pairs={{0,4},{4,0},{8,12},{12,8},{16,20},{20,16},{24,28},{28,24},{1,5},{5... | collective-permute-start | bytes 417800 | tf_op jit(solution)/shard_map/ppermute | solution.py:648
  19.2 0.6 copy-start.8
  19.2 0.7 copy-start.9
  32.7 0.7 copy-start.1
  32.8 0.7 %copy-start.2 = (bf16[32,2176]{1,0:T(8,128)(2,1)}, bf16[32,2176]{1,0:T(8,128)(2,1)S(1)}, u32[]{:S(2)}) copy-start(bf16[32,2176]{1,0:T(8,128)(2,1)S(1)} %collective-permute-done.4.refs_7_) | copy-start | bytes 417796
  32.8 0.7 %copy-start.3 = (bf16[32,2176]{1,0:T(8,128)(2,1)}, bf16[32,2176]{1,0:T(8,128)(2,1)S(1)}, u32[]{:S(2)}) copy-start(bf16[32,2176]{1,0:T(8,128)(2,1)S(1)} %collective-permute-done.5.refs_8_) | copy-start | bytes 417796
  38.3 14.9 %collective-permute-start.9 = (f32[9,32,128]{2,1,0:T(8,128)}, f32[9,32,128]{2,1,0:T(8,128)S(1)}, u32[]{:S(2)}, u32[]{:S(2)}) collective-permute-start(f32[9,32,128]{2,1,0:T(8,128)} %get-tuple-element.32), channel_id=1, source_target_pairs={{0,4},{4,0},{8,12},{12,8},{16,20},{20,16},{24,28},{28,24},{1,5},{5... | collective-permute-start | bytes 442376 | tf_op jit(solution)/shard_map/ppermute | solution.py:624
  38.9 18.9 %collective-permute-start.6 = (bf16[64,2048]{1,0:T(8,128)(2,1)}, bf16[64,2048]{1,0:T(8,128)(2,1)S(1)}, u32[]{:S(2)}, u32[]{:S(2)}) collective-permute-start(bf16[64,2048]{1,0:T(8,128)(2,1)} %get-tuple-element.26), channel_id=1, source_target_pairs={{0,24},{4,28},{8,0},{12,4},{16,8},{20,12},{24,16},{28,20},{1,25},{... | collective-permute-start | bytes 786440 | tf_op jit(solution)/shard_map/ppermute | solution.py:646
  42.6 15.1 %collective-permute-start.7 = (bf16[64,2048]{1,0:T(8,128)(2,1)}, bf16[64,2048]{1,0:T(8,128)(2,1)S(1)}, u32[]{:S(2)}, u32[]{:S(2)}) collective-permute-start(bf16[64,2048]{1,0:T(8,128)(2,1)} %get-tuple-element.27), channel_id=1, source_target_pairs={{0,8},{4,12},{8,16},{12,20},{16,24},{20,28},{24,0},{28,4},{1,9},{5... | collective-permute-start | bytes 786440 | tf_op jit(solution)/shard_map/ppermute | solution.py:647
  42.6 10.6 %copy-start = (f32[9,32,128]{2,1,0:T(8,128)S(1)}, f32[9,32,128]{2,1,0:T(8,128)}, u32[]{:S(2)}) copy-start(f32[9,32,128]{2,1,0:T(8,128)} %get-tuple-element.32) | copy-start | bytes 442372
  42.6 15.2 %collective-permute-start.8 = (bf16[64,2048]{1,0:T(8,128)(2,1)}, bf16[64,2048]{1,0:T(8,128)(2,1)S(1)}, u32[]{:S(2)}, u32[]{:S(2)}) collective-permute-start(bf16[64,2048]{1,0:T(8,128)(2,1)} %get-tuple-element.28), channel_id=1, source_target_pairs={{0,4},{4,0},{8,12},{12,8},{16,20},{20,16},{24,28},{28,24},{1,5},{5... | collective-permute-start | bytes 786440 | tf_op jit(solution)/shard_map/ppermute | solution.py:648
  53.3 15.6 %collective-permute-start.10 = (f32[9,32,128]{2,1,0:T(8,128)S(1)}, f32[9,32,128]{2,1,0:T(8,128)S(1)}, u32[]{:S(2)}, u32[]{:S(2)}) collective-permute-start(f32[9,32,128]{2,1,0:T(8,128)S(1)} %add.12), channel_id=1, source_target_pairs={{0,8},{4,12},{8,0},{12,4},{16,24},{20,28},{24,16},{28,20},{1,9},{5... | collective-permute-start | bytes 442376 | tf_op jit(solution)/shard_map/ppermute | solution.py:624
  53.4 15.5 %collective-permute-start.11 = (f32[9,32,128]{2,1,0:T(8,128)S(1)}, f32[9,32,128]{2,1,0:T(8,128)S(1)}, u32[]{:S(2)}, u32[]{:S(2)}) collective-permute-start(f32[9,32,128]{2,1,0:T(8,128)S(1)} %add.12), channel_id=1, source_target_pairs={{0,16},{4,20},{8,24},{12,28},{16,0},{20,4},{24,8},{28,12},{1,17},{... | collective-permute-start | bytes 442376 | tf_op jit(solution)/shard_map/ppermute | solution.py:624
  57.8 0.7 %copy-start.4 = (bf16[64,2048]{1,0:T(8,128)(2,1)}, bf16[64,2048]{1,0:T(8,128)(2,1)S(1)}, u32[]{:S(2)}) copy-start(bf16[64,2048]{1,0:T(8,128)(2,1)S(1)} %collective-permute-done.6.refs_1_) | copy-start | bytes 786436
  57.8 11.2 %collective-permute-start.12 = (f32[9,32,128]{2,1,0:T(8,128)S(1)}, f32[9,32,128]{2,1,0:T(8,128)S(1)}, u32[]{:S(2)}, u32[]{:S(2)}) collective-permute-start(f32[9,32,128]{2,1,0:T(8,128)S(1)} %add.12), channel_id=1, source_target_pairs={{0,24},{4,28},{8,16},{12,20},{16,8},{20,12},{24,0},{28,4},{1,25},{... | collective-permute-start | bytes 442376 | tf_op jit(solution)/shard_map/ppermute | solution.py:624
  57.8 0.8 %copy-start.5 = (bf16[64,2048]{1,0:T(8,128)(2,1)}, bf16[64,2048]{1,0:T(8,128)(2,1)S(1)}, u32[]{:S(2)}) copy-start(bf16[64,2048]{1,0:T(8,128)(2,1)S(1)} %collective-permute-done.7.refs_2_) | copy-start | bytes 786436
  57.8 0.9 %copy-start.6 = (bf16[64,2048]{1,0:T(8,128)(2,1)}, bf16[64,2048]{1,0:T(8,128)(2,1)S(1)}, u32[]{:S(2)}) copy-start(bf16[64,2048]{1,0:T(8,128)(2,1)S(1)} %collective-permute-done.8.refs_3_) | copy-start | bytes 786436

commit v8 on v7

--- a/solution.py
+++ b/solution.py
@@ -88,13 +88,12 @@
     ).astype(jnp.bfloat16)
 
 
-def gather_filters(parts, whole):
-    taps, share, _ = parts[0].shape
+def gather_filters(tap, parts, whole):
+    share = parts[0].shape[1]
     chan = lax.axis_index("chan").astype(jnp.int32)
     for flip, part in enumerate(parts):
         start = pl.multiple_of((chan ^ flip) * share, share)
-        for tap in range(taps):
-            whole[tap, pl.ds(start, share)] = part[tap]
+        whole[tap, pl.ds(start, share)] = part[tap]
 
 
 def pair_in(source, stage, sems, pair):
@@ -106,15 +105,6 @@
 def turned_out(flat, turned, sems, pair):
     part = pl.ds(2 * pair, 2)
     return pltpu.make_async_copy(flat.at[part], turned.at[part], sems.at[pair])
-
-
-def lay_pair(stage, held, flat, pair):
-    _, batch, rows, side, _ = stage.shape
-    for row in range(rows):
-        block = jnp.swapaxes(stage[pair, :, row], 0, 1)
-        held[pl.ds((2 * pair + row) * side, side)] = block
-        for col in range(side):
-            flat[2 * pair + row, :, col * batch : (col + 1) * batch] = block[col].T
 
 
 def upstream_kernel(
@@ -229,7 +219,8 @@
 
 def field_kernel(
     own_turn, weight, other1, other2, other3, field, turned, laid, edges, inner, rowed,
-    stage, held, flat, padded, total, whole, in_sems, out_sems, turned_sem, edge_sems,
+    stage, held, even, odd, flat, padded, total, whole,
+    in_sems, out_sems, turned_sem, edge_sems,
 ):
     pairs, batch, rows, side, channels = stage.shape
     share = padded.shape[1]
@@ -250,17 +241,27 @@
     padded[1 : side + 1, :, width + batch :] = column
     total[...] = jnp.zeros_like(total)
 
-    def lay(pair):
+    def lay(pair, block, full_row=None):
         pair_in(field, stage, in_sems, pair).wait()
-        lay_pair(stage, held, flat, pair)
+        for row in range(rows):
+            moved = jnp.swapaxes(stage[pair, :, row], 0, 1)
+            block[row * side : (row + 1) * side] = moved
+            first = (2 * pair + row) * side
+            if row == full_row:
+                held[pl.ds(first, side)] = moved
+            else:
+                held[first] = moved[0]
+                held[first + side - 1] = moved[side - 1]
+            for col in range(side):
+                flat[2 * pair + row, :, col * batch : (col + 1) * batch] = moved[col].T
         turned_out(flat, laid, out_sems, pair).start()
 
-    def add_filters(pair):
+    def add_filters(pair, block):
         cols = 8
         for start in range(0, side, cols):
             right = jnp.concatenate(
                 [
-                    held[pl.ds((2 * pair + row) * side + start, cols)].reshape(
+                    block[row * side + start : row * side + start + cols].reshape(
                         cols * batch, channels
                     )
                     for row in range(rows)
@@ -277,21 +278,36 @@
                 left = jnp.concatenate(parts[3 * half : 3 * half + 3], axis=0)
                 total[6 * share * half : 6 * share * (half + 1)] += dot(left, right, FLAT)
 
-    gather_filters((weight, other1, other2, other3), whole)
     pick = one_hot(share, channels)
-    for tap in range(9):
+
+    def by_rows(tap):
+        gather_filters(tap, (weight, other1, other2, other3), whole)
         rowed[tap] = dot(pick, whole[tap], TURNED).astype(jnp.bfloat16)
-    lay(0)
+
+    def request(pair):
+        @pl.when(pair < pairs)
+        def _():
+            pair_in(field, stage, in_sems, pair).start()
+
+    lay(0, even, 0)
     turned_in.wait()
 
-    @pl.loop(1, pairs)
-    def _(pair):
-        @pl.when(pair + AHEAD - 1 < pairs)
-        def _():
-            pair_in(field, stage, in_sems, pair + AHEAD - 1).start()
-
-        add_filters(pair - 1)
-        lay(pair)
+    @pl.loop(0, pairs // 2 - 1)
+    def _(step):
+        pair = 2 * step
+        request(pair + AHEAD)
+        add_filters(pair, even)
+        lay(pair + 1, odd)
+        by_rows(pair)
+        request(pair + 1 + AHEAD)
+        add_filters(pair + 1, odd)
+        lay(pair + 2, even)
+        by_rows(pair + 1)
+
+    add_filters(pairs - 2, even)
+    lay(pairs - 1, odd, rows - 1)
+    for tap in range(pairs - 2, 9):
+        by_rows(tap)
 
     lower = half_of_band()
     turn = own_turn[0]
@@ -301,7 +317,7 @@
             pltpu.make_async_copy(
                 held.at[first + pos * step], edges.at[edge, pos], edge_sems.at[edge]
             ).start()
-    add_filters(pairs - 1)
+    add_filters(pairs - 1, odd)
     for row_tap in range(3):
         for col_tap in range(3):
             value = jnp.zeros((share, channels), jnp.float32)
@@ -336,6 +352,8 @@
         scratch_shapes=[
             pltpu.VMEM((pairs, batch, 2, side, channels), jnp.bfloat16),
             pltpu.VMEM((side * side, batch, channels), jnp.bfloat16),
+            pltpu.VMEM((2 * side, batch, channels), jnp.bfloat16),
+            pltpu.VMEM((2 * side, batch, channels), jnp.bfloat16),
             pltpu.VMEM(laid.shape, jnp.bfloat16),
             pltpu.VMEM((side + 2, share, (side + 2) * batch), jnp.bfloat16),
             pltpu.VMEM((12 * share, 2 * channels), jnp.float32),
@@ -353,21 +371,8 @@
     )(turn, *weights, field, turned)
 
 
-def seam_kernel(scale, own_turn, edges_in, upstream_in, inner, weight, rowed, *refs):
+def seam_kernel(scale, own_turn, edges, upstream_edges, inner, weight, rowed, *refs):
     messages, out, terms_out = refs[:3], refs[3], refs[4:7]
-    edges, upstream_edges, sems = refs[7:]
-
-    def edge_in(edge):
-        return (
-            pltpu.make_async_copy(edges_in.at[edge], edges.at[edge], sems.at[0, edge]),
-            pltpu.make_async_copy(
-                upstream_in.at[edge], upstream_edges.at[edge], sems.at[1, edge]
-            ),
-        )
-
-    for edge in range(3):
-        for copy in edge_in(edge):
-            copy.start()
     side, batch, channels = edges.shape[1:]
     share = out.shape[1]
     width = side * batch
@@ -377,8 +382,6 @@
         turn = jnp.max(message[0:16, width:].astype(jnp.float32)).astype(jnp.int32)
         taps = [edge_tap(turn, lower, edge, d, False) for d in range(3)]
         turned = message[:, 0:width]
-        for copy in edge_in(edge):
-            copy.wait()
         left = jnp.concatenate([earlier(turned, batch), turned, later(turned, batch)], axis=0)
         pixels = edges[edge].reshape(width, channels)
         terms = dot(left, pixels, FLAT)
@@ -405,15 +408,8 @@
 
     return pl.pallas_call(
         body,
-        in_specs=[pl.BlockSpec(memory_space=pltpu.SMEM)]
-        + [pl.BlockSpec(memory_space=pl.ANY)] * 2
-        + [vmem] * 6,
+        in_specs=[pl.BlockSpec(memory_space=pltpu.SMEM)] + [vmem] * 8,
         out_specs=[vmem] * 4,
-        scratch_shapes=[
-            pltpu.VMEM(edges.shape, jnp.bfloat16),
-            pltpu.VMEM(upstream_edges.shape, jnp.bfloat16),
-            pltpu.SemaphoreType.DMA((2, 3)),
-        ],
         out_shape=[jax.ShapeDtypeStruct(inner.shape, jnp.float32)]
         + [jax.ShapeDtypeStruct((2 * share, side * batch), jnp.bfloat16)] * 3,
         compiler_params=pltpu.CompilerParams(vmem_limit_bytes=BIG),

time: 70.4 us -> 70.6 us (level)
    pallas_call x1, Pallas kernels: 12.9 us -> 13.9 us  [lay_field(): pl.pallas_call(field_kernel, in_specs=[pl.BlockSpec(memory_space=pltpu.SM...]
    pallas_call x1, Pallas kernels: 4.77 us -> 4.04 us  [seam_filters(): pl.pallas_call(body, in_specs=[pl.BlockSpec(memory_space=pltpu.SMEM)] + [...]
  transfers between devices with their start and end apart: 13 -> 13, of which waited for: 0 -> 0; matrix products, arithmetic and copies ran while one was open for 0% -> 0% of each run, Pallas kernels for 59% -> 61%
where the time goes in v8:
time: 70.6 us; the launch traced here: 69.8 us
  Pallas kernels  46.4 us (66%)
  starting transfers between devices  18.8 us (27%)
  local copies, waits for them, and re-layouts  2.31 us (3%)
  between operations  1.49 us (2%)
  other arithmetic  0.73 us (1%)
    pallas_call x1, Pallas kernels, lay_field(): pl.pallas_call(field_kernel, in_specs=[pl.BlockSpec(memory_space=pltpu.SM...  13.9 us
    pallas_call x1, Pallas kernels, convolved(): call(turn, *messages, source, weight, other)  10.2 us
    pallas_call x1, Pallas kernels, lay_upstream(): pl.pallas_call(upstream_kernel, in_specs=[pl.BlockSpec(memory_space=pltpu...  9.28 us
    pallas_call x1, Pallas kernels, convolved(): call(source, weight)  9.09 us
    ppermute x2, starting transfers between devices, exchanged(): lax.ppermute(sends[1], 'tile', westward)  7.6 us
    ppermute x4, starting transfers between devices, other(): return lax.ppermute(total, 'tile', [(i, i ^ flip) for i in range(count)])  4.97 us
    pallas_call x1, Pallas kernels, seam_filters(): pl.pallas_call(body, in_specs=[pl.BlockSpec(memory_space=pltpu.SMEM)] + [...  4.04 us
    ppermute x3, starting transfers between devices, per_device(): lax.ppermute(own, 'chan', [(i, i ^ flip) for i in range(channels // share)])  3.18 us
  transfers between devices with their start and end apart: 13, of which 0 were waited for; matrix products, arithmetic and copies ran while one was open for 0% of the time, Pallas kernels for 61%

profile of v8, /device:TPU:0, one launch (start us, length us, event | category | flops | bytes accessed | tf_op | source)
XLA Modules:
  0.0 69.8 jit_solution(7848601857528853495)
XLA Ops:
  0.6 0.5 collective-permute-start
  1.1 2.6 %collective-permute-start.1 = (bf16[9,32,128]{2,1,0:T(8,128)(2,1)}, bf16[9,32,128]{2,1,0:T(8,128)(2,1)S(1)}, u32[]{:S(2)}, u32[]{:S(2)}) collective-permute-start(bf16[9,32,128]{2,1,0:T(8,128)(2,1)} %bitcast.20), channel_id=1, source_target_pairs={{0,2},{1,3},{2,0},{3,1},{4,6},{5,7},{6,4},{7,5},{8,10},{9,11},{10,... | collective-permute-start | bytes 221192 | tf_op jit(solution)/shard_map/ppermute | solution.py:649
  3.7 0.1 collective-permute-start.2
  4.5 9.3 %lay_upstream.1 = (bf16[16,128,2048]{2,1,0:T(8,128)(2,1)}, bf16[3,128,2048]{2,1,0:T(8,128)(2,1)}, bf16[32,2176]{1,0:T(8,128)(2,1)}, bf16[32,2176]{1,0:T(8,128)(2,1)}, bf16[32,2176]{1,0:T(8,128)(2,1)}) custom-call(s32[1]{0:T(128)S(6)} %copy.9.own_turn.refs_0_, bf16[128,16,16,128]{3,2,1,0:T(8,128)(2,1)} %bitcast.25), custom_call_target="tpu_custom_call" | custom-call | flops 4294967296 | bytes 16777216 | tf_op jit(solution)/shard_map/lay_upstream/pallas_call | solution.py:197
  13.8 3.8 %collective-permute-start.3 = (bf16[32,2176]{1,0:T(8,128)(2,1)}, bf16[32,2176]{1,0:T(8,128)(2,1)S(1)}, u32[]{:S(2)}, u32[]{:S(2)}) collective-permute-start(bf16[32,2176]{1,0:T(8,128)(2,1)} %get-tuple-element.23), channel_id=1, source_target_pairs={{0,24},{4,28},{8,0},{12,4},{16,8},{20,12},{24,16},{28,20},{1,25},{... | collective-permute-start | bytes 417800 | tf_op jit(solution)/shard_map/ppermute | solution.py:642
  17.6 0.0 collective-permute-start.4
  17.6 0.0 collective-permute-done.other1
  17.6 1.6 %collective-permute-start.5 = (bf16[32,2176]{1,0:T(8,128)(2,1)}, bf16[32,2176]{1,0:T(8,128)(2,1)S(1)}, u32[]{:S(2)}, u32[]{:S(2)}) collective-permute-start(bf16[32,2176]{1,0:T(8,128)(2,1)} %get-tuple-element.25), channel_id=1, source_target_pairs={{0,4},{4,0},{8,12},{12,8},{16,20},{20,16},{24,28},{28,24},{1,5},{5... | collective-permute-start | bytes 417800 | tf_op jit(solution)/shard_map/ppermute | solution.py:644
  19.2 0.0 collective-permute-done.1.other2
  19.2 0.0 collective-permute-done.2.other3
  19.2 0.0 copy-start.9
  19.2 0.0 copy-done.7
  19.2 0.6 copy-done.8
  19.8 0.0 copy-done.9
  19.9 13.9 %lay_field.1 = (bf16[16,128,2048]{2,1,0:T(8,128)(2,1)}, bf16[3,16,128,128]{3,2,1,0:T(8,128)(2,1)}, f32[9,32,128]{2,1,0:T(8,128)}, bf16[9,32,128]{2,1,0:T(8,128)(2,1)}) custom-call(s32[1]{0:T(128)S(6)} %copy.9.own_turn.refs_0_, bf16[9,32,128]{2,1,0:T(8,128)(2,1)} %bitcast.22, bf16[9,32,128]{2,1,0:T(8,128)(2,1)} %copy-done.7, bf16[9,32,128]{2,1,0:T(8,128)(2,1)} %copy-done.8, ...), custom_call_target="tpu_custom_call" | custom-call | flops 7549747200 | bytes 20971520 | tf_op jit(solution)/shard_map/lay_field/pallas_call | solution.py:345
  33.7 0.0 collective-permute-done.3.refs_6_
  33.7 0.0 copy-start.1
  33.8 0.0 collective-permute-done.4.refs_7_
  33.8 0.0 copy-start.2
  33.8 0.0 collective-permute-done.5.refs_8_
  33.8 0.0 copy-start.3
  33.8 0.6 copy-done.1
  34.4 0.1 copy-done.2
  34.5 0.0 copy-done.3
  34.5 4.0 %seam_filters.1 = (f32[9,32,128]{2,1,0:T(8,128)}, bf16[64,2048]{1,0:T(8,128)(2,1)}, bf16[64,2048]{1,0:T(8,128)(2,1)}, bf16[64,2048]{1,0:T(8,128)(2,1)}) custom-call(s32[1]{0:T(128)S(6)} %copy.9.own_turn.refs_0_, bf16[3,16,128,128]{3,2,1,0:T(8,128)(2,1)} %get-tuple-element.19.refs_1_, bf16[3,128,2048]{2,1,0:T(8,128)(2,1)} %get-tuple-element.20.refs_2_, ...), custom_call_target="tpu_custom_call" | custom-call | flops 452984832 | bytes 3145728 | tf_op jit(solution)/shard_map/seam_filters/pallas_call | solution.py:409
  38.6 0.5 collective-permute-start.9
  39.1 3.8 %collective-permute-start.6 = (bf16[64,2048]{1,0:T(8,128)(2,1)}, bf16[64,2048]{1,0:T(8,128)(2,1)S(1)}, u32[]{:S(2)}, u32[]{:S(2)}) collective-permute-start(bf16[64,2048]{1,0:T(8,128)(2,1)} %get-tuple-element.26), channel_id=1, source_target_pairs={{0,24},{4,28},{8,0},{12,4},{16,8},{20,12},{24,16},{28,20},{1,25},{... | collective-permute-start | bytes 786440 | tf_op jit(solution)/shard_map/ppermute | solution.py:642
  42.8 0.0 collective-permute-start.7
  42.8 1.5 %collective-permute-start.8 = (bf16[64,2048]{1,0:T(8,128)(2,1)}, bf16[64,2048]{1,0:T(8,128)(2,1)S(1)}, u32[]{:S(2)}, u32[]{:S(2)}) collective-permute-start(bf16[64,2048]{1,0:T(8,128)(2,1)} %get-tuple-element.28), channel_id=1, source_target_pairs={{0,4},{4,0},{8,12},{12,8},{16,20},{20,16},{24,28},{28,24},{1,5},{5... | collective-permute-start | bytes 786440 | tf_op jit(solution)/shard_map/ppermute | solution.py:644
  44.3 9.1 %grad_conv.1.refs_6_ = bf16[256,32,128]{2,1,0:T(8,128)(2,1)} custom-call(bf16[16,128,2048]{2,1,0:T(8,128)(2,1)} %get-tuple-element.18.turned.refs_0_, bf16[9,32,128]{2,1,0:T(8,128)(2,1)} %get-tuple-element.22.refs_5_.refs_1_), custom_call_target="tpu_custom_call" | custom-call | flops 10066329600 | bytes 12582912 | tf_op jit(solution)/shard_map/grad_conv/pallas_call | solution.py:611
  53.4 0.0 collective-permute-done.9
  53.5 0.0 copy-done
  53.5 0.1 collective-permute-start.10
  53.6 4.4 %collective-permute-start.11 = (f32[9,32,128]{2,1,0:T(8,128)S(1)}, f32[9,32,128]{2,1,0:T(8,128)S(1)}, u32[]{:S(2)}, u32[]{:S(2)}) collective-permute-start(f32[9,32,128]{2,1,0:T(8,128)S(1)} %add.12), channel_id=1, source_target_pairs={{0,16},{4,20},{8,24},{12,28},{16,0},{20,4},{24,8},{28,12},{1,17},{... | collective-permute-start | bytes 442376 | tf_op jit(solution)/shard_map/ppermute | solution.py:620
  58.0 0.0 collective-permute-done.6.refs_1_
  58.0 0.0 collective-permute-start.12
  58.0 0.0 collective-permute-done.7.refs_2_
  58.0 0.0 copy-start.5
  58.0 0.0 collective-permute-done.8.refs_3_
  58.0 0.0 copy-start.6
  58.0 0.7 copy-done.4
  58.7 0.1 copy-done.5
  58.8 0.1 copy-done.6
  58.9 10.2 %conv.1 = (bf16[256,32,128]{2,1,0:T(8,128)(2,1)}, bf16[256,32,128]{2,1,0:T(8,128)(2,1)}) custom-call(s32[1]{0:T(128)S(6)} %copy.9.own_turn.refs_0_, bf16[64,2048]{1,0:T(8,128)(2,1)} %copy-done.4, bf16[64,2048]{1,0:T(8,128)(2,1)} %copy-done.5, bf16[64,2048]{1,0:T(8,128)(2,1)} %copy-done.6, ...), custom_call_target="tpu_custom_call", output_to_operand_aliasing={{1}: (6, {})} | custom-call | flops 10066329600 | bytes 12582912 | tf_op jit(solution)/shard_map/conv/pallas_call | solution.py:611
  69.1 0.0 collective-permute-done.10
  69.1 0.0 collective-permute-done.11
  69.1 0.0 collective-permute-done.12
  69.1 0.7 %add_add_fusion = f32[9,32,128]{2,1,0:T(8,128)} fusion(f32[9,32,128]{2,1,0:T(8,128)S(1)} %collective-permute-done.11, f32[9,32,128]{2,1,0:T(8,128)S(1)} %collective-permute-done.12, f32[9,32,128]{2,1,0:T(8,128)S(1)} %add.12, f32[9,32,128]{2,1,0:T(8,128)S(1)} %collective-permute-done.10), kind=kLoop, calls=%fused_computation | loop fusion | flops 110592 | bytes 737280 | tf_op jit(solution)/shard_map/add | solution.py:624
  (5 shorter events, 0.0 us)
Async XLA Ops:
  0.6 17.0 %collective-permute-start = (bf16[9,32,128]{2,1,0:T(8,128)(2,1)}, bf16[9,32,128]{2,1,0:T(8,128)(2,1)S(1)}, u32[]{:S(2)}, u32[]{:S(2)}) collective-permute-start(bf16[9,32,128]{2,1,0:T(8,128)(2,1)} %bitcast.19), channel_id=1, source_target_pairs={{0,1},{1,0},{2,3},{3,2},{4,5},{5,4},{6,7},{7,6},{8,9},{9,8},{10,11... | collective-permute-start | bytes 221192 | tf_op jit(solution)/shard_map/ppermute | solution.py:649
  1.1 18.0 %collective-permute-start.1 = (bf16[9,32,128]{2,1,0:T(8,128)(2,1)}, bf16[9,32,128]{2,1,0:T(8,128)(2,1)S(1)}, u32[]{:S(2)}, u32[]{:S(2)}) collective-permute-start(bf16[9,32,128]{2,1,0:T(8,128)(2,1)} %bitcast.20), channel_id=1, source_target_pairs={{0,2},{1,3},{2,0},{3,1},{4,6},{5,7},{6,4},{7,5},{8,10},{9,11},{10,... | collective-permute-start | bytes 221192 | tf_op jit(solution)/shard_map/ppermute | solution.py:649
  3.7 15.5 %collective-permute-start.2 = (bf16[9,32,128]{2,1,0:T(8,128)(2,1)}, bf16[9,32,128]{2,1,0:T(8,128)(2,1)S(1)}, u32[]{:S(2)}, u32[]{:S(2)}) collective-permute-start(bf16[9,32,128]{2,1,0:T(8,128)(2,1)} %bitcast.21), channel_id=1, source_target_pairs={{0,3},{1,2},{2,1},{3,0},{4,7},{5,6},{6,5},{7,4},{8,11},{9,10},{10,... | collective-permute-start | bytes 221192 | tf_op jit(solution)/shard_map/ppermute | solution.py:649
  13.8 20.0 %collective-permute-start.3 = (bf16[32,2176]{1,0:T(8,128)(2,1)}, bf16[32,2176]{1,0:T(8,128)(2,1)S(1)}, u32[]{:S(2)}, u32[]{:S(2)}) collective-permute-start(bf16[32,2176]{1,0:T(8,128)(2,1)} %get-tuple-element.23), channel_id=1, source_target_pairs={{0,24},{4,28},{8,0},{12,4},{16,8},{20,12},{24,16},{28,20},{1,25},{... | collective-permute-start | bytes 417800 | tf_op jit(solution)/shard_map/ppermute | solution.py:642
  17.6 16.2 %collective-permute-start.4 = (bf16[32,2176]{1,0:T(8,128)(2,1)}, bf16[32,2176]{1,0:T(8,128)(2,1)S(1)}, u32[]{:S(2)}, u32[]{:S(2)}) collective-permute-start(bf16[32,2176]{1,0:T(8,128)(2,1)} %get-tuple-element.24), channel_id=1, source_target_pairs={{0,8},{4,12},{8,16},{12,20},{16,24},{20,28},{24,0},{28,4},{1,9},{5... | collective-permute-start | bytes 417800 | tf_op jit(solution)/shard_map/ppermute | solution.py:643
  17.6 1.6 %copy-start.7 = (bf16[9,32,128]{2,1,0:T(8,128)(2,1)}, bf16[9,32,128]{2,1,0:T(8,128)(2,1)S(1)}, u32[]{:S(2)}) copy-start(bf16[9,32,128]{2,1,0:T(8,128)(2,1)S(1)} %collective-permute-done.other1) | copy-start | bytes 221188
  17.6 16.2 %collective-permute-start.5 = (bf16[32,2176]{1,0:T(8,128)(2,1)}, bf16[32,2176]{1,0:T(8,128)(2,1)S(1)}, u32[]{:S(2)}, u32[]{:S(2)}) collective-permute-start(bf16[32,2176]{1,0:T(8,128)(2,1)} %get-tuple-element.25), channel_id=1, source_target_pairs={{0,4},{4,0},{8,12},{12,8},{16,20},{20,16},{24,28},{28,24},{1,5},{5... | collective-permute-start | bytes 417800 | tf_op jit(solution)/shard_map/ppermute | solution.py:644
  19.2 0.6 copy-start.8
  19.2 0.7 copy-start.9
  33.7 0.7 copy-start.1
  33.8 0.7 %copy-start.2 = (bf16[32,2176]{1,0:T(8,128)(2,1)}, bf16[32,2176]{1,0:T(8,128)(2,1)S(1)}, u32[]{:S(2)}) copy-start(bf16[32,2176]{1,0:T(8,128)(2,1)S(1)} %collective-permute-done.4.refs_7_) | copy-start | bytes 417796
  33.8 0.7 %copy-start.3 = (bf16[32,2176]{1,0:T(8,128)(2,1)}, bf16[32,2176]{1,0:T(8,128)(2,1)S(1)}, u32[]{:S(2)}) copy-start(bf16[32,2176]{1,0:T(8,128)(2,1)S(1)} %collective-permute-done.5.refs_8_) | copy-start | bytes 417796
  38.6 14.9 %collective-permute-start.9 = (f32[9,32,128]{2,1,0:T(8,128)}, f32[9,32,128]{2,1,0:T(8,128)S(1)}, u32[]{:S(2)}, u32[]{:S(2)}) collective-permute-start(f32[9,32,128]{2,1,0:T(8,128)} %get-tuple-element.32), channel_id=1, source_target_pairs={{0,4},{4,0},{8,12},{12,8},{16,20},{20,16},{24,28},{28,24},{1,5},{5... | collective-permute-start | bytes 442376 | tf_op jit(solution)/shard_map/ppermute | solution.py:620
  39.1 18.9 %collective-permute-start.6 = (bf16[64,2048]{1,0:T(8,128)(2,1)}, bf16[64,2048]{1,0:T(8,128)(2,1)S(1)}, u32[]{:S(2)}, u32[]{:S(2)}) collective-permute-start(bf16[64,2048]{1,0:T(8,128)(2,1)} %get-tuple-element.26), channel_id=1, source_target_pairs={{0,24},{4,28},{8,0},{12,4},{16,8},{20,12},{24,16},{28,20},{1,25},{... | collective-permute-start | bytes 786440 | tf_op jit(solution)/shard_map/ppermute | solution.py:642
  42.8 15.1 %collective-permute-start.7 = (bf16[64,2048]{1,0:T(8,128)(2,1)}, bf16[64,2048]{1,0:T(8,128)(2,1)S(1)}, u32[]{:S(2)}, u32[]{:S(2)}) collective-permute-start(bf16[64,2048]{1,0:T(8,128)(2,1)} %get-tuple-element.27), channel_id=1, source_target_pairs={{0,8},{4,12},{8,16},{12,20},{16,24},{20,28},{24,0},{28,4},{1,9},{5... | collective-permute-start | bytes 786440 | tf_op jit(solution)/shard_map/ppermute | solution.py:643
  42.8 10.6 %copy-start = (f32[9,32,128]{2,1,0:T(8,128)S(1)}, f32[9,32,128]{2,1,0:T(8,128)}, u32[]{:S(2)}) copy-start(f32[9,32,128]{2,1,0:T(8,128)} %get-tuple-element.32) | copy-start | bytes 442372
  42.8 15.2 %collective-permute-start.8 = (bf16[64,2048]{1,0:T(8,128)(2,1)}, bf16[64,2048]{1,0:T(8,128)(2,1)S(1)}, u32[]{:S(2)}, u32[]{:S(2)}) collective-permute-start(bf16[64,2048]{1,0:T(8,128)(2,1)} %get-tuple-element.28), channel_id=1, source_target_pairs={{0,4},{4,0},{8,12},{12,8},{16,20},{20,16},{24,28},{28,24},{1,5},{5... | collective-permute-start | bytes 786440 | tf_op jit(solution)/shard_map/ppermute | solution.py:644
  53.5 15.6 %collective-permute-start.10 = (f32[9,32,128]{2,1,0:T(8,128)S(1)}, f32[9,32,128]{2,1,0:T(8,128)S(1)}, u32[]{:S(2)}, u32[]{:S(2)}) collective-permute-start(f32[9,32,128]{2,1,0:T(8,128)S(1)} %add.12), channel_id=1, source_target_pairs={{0,8},{4,12},{8,0},{12,4},{16,24},{20,28},{24,16},{28,20},{1,9},{5... | collective-permute-start | bytes 442376 | tf_op jit(solution)/shard_map/ppermute | solution.py:620
  53.6 15.5 %collective-permute-start.11 = (f32[9,32,128]{2,1,0:T(8,128)S(1)}, f32[9,32,128]{2,1,0:T(8,128)S(1)}, u32[]{:S(2)}, u32[]{:S(2)}) collective-permute-start(f32[9,32,128]{2,1,0:T(8,128)S(1)} %add.12), channel_id=1, source_target_pairs={{0,16},{4,20},{8,24},{12,28},{16,0},{20,4},{24,8},{28,12},{1,17},{... | collective-permute-start | bytes 442376 | tf_op jit(solution)/shard_map/ppermute | solution.py:620
  58.0 0.7 %copy-start.4 = (bf16[64,2048]{1,0:T(8,128)(2,1)}, bf16[64,2048]{1,0:T(8,128)(2,1)S(1)}, u32[]{:S(2)}) copy-start(bf16[64,2048]{1,0:T(8,128)(2,1)S(1)} %collective-permute-done.6.refs_1_) | copy-start | bytes 786436
  58.0 11.2 %collective-permute-start.12 = (f32[9,32,128]{2,1,0:T(8,128)S(1)}, f32[9,32,128]{2,1,0:T(8,128)S(1)}, u32[]{:S(2)}, u32[]{:S(2)}) collective-permute-start(f32[9,32,128]{2,1,0:T(8,128)S(1)} %add.12), channel_id=1, source_target_pairs={{0,24},{4,28},{8,16},{12,20},{16,8},{20,12},{24,0},{28,4},{1,25},{... | collective-permute-start | bytes 442376 | tf_op jit(solution)/shard_map/ppermute | solution.py:620
  58.0 0.8 %copy-start.5 = (bf16[64,2048]{1,0:T(8,128)(2,1)}, bf16[64,2048]{1,0:T(8,128)(2,1)S(1)}, u32[]{:S(2)}) copy-start(bf16[64,2048]{1,0:T(8,128)(2,1)S(1)} %collective-permute-done.7.refs_2_) | copy-start | bytes 786436
  58.0 0.9 %copy-start.6 = (bf16[64,2048]{1,0:T(8,128)(2,1)}, bf16[64,2048]{1,0:T(8,128)(2,1)S(1)}, u32[]{:S(2)}) copy-start(bf16[64,2048]{1,0:T(8,128)(2,1)S(1)} %collective-permute-done.8.refs_3_) | copy-start | bytes 786436
